TPU v7x, 128 devices: a whole 4x4x4 slice. The times are simulated.
128 devices in a mesh: brick: 8 (over x, core), group: 16 (over y, z).
Axes of the slice: x: 4, y: 4, z: 4, core: 2. Of those that a mesh axis runs over, the one named last changes fastest.
Arguments:
- right_side: float32 [64, 16384], P(None, ('brick', 'group')), may hold values from -6 to 6
- fine_diag: bfloat16 [64, 64, 16384], P(None, None, ('brick', 'group'))
- fine_off: bfloat16 [6, 64, 64, 16384], P(None, None, None, ('brick', 'group')), may hold values from -0.1875 to 0.1875
- fine_inv: bfloat16 [64, 64, 16384], P(None, None, ('brick', 'group'))
- fine_columns: int32 [6, 16384], P(None, ('brick', 'group')), may hold values from -32 to 16415, as said below
- aggregate: int32 [16384], P(('brick', 'group')), may hold values from 0 to 15, as said below
- coarse_diag: bfloat16 [64, 64, 2048], P(None, None, ('brick', 'group'))
- coarse_off: bfloat16 [8, 64, 64, 2048], P(None, None, None, ('brick', 'group')), may hold values from -0.125 to 0.125
- coarse_inv: bfloat16 [64, 64, 2048], P(None, None, ('brick', 'group'))
- coarse_columns: int32 [8, 2048], P(None, ('brick', 'group')), may hold values from 0 to 2047, as said below
Outputs:
- solution: float32 [64, 16384], P(None, ('brick', 'group'))
Inputs may be any that keep to these rules, and one draw needn't show every extreme that they name: `fine_columns`: each fine block row has exactly 6 off-diagonal blocks, whose columns lie within 32 block rows of their row. Within each device's 128 fine block rows aggregate never falls and takes every value; each aggregate is a run of consecutive rows. `coarse_columns`: each coarse block row has exactly 8 off-diagonal blocks, whose columns lie within 16 coarse rows of their row.
All inputs are finite; a program needn't handle non-finite values.
Results may differ from a plain program's by a relative error of at most 0.0003.
Values sent between devices are 32-bit elements; how exact they have to be, the bound alone decides.
No kernel may reach another device: no remote copies, remote signals or barrier semaphores. Data moves between devices by JAX's collectives and lax.ppermute only.
A program may use at most 64 MiB of HBM per device.

v0:
```python
import jax
import jax.numpy as jnp
from jax import lax
from jax.experimental import pallas as pl
from jax.experimental.pallas import tpu as pltpu
from jax.sharding import PartitionSpec as P

SWEEPS = 2
CSWEEPS = 4
CYCLES = 2
AXES = ("brick", "group")
LINE = 4

damping = 0.7
LANES = 128
F32 = jnp.float32


def routes(count):
    lines = count // LINE
    up, down, cross = [], [], []
    for i in range(count):
        base = i - i % LINE
        up.append((i, base + (i + 1) % LINE))
        down.append((i, base + (i - 1) % LINE))
    for k in range(lines - 1):
        a, b = LINE * k + LINE - 1, LINE * k + LINE
        cross += [(a, b), (b, a)]
    for k in range(1, lines - 1):
        a, b = LINE * k + 1, LINE * k + 2
        cross += [(a, b), (b, a)]
    last = count - 1
    cross += [(0, 1), (1, 2), (2, 0), (last - 2, last - 1), (last - 1, last), (last, last - 2)]
    return up, down, cross


def exchange(field, ways):
    return [lax.ppermute(field, AXES, way) for way in ways]


def iota(shape, dim):
    return lax.broadcasted_iota(jnp.int32, shape, dim)


def fold_sublanes(parts):
    rows = iota(parts[0].shape, 0)
    shift = 4
    while shift:
        low = (rows & shift) == 0
        parts = [
            jnp.where(low, a, b) + pltpu.roll(jnp.where(low, b, a), 4 if shift == 4 else (8 - shift), 0)
            if shift == 4
            else fold_pair(a, b, low, shift, 0)
            for a, b in zip(parts[:shift], parts[shift:])
        ]
        shift //= 2
    return parts[0]


def fold_pair(a, b, low, shift, axis):
    size = a.shape[axis]
    own = jnp.where(low, a, b)
    other = jnp.where(low, b, a)
    return own + jnp.where(
        low, pltpu.roll(other, size - shift, axis), pltpu.roll(other, shift, axis)
    )


def fold_lanes(parts):
    lanes = iota(parts[0].shape, 1)
    shift, half = 64, 4
    while half:
        low = (lanes & shift) == 0
        if shift == 64:
            parts = [
                jnp.where(low, a, b) + pltpu.roll(jnp.where(low, b, a), 64, 1)
                for a, b in zip(parts[:half], parts[half:])
            ]
        else:
            parts = [fold_pair(a, b, low, shift, 1) for a, b in zip(parts[:half], parts[half:])]
        shift //= 2
        half //= 2
    return parts[0]


def take_lanes(field, places):
    return jnp.take_along_axis(field, places, axis=1, mode="promise_in_bounds")


def apply_fine(blocks, fields, a_block):
    acc = jnp.zeros((8, 8, LANES), F32)
    for slot in range(blocks.shape[0]):
        for g in range(4):
            piece = blocks[slot, pl.ds(pl.multiple_of(a_block * 8, 8), 8), 16 * g : 16 * g + 16, :].astype(F32)
            v = fields[slot, 16 * g : 16 * g + 16, :]
            acc = acc + piece[:, :8] * v[None, :8]
            acc = acc + piece[:, 8:] * v[None, 8:]
    return fold_sublanes([acc[i] for i in range(8)])


def neighbours(flags, up, down, cross):
    left = jnp.where(flags[0] == 1, cross, up)
    right = jnp.where(flags[1] == 1, cross, down)
    left = jnp.where(flags[2] == 1, 0.0, left)
    right = jnp.where(flags[3] == 1, 0.0, right)
    return left, right


def gather_fine(flags, columns, x_ref, up, down, cross, fields):
    lanes = iota((8, LANES), 1)
    slots = columns.shape[0]
    places = [jnp.broadcast_to(columns[s : s + 1, :], (8, LANES)) for s in range(slots)]
    lane_of = [p & (LANES - 1) for p in places]
    own = [(p >= 0) & (p < LANES) for p in places]
    for g in range(8):
        part = slice(8 * g, 8 * g + 8)
        left, right = neighbours(flags, up[part, :], down[part, :], cross[part, :])
        rim = jnp.where(lanes < LANES // 2, right, left)
        x = x_ref[part, :]
        fields[0, part, :] = x
        for s in range(slots):
            fields[s + 1, part, :] = jnp.where(
                own[s], take_lanes(x, lane_of[s]), take_lanes(rim, lane_of[s])
            )


def residual_into(res, rhs, diag, off, fields):
    def body(ab, carry):
        acc = jnp.zeros((8, 8, LANES), F32)
        rows = pl.ds(pl.multiple_of(ab * 8, 8), 8)
        for slot in range(fields.shape[0]):
            for g in range(4):
                src = diag[rows, 16 * g : 16 * g + 16, :] if slot == 0 else off[slot - 1, rows, 16 * g : 16 * g + 16, :]
                piece = src.astype(F32)
                v = fields[slot, 16 * g : 16 * g + 16, :]
                acc = acc + piece[:, :8] * v[None, :8]
                acc = acc + piece[:, 8:] * v[None, 8:]
        res[rows, :] = rhs[rows, :] - fold_sublanes([acc[i] for i in range(8)])
        return carry

    lax.fori_loop(0, 8, body, 0)


def smooth_into(out, x, inv, res):
    def body(ab, carry):
        acc = jnp.zeros((8, 8, LANES), F32)
        rows = pl.ds(pl.multiple_of(ab * 8, 8), 8)
        for g in range(4):
            piece = inv[rows, 16 * g : 16 * g + 16, :].astype(F32)
            v = res[16 * g : 16 * g + 16, :]
            acc = acc + piece[:, :8] * v[None, :8]
            acc = acc + piece[:, 8:] * v[None, 8:]
        step = damping * fold_sublanes([acc[i] for i in range(8)])
        out[rows, :] = step if x is None else x[rows, :] + step
        return carry

    lax.fori_loop(0, 8, body, 0)


def first_kernel(inv, rhs, out):
    smooth_into(out, None, inv, rhs)


def sweep_kernel(flags, columns, diag, off, inv, rhs, x, up, down, cross, out, fields, res):
    gather_fine(flags, columns, x, up, down, cross, fields)
    residual_into(res, rhs, diag, off, fields)
    smooth_into(out, x, inv, res)


def pack_rows(full):
    group = iota((8, LANES), 1) // 16
    out = full[0:8, :]
    for g in range(1, 8):
        out = jnp.where(group == g, full[8 * g : 8 * g + 8, :], out)
    return out


def small_apply(blocks, packed, extra=None, fields=None):
    parts = []
    for ab in range(8):
        acc = blocks[8 * ab : 8 * ab + 8] * packed[None]
        if extra is not None:
            for g in range(8):
                acc = acc + extra[8 * ab : 8 * ab + 8, 8 * g : 8 * g + 8, :] * fields[g][None]
        parts.append(fold_sublanes([acc[i] for i in range(8)]))
    return fold_lanes(parts)


def restrict_kernel(flags, columns, diag, off, rhs, x, up, down, cross, agg, cinv, coarse_rhs, out, fields, res):
    gather_fine(flags, columns, x, up, down, cross, fields)
    residual_into(res, rhs, diag, off, fields)
    r = res[...]
    hi = r.astype(jnp.bfloat16)
    rest = r - hi.astype(F32)
    mid = rest.astype(jnp.bfloat16)
    low = (rest - mid.astype(F32)).astype(jnp.bfloat16)
    parts = jnp.concatenate([hi, mid, low], axis=0)
    row_of = jnp.broadcast_to(agg[...], (LANES, LANES))
    select = jnp.where(row_of == (iota((LANES, LANES), 0) & 15), 1.0, 0.0).astype(jnp.bfloat16)
    sums = lax.dot_general(parts, select, (((1,), (1,)), ((), ())), preferred_element_type=F32)
    full = sums[0:64] + (sums[64:128] + sums[128:192])
    packed = pack_rows(full)
    coarse_rhs[...] = packed
    out[...] = damping * small_apply(cinv, packed)


def coarse_step(flags, columns, cdiag, coff, cinv, coarse_rhs, u, up, down, cross):
    left, right = neighbours(flags, up[...], down[...], cross[...])
    places = jnp.broadcast_to(columns[...], (8, LANES))
    inner = places & 15
    mine = u[...]
    fields = []
    for g in range(8):
        lane = inner + 16 * g
        fields.append(
            jnp.where(
                places < 0,
                take_lanes(left, lane),
                jnp.where(places < 16, take_lanes(mine, lane), take_lanes(right, lane)),
            )
        )
    total = small_apply(cdiag, mine, coff, fields)
    return mine + damping * small_apply(cinv, coarse_rhs[...] - total)


def coarse_kernel(flags, columns, cdiag, coff, cinv, coarse_rhs, u, up, down, cross, out):
    out[...] = coarse_step(flags, columns, cdiag, coff, cinv, coarse_rhs, u, up, down, cross)


def prolong_kernel(flags, columns, cdiag, coff, cinv, coarse_rhs, u, up, down, cross, agg, x, out):
    last = coarse_step(flags, columns, cdiag, coff, cinv, coarse_rhs, u, up, down, cross)
    lane = jnp.broadcast_to(agg[...], (8, LANES))
    for g in range(8):
        part = slice(8 * g, 8 * g + 8)
        out[part, :] = x[part, :] + take_lanes(last, lane + 16 * g)


def in_vmem(array):
    return pltpu.with_memory_space_constraint(array, pltpu.VMEM)


VM = pl.BlockSpec(memory_space=pltpu.VMEM)
SM = pl.BlockSpec(memory_space=pltpu.SMEM)


def call(kernel, outs, args, scratch=(), smem=False, flops=0, name=None):
    shapes = [pltpu.VMEM(shape, F32) for shape in outs]
    specs = [VM] * len(args)
    if smem:
        specs[0] = SM
    args = [a if (smem and i == 0) else in_vmem(a) for i, a in enumerate(args)]
    result = pl.pallas_call(
        kernel,
        out_shape=shapes if len(shapes) > 1 else shapes[0],
        in_specs=specs,
        out_specs=[VM] * len(shapes) if len(shapes) > 1 else VM,
        scratch_shapes=list(scratch),
        compiler_params=pltpu.CompilerParams(vmem_limit_bytes=4 * 1024 * 1024),
        name=name,
    )(*args)
    return result


def shards(
    right_side,
    fine_diag,
    fine_off,
    fine_inv,
    fine_columns,
    aggregate,
    coarse_diag,
    coarse_off,
    coarse_inv,
    coarse_columns,
):
    size, rows = right_side.shape
    slots = fine_off.shape[0]
    own_rows = coarse_diag.shape[2]
    cslots = coarse_off.shape[0]
    count = lax.axis_size(AXES)
    device = lax.axis_index(AXES)
    ways = routes(count)
    flags = jnp.stack(
        [
            device % LINE == 0,
            device % LINE == LINE - 1,
            device == 0,
            device == count - 1,
        ]
    ).astype(jnp.int32)
    columns = fine_columns - device * rows
    ccolumns = (coarse_columns - device * own_rows).reshape(1, cslots * own_rows)
    agg = aggregate.reshape(1, rows)
    coff = jnp.transpose(coarse_off, (1, 2, 0, 3)).reshape(size, size, cslots * own_rows).astype(F32)

    def packed_blocks(blocks):
        split = blocks.reshape(size, 8, 8, own_rows)
        return jnp.transpose(split, (0, 2, 1, 3)).reshape(size, 8, 8 * own_rows).astype(F32)

    cdiag = packed_blocks(coarse_diag)
    cinv = packed_blocks(coarse_inv)

    full = (size, rows)
    packed = (8, LANES)
    scratch = [pltpu.VMEM((slots + 1,) + full, F32), pltpu.VMEM(full, F32)]

    def sweep(x):
        return call(
            sweep_kernel,
            [full],
            [flags, columns, fine_diag, fine_off, fine_inv, right_side, x, *exchange(x, ways)],
            scratch,
            smem=True,
        )

    x = call(first_kernel, [full], [fine_inv, right_side])
    for cycle in range(CYCLES):
        for step in range(SWEEPS):
            if cycle or step:
                x = sweep(x)
        crhs, u = call(
            restrict_kernel,
            [packed, packed],
            [flags, columns, fine_diag, fine_off, right_side, x, *exchange(x, ways), agg, cinv],
            scratch,
            smem=True,
        )
        for step in range(1, CSWEEPS):
            base = [flags, ccolumns, cdiag, coff, cinv, crhs, u, *exchange(u, ways)]
            if step < CSWEEPS - 1:
                u = call(coarse_kernel, [packed], base, smem=True)
            else:
                x = call(prolong_kernel, [full], base + [agg, x], smem=True)
        for step in range(SWEEPS):
            x = sweep(x)
    return x


def solution(mesh):
    placed = (
        P(None, AXES),
        P(None, None, AXES),
        P(None, None, None, AXES),
        P(None, None, AXES),
        P(None, AXES),
        P(AXES),
        P(None, None, AXES),
        P(None, None, None, AXES),
        P(None, None, AXES),
        P(None, AXES),
    )
    return jax.shard_map(
        shards, mesh=mesh, in_specs=placed, out_specs=P(None, AXES), check_vma=False
    )
```

profile of v0, /device:TPU:6, one launch (start us, length us, event | category | flops | bytes accessed | tf_op | source)
XLA Modules:
  0.0 214.1 jit_solution(7902773184189713782)
XLA Ops:
  6.5 3.5 %collective-permute-start.2 = (f32[64,128]{1,0:T(8,128)S(1)}, f32[64,128]{1,0:T(8,128)S(1)}, u32[]{:S(2)}, u32[]{:S(2)}) collective-permute-start(f32[64,128]{1,0:T(8,128)S(1)} %shard_map.100.x), channel_id=1, source_target_pairs={{3,4},{4,3},{7,8},{8,7},{11,12},{12,11},{15,16},{16,15},{19,20},{2... | collective-permute-start | bytes 98312 | tf_op jit(solution)/shard_map/ppermute | solution.py:38
  11.4 4.0 %convert_bitcast_fusion = f32[64,64,8,16]{1,3,0,2:T(8,128)} fusion(bf16[8,64,64,16]{2,3,1,0:T(8,128)(2,1)} %param.17), kind=kLoop, calls=%fused_computation | loop fusion | flops 524288 | bytes 3145728 | tf_op jit(solution)/shard_map/convert_element_type | solution.py:294
  22.2 3.2 %collective-permute-start.4 = (f32[64,128]{1,0:T(8,128)S(1)}, f32[64,128]{1,0:T(8,128)S(1)}, u32[]{:S(2)}, u32[]{:S(2)}) collective-permute-start(f32[64,128]{1,0:T(8,128)S(1)} %shard_map.101.x), channel_id=1, source_target_pairs={{0,3},{1,0},{2,1},{3,2},{4,7},{5,4},{6,5},{7,6},{8,11},{9,8},{10,9... | collective-permute-start | bytes 98312 | tf_op jit(solution)/shard_map/ppermute | solution.py:38
  27.6 5.4 %collective-permute-done.5.cross = f32[64,128]{1,0:T(8,128)S(1)} collective-permute-done((f32[64,128]{1,0:T(8,128)S(1)}, f32[64,128]{1,0:T(8,128)S(1)}, u32[]{:S(2)}, u32[]{:S(2)}) %collective-permute-start.5) | collective-permute-done | bytes 32800 | tf_op jit(solution)/shard_map/ppermute | solution.py:38
  38.6 3.2 %collective-permute-start.7 = (f32[8,128]{1,0:T(8,128)S(1)}, f32[8,128]{1,0:T(8,128)S(1)}, u32[]{:S(2)}, u32[]{:S(2)}) collective-permute-start(f32[8,128]{1,0:T(8,128)S(1)} %get-tuple-element.10.u), channel_id=1, source_target_pairs={{0,3},{1,0},{2,1},{3,2},{4,7},{5,4},{6,5},{7,6},{8,11},{9,8},{10,9... | collective-permute-start | bytes 12296 | tf_op jit(solution)/shard_map/ppermute | solution.py:38
  42.9 4.8 %copy.16 = f32[64,64,8,16]{1,3,2,0:T(8,128)} copy(f32[64,64,8,16]{1,3,0,2:T(8,128)} %convert_bitcast_fusion) | data formatting | bytes 4194304 | tf_op jit(solution)/shard_map/convert_element_type | solution.py:294
  47.7 4.0 %copy.37.coff = f32[64,64,128]{2,1,0:T(8,128)} copy(f32[64,64,128]{1,2,0:T(8,128)} %bitcast.24) | data formatting | bytes 4194304 | tf_op jit(solution)/shard_map/convert_element_type | solution.py:294
  55.5 3.2 %collective-permute-start.10 = (f32[8,128]{1,0:T(8,128)S(1)}, f32[8,128]{1,0:T(8,128)S(1)}, u32[]{:S(2)}, u32[]{:S(2)}) collective-permute-start(f32[8,128]{1,0:T(8,128)S(1)} %shard_map.103.u), channel_id=1, source_target_pairs={{0,3},{1,0},{2,1},{3,2},{4,7},{5,4},{6,5},{7,6},{8,11},{9,8},{10,9... | collective-permute-start | bytes 12296 | tf_op jit(solution)/shard_map/ppermute | solution.py:38
  58.7 4.2 %collective-permute-start.11 = (f32[8,128]{1,0:T(8,128)S(1)}, f32[8,128]{1,0:T(8,128)S(1)}, u32[]{:S(2)}, u32[]{:S(2)}) collective-permute-start(f32[8,128]{1,0:T(8,128)S(1)} %shard_map.103.u), channel_id=1, source_target_pairs={{3,4},{4,3},{7,8},{8,7},{11,12},{12,11},{15,16},{16,15},{19,20},{2... | collective-permute-start | bytes 12296 | tf_op jit(solution)/shard_map/ppermute | solution.py:38
  68.8 3.2 %collective-permute-start.13 = (f32[8,128]{1,0:T(8,128)S(1)}, f32[8,128]{1,0:T(8,128)S(1)}, u32[]{:S(2)}, u32[]{:S(2)}) collective-permute-start(f32[8,128]{1,0:T(8,128)S(1)} %shard_map.104.u), channel_id=1, source_target_pairs={{0,3},{1,0},{2,1},{3,2},{4,7},{5,4},{6,5},{7,6},{8,11},{9,8},{10,9... | collective-permute-start | bytes 12296 | tf_op jit(solution)/shard_map/ppermute | solution.py:38
  74.5 4.8 %collective-permute-done.14.cross = f32[8,128]{1,0:T(8,128)S(1)} collective-permute-done((f32[8,128]{1,0:T(8,128)S(1)}, f32[8,128]{1,0:T(8,128)S(1)}, u32[]{:S(2)}, u32[]{:S(2)}) %collective-permute-start.14) | collective-permute-done | bytes 4128 | tf_op jit(solution)/shard_map/ppermute | solution.py:38
  88.4 5.7 %collective-permute-done.17.cross = f32[64,128]{1,0:T(8,128)S(1)} collective-permute-done((f32[64,128]{1,0:T(8,128)S(1)}, f32[64,128]{1,0:T(8,128)S(1)}, u32[]{:S(2)}, u32[]{:S(2)}) %collective-permute-start.17) | collective-permute-done | bytes 32800 | tf_op jit(solution)/shard_map/ppermute | solution.py:38
  102.0 5.7 %collective-permute-done.20.cross = f32[64,128]{1,0:T(8,128)S(1)} collective-permute-done((f32[64,128]{1,0:T(8,128)S(1)}, f32[64,128]{1,0:T(8,128)S(1)}, u32[]{:S(2)}, u32[]{:S(2)}) %collective-permute-start.20) | collective-permute-done | bytes 32800 | tf_op jit(solution)/shard_map/ppermute | solution.py:38
  115.5 5.7 %collective-permute-done.23.cross = f32[64,128]{1,0:T(8,128)S(1)} collective-permute-done((f32[64,128]{1,0:T(8,128)S(1)}, f32[64,128]{1,0:T(8,128)S(1)}, u32[]{:S(2)}, u32[]{:S(2)}) %collective-permute-start.23) | collective-permute-done | bytes 32800 | tf_op jit(solution)/shard_map/ppermute | solution.py:38
  129.0 5.7 %collective-permute-done.26.cross = f32[64,128]{1,0:T(8,128)S(1)} collective-permute-done((f32[64,128]{1,0:T(8,128)S(1)}, f32[64,128]{1,0:T(8,128)S(1)}, u32[]{:S(2)}, u32[]{:S(2)}) %collective-permute-start.26) | collective-permute-done | bytes 32800 | tf_op jit(solution)/shard_map/ppermute | solution.py:38
  142.6 5.7 %collective-permute-done.29.cross = f32[64,128]{1,0:T(8,128)S(1)} collective-permute-done((f32[64,128]{1,0:T(8,128)S(1)}, f32[64,128]{1,0:T(8,128)S(1)}, u32[]{:S(2)}, u32[]{:S(2)}) %collective-permute-start.29) | collective-permute-done | bytes 32800 | tf_op jit(solution)/shard_map/ppermute | solution.py:38
  151.0 3.2 %collective-permute-start.31 = (f32[8,128]{1,0:T(8,128)S(1)}, f32[8,128]{1,0:T(8,128)S(1)}, u32[]{:S(2)}, u32[]{:S(2)}) collective-permute-start(f32[8,128]{1,0:T(8,128)S(1)} %get-tuple-element.12.u), channel_id=1, source_target_pairs={{0,3},{1,0},{2,1},{3,2},{4,7},{5,4},{6,5},{7,6},{8,11},{9,8},{10,9... | collective-permute-start | bytes 12296 | tf_op jit(solution)/shard_map/ppermute | solution.py:38
  155.9 5.7 %collective-permute-done.32.cross = f32[8,128]{1,0:T(8,128)S(1)} collective-permute-done((f32[8,128]{1,0:T(8,128)S(1)}, f32[8,128]{1,0:T(8,128)S(1)}, u32[]{:S(2)}, u32[]{:S(2)}) %collective-permute-start.32) | collective-permute-done | bytes 4128 | tf_op jit(solution)/shard_map/ppermute | solution.py:38
  162.8 3.2 %collective-permute-start.34 = (f32[8,128]{1,0:T(8,128)S(1)}, f32[8,128]{1,0:T(8,128)S(1)}, u32[]{:S(2)}, u32[]{:S(2)}) collective-permute-start(f32[8,128]{1,0:T(8,128)S(1)} %shard_map.111.u), channel_id=1, source_target_pairs={{0,3},{1,0},{2,1},{3,2},{4,7},{5,4},{6,5},{7,6},{8,11},{9,8},{10,9... | collective-permute-start | bytes 12296 | tf_op jit(solution)/shard_map/ppermute | solution.py:38
  167.6 5.7 %collective-permute-done.35.cross = f32[8,128]{1,0:T(8,128)S(1)} collective-permute-done((f32[8,128]{1,0:T(8,128)S(1)}, f32[8,128]{1,0:T(8,128)S(1)}, u32[]{:S(2)}, u32[]{:S(2)}) %collective-permute-start.35) | collective-permute-done | bytes 4128 | tf_op jit(solution)/shard_map/ppermute | solution.py:38
  174.6 3.2 %collective-permute-start.37 = (f32[8,128]{1,0:T(8,128)S(1)}, f32[8,128]{1,0:T(8,128)S(1)}, u32[]{:S(2)}, u32[]{:S(2)}) collective-permute-start(f32[8,128]{1,0:T(8,128)S(1)} %shard_map.112.u), channel_id=1, source_target_pairs={{0,3},{1,0},{2,1},{3,2},{4,7},{5,4},{6,5},{7,6},{8,11},{9,8},{10,9... | collective-permute-start | bytes 12296 | tf_op jit(solution)/shard_map/ppermute | solution.py:38
  179.4 5.7 %collective-permute-done.38.cross = f32[8,128]{1,0:T(8,128)S(1)} collective-permute-done((f32[8,128]{1,0:T(8,128)S(1)}, f32[8,128]{1,0:T(8,128)S(1)}, u32[]{:S(2)}, u32[]{:S(2)}) %collective-permute-start.38) | collective-permute-done | bytes 4128 | tf_op jit(solution)/shard_map/ppermute | solution.py:38
  191.6 5.7 %collective-permute-done.41.cross = f32[64,128]{1,0:T(8,128)S(1)} collective-permute-done((f32[64,128]{1,0:T(8,128)S(1)}, f32[64,128]{1,0:T(8,128)S(1)}, u32[]{:S(2)}, u32[]{:S(2)}) %collective-permute-start.41) | collective-permute-done | bytes 32800 | tf_op jit(solution)/shard_map/ppermute | solution.py:38
  205.1 5.7 %collective-permute-done.44.cross = f32[64,128]{1,0:T(8,128)S(1)} collective-permute-done((f32[64,128]{1,0:T(8,128)S(1)}, f32[64,128]{1,0:T(8,128)S(1)}, u32[]{:S(2)}, u32[]{:S(2)}) %collective-permute-start.44) | collective-permute-done | bytes 32800 | tf_op jit(solution)/shard_map/ppermute | solution.py:38
  (143 shorter events, 103.7 us)
Async XLA Ops:
  2.3 14.2 %collective-permute-start = (f32[64,128]{1,0:T(8,128)S(1)}, f32[64,128]{1,0:T(8,128)S(1)}, u32[]{:S(2)}, u32[]{:S(2)}) collective-permute-start(f32[64,128]{1,0:T(8,128)S(1)} %shard_map.100.x), channel_id=1, source_target_pairs={{0,1},{1,2},{2,3},{3,0},{4,5},{5,6},{6,7},{7,4},{8,9},{9,10},{10,1... | collective-permute-start | bytes 98312 | tf_op jit(solution)/shard_map/ppermute | solution.py:38
  4.3 12.3 %collective-permute-start.1 = (f32[64,128]{1,0:T(8,128)S(1)}, f32[64,128]{1,0:T(8,128)S(1)}, u32[]{:S(2)}, u32[]{:S(2)}) collective-permute-start(f32[64,128]{1,0:T(8,128)S(1)} %shard_map.100.x), channel_id=1, source_target_pairs={{0,3},{1,0},{2,1},{3,2},{4,7},{5,4},{6,5},{7,6},{8,11},{9,8},{10,9... | collective-permute-start | bytes 98312 | tf_op jit(solution)/shard_map/ppermute | solution.py:38
  6.5 10.1 %collective-permute-start.2 = (f32[64,128]{1,0:T(8,128)S(1)}, f32[64,128]{1,0:T(8,128)S(1)}, u32[]{:S(2)}, u32[]{:S(2)}) collective-permute-start(f32[64,128]{1,0:T(8,128)S(1)} %shard_map.100.x), channel_id=1, source_target_pairs={{3,4},{4,3},{7,8},{8,7},{11,12},{12,11},{15,16},{16,15},{19,20},{2... | collective-permute-start | bytes 98312 | tf_op jit(solution)/shard_map/ppermute | solution.py:38
  22.1 5.5 %collective-permute-start.3 = (f32[64,128]{1,0:T(8,128)S(1)}, f32[64,128]{1,0:T(8,128)S(1)}, u32[]{:S(2)}, u32[]{:S(2)}) collective-permute-start(f32[64,128]{1,0:T(8,128)S(1)} %shard_map.101.x), channel_id=1, source_target_pairs={{0,1},{1,2},{2,3},{3,0},{4,5},{5,6},{6,7},{7,4},{8,9},{9,10},{10,1... | collective-permute-start | bytes 98312 | tf_op jit(solution)/shard_map/ppermute | solution.py:38
  25.4 7.6 %collective-permute-start.5 = (f32[64,128]{1,0:T(8,128)S(1)}, f32[64,128]{1,0:T(8,128)S(1)}, u32[]{:S(2)}, u32[]{:S(2)}) collective-permute-start(f32[64,128]{1,0:T(8,128)S(1)} %shard_map.101.x), channel_id=1, source_target_pairs={{3,4},{4,3},{7,8},{8,7},{11,12},{12,11},{15,16},{16,15},{19,20},{2... | collective-permute-start | bytes 98312 | tf_op jit(solution)/shard_map/ppermute | solution.py:38
  38.6 13.0 %collective-permute-start.6 = (f32[8,128]{1,0:T(8,128)S(1)}, f32[8,128]{1,0:T(8,128)S(1)}, u32[]{:S(2)}, u32[]{:S(2)}) collective-permute-start(f32[8,128]{1,0:T(8,128)S(1)} %get-tuple-element.10.u), channel_id=1, source_target_pairs={{0,1},{1,2},{2,3},{3,0},{4,5},{5,6},{6,7},{7,4},{8,9},{9,10},{10,1... | collective-permute-start | bytes 12296 | tf_op jit(solution)/shard_map/ppermute | solution.py:38
  38.6 13.0 %collective-permute-start.7 = (f32[8,128]{1,0:T(8,128)S(1)}, f32[8,128]{1,0:T(8,128)S(1)}, u32[]{:S(2)}, u32[]{:S(2)}) collective-permute-start(f32[8,128]{1,0:T(8,128)S(1)} %get-tuple-element.10.u), channel_id=1, source_target_pairs={{0,3},{1,0},{2,1},{3,2},{4,7},{5,4},{6,5},{7,6},{8,11},{9,8},{10,9... | collective-permute-start | bytes 12296 | tf_op jit(solution)/shard_map/ppermute | solution.py:38
  41.8 9.8 %collective-permute-start.8 = (f32[8,128]{1,0:T(8,128)S(1)}, f32[8,128]{1,0:T(8,128)S(1)}, u32[]{:S(2)}, u32[]{:S(2)}) collective-permute-start(f32[8,128]{1,0:T(8,128)S(1)} %get-tuple-element.10.u), channel_id=1, source_target_pairs={{3,4},{4,3},{7,8},{8,7},{11,12},{12,11},{15,16},{16,15},{19,20},{2... | collective-permute-start | bytes 12296 | tf_op jit(solution)/shard_map/ppermute | solution.py:38
  55.5 7.4 %collective-permute-start.9 = (f32[8,128]{1,0:T(8,128)S(1)}, f32[8,128]{1,0:T(8,128)S(1)}, u32[]{:S(2)}, u32[]{:S(2)}) collective-permute-start(f32[8,128]{1,0:T(8,128)S(1)} %shard_map.103.u), channel_id=1, source_target_pairs={{0,1},{1,2},{2,3},{3,0},{4,5},{5,6},{6,7},{7,4},{8,9},{9,10},{10,1... | collective-permute-start | bytes 12296 | tf_op jit(solution)/shard_map/ppermute | solution.py:38
  55.5 7.4 %collective-permute-start.10 = (f32[8,128]{1,0:T(8,128)S(1)}, f32[8,128]{1,0:T(8,128)S(1)}, u32[]{:S(2)}, u32[]{:S(2)}) collective-permute-start(f32[8,128]{1,0:T(8,128)S(1)} %shard_map.103.u), channel_id=1, source_target_pairs={{0,3},{1,0},{2,1},{3,2},{4,7},{5,4},{6,5},{7,6},{8,11},{9,8},{10,9... | collective-permute-start | bytes 12296 | tf_op jit(solution)/shard_map/ppermute | solution.py:38
  58.7 7.3 %collective-permute-start.11 = (f32[8,128]{1,0:T(8,128)S(1)}, f32[8,128]{1,0:T(8,128)S(1)}, u32[]{:S(2)}, u32[]{:S(2)}) collective-permute-start(f32[8,128]{1,0:T(8,128)S(1)} %shard_map.103.u), channel_id=1, source_target_pairs={{3,4},{4,3},{7,8},{8,7},{11,12},{12,11},{15,16},{16,15},{19,20},{2... | collective-permute-start | bytes 12296 | tf_op jit(solution)/shard_map/ppermute | solution.py:38
  68.8 5.7 %collective-permute-start.12 = (f32[8,128]{1,0:T(8,128)S(1)}, f32[8,128]{1,0:T(8,128)S(1)}, u32[]{:S(2)}, u32[]{:S(2)}) collective-permute-start(f32[8,128]{1,0:T(8,128)S(1)} %shard_map.104.u), channel_id=1, source_target_pairs={{0,1},{1,2},{2,3},{3,0},{4,5},{5,6},{6,7},{7,4},{8,9},{9,10},{10,1... | collective-permute-start | bytes 12296 | tf_op jit(solution)/shard_map/ppermute | solution.py:38
  68.8 5.7 %collective-permute-start.13 = (f32[8,128]{1,0:T(8,128)S(1)}, f32[8,128]{1,0:T(8,128)S(1)}, u32[]{:S(2)}, u32[]{:S(2)}) collective-permute-start(f32[8,128]{1,0:T(8,128)S(1)} %shard_map.104.u), channel_id=1, source_target_pairs={{0,3},{1,0},{2,1},{3,2},{4,7},{5,4},{6,5},{7,6},{8,11},{9,8},{10,9... | collective-permute-start | bytes 12296 | tf_op jit(solution)/shard_map/ppermute | solution.py:38
  72.1 7.3 %collective-permute-start.14 = (f32[8,128]{1,0:T(8,128)S(1)}, f32[8,128]{1,0:T(8,128)S(1)}, u32[]{:S(2)}, u32[]{:S(2)}) collective-permute-start(f32[8,128]{1,0:T(8,128)S(1)} %shard_map.104.u), channel_id=1, source_target_pairs={{3,4},{4,3},{7,8},{8,7},{11,12},{12,11},{15,16},{16,15},{19,20},{2... | collective-permute-start | bytes 12296 | tf_op jit(solution)/shard_map/ppermute | solution.py:38
  86.5 7.6 %collective-permute-start.17 = (f32[64,128]{1,0:T(8,128)S(1)}, f32[64,128]{1,0:T(8,128)S(1)}, u32[]{:S(2)}, u32[]{:S(2)}) collective-permute-start(f32[64,128]{1,0:T(8,128)S(1)} %shard_map.105.x), channel_id=1, source_target_pairs={{3,4},{4,3},{7,8},{8,7},{11,12},{12,11},{15,16},{16,15},{19,20},{2... | collective-permute-start | bytes 98312 | tf_op jit(solution)/shard_map/ppermute | solution.py:38
  100.1 7.6 %collective-permute-start.20 = (f32[64,128]{1,0:T(8,128)S(1)}, f32[64,128]{1,0:T(8,128)S(1)}, u32[]{:S(2)}, u32[]{:S(2)}) collective-permute-start(f32[64,128]{1,0:T(8,128)S(1)} %shard_map.106.x), channel_id=1, source_target_pairs={{3,4},{4,3},{7,8},{8,7},{11,12},{12,11},{15,16},{16,15},{19,20},{2... | collective-permute-start | bytes 98312 | tf_op jit(solution)/shard_map/ppermute | solution.py:38
  113.6 7.6 %collective-permute-start.23 = (f32[64,128]{1,0:T(8,128)S(1)}, f32[64,128]{1,0:T(8,128)S(1)}, u32[]{:S(2)}, u32[]{:S(2)}) collective-permute-start(f32[64,128]{1,0:T(8,128)S(1)} %shard_map.107.x), channel_id=1, source_target_pairs={{3,4},{4,3},{7,8},{8,7},{11,12},{12,11},{15,16},{16,15},{19,20},{2... | collective-permute-start | bytes 98312 | tf_op jit(solution)/shard_map/ppermute | solution.py:38
  127.1 7.6 %collective-permute-start.26 = (f32[64,128]{1,0:T(8,128)S(1)}, f32[64,128]{1,0:T(8,128)S(1)}, u32[]{:S(2)}, u32[]{:S(2)}) collective-permute-start(f32[64,128]{1,0:T(8,128)S(1)} %shard_map.108.x), channel_id=1, source_target_pairs={{3,4},{4,3},{7,8},{8,7},{11,12},{12,11},{15,16},{16,15},{19,20},{2... | collective-permute-start | bytes 98312 | tf_op jit(solution)/shard_map/ppermute | solution.py:38
  140.7 7.6 %collective-permute-start.29 = (f32[64,128]{1,0:T(8,128)S(1)}, f32[64,128]{1,0:T(8,128)S(1)}, u32[]{:S(2)}, u32[]{:S(2)}) collective-permute-start(f32[64,128]{1,0:T(8,128)S(1)} %shard_map.109.x), channel_id=1, source_target_pairs={{3,4},{4,3},{7,8},{8,7},{11,12},{12,11},{15,16},{16,15},{19,20},{2... | collective-permute-start | bytes 98312 | tf_op jit(solution)/shard_map/ppermute | solution.py:38
  154.3 7.3 %collective-permute-start.32 = (f32[8,128]{1,0:T(8,128)S(1)}, f32[8,128]{1,0:T(8,128)S(1)}, u32[]{:S(2)}, u32[]{:S(2)}) collective-permute-start(f32[8,128]{1,0:T(8,128)S(1)} %get-tuple-element.12.u), channel_id=1, source_target_pairs={{3,4},{4,3},{7,8},{8,7},{11,12},{12,11},{15,16},{16,15},{19,20},{2... | collective-permute-start | bytes 12296 | tf_op jit(solution)/shard_map/ppermute | solution.py:38
  166.0 7.3 %collective-permute-start.35 = (f32[8,128]{1,0:T(8,128)S(1)}, f32[8,128]{1,0:T(8,128)S(1)}, u32[]{:S(2)}, u32[]{:S(2)}) collective-permute-start(f32[8,128]{1,0:T(8,128)S(1)} %shard_map.111.u), channel_id=1, source_target_pairs={{3,4},{4,3},{7,8},{8,7},{11,12},{12,11},{15,16},{16,15},{19,20},{2... | collective-permute-start | bytes 12296 | tf_op jit(solution)/shard_map/ppermute | solution.py:38
  177.8 7.3 %collective-permute-start.38 = (f32[8,128]{1,0:T(8,128)S(1)}, f32[8,128]{1,0:T(8,128)S(1)}, u32[]{:S(2)}, u32[]{:S(2)}) collective-permute-start(f32[8,128]{1,0:T(8,128)S(1)} %shard_map.112.u), channel_id=1, source_target_pairs={{3,4},{4,3},{7,8},{8,7},{11,12},{12,11},{15,16},{16,15},{19,20},{2... | collective-permute-start | bytes 12296 | tf_op jit(solution)/shard_map/ppermute | solution.py:38
  189.7 7.6 %collective-permute-start.41 = (f32[64,128]{1,0:T(8,128)S(1)}, f32[64,128]{1,0:T(8,128)S(1)}, u32[]{:S(2)}, u32[]{:S(2)}) collective-permute-start(f32[64,128]{1,0:T(8,128)S(1)} %shard_map.113.x), channel_id=1, source_target_pairs={{3,4},{4,3},{7,8},{8,7},{11,12},{12,11},{15,16},{16,15},{19,20},{2... | collective-permute-start | bytes 98312 | tf_op jit(solution)/shard_map/ppermute | solution.py:38
  203.2 7.6 %collective-permute-start.44 = (f32[64,128]{1,0:T(8,128)S(1)}, f32[64,128]{1,0:T(8,128)S(1)}, u32[]{:S(2)}, u32[]{:S(2)}) collective-permute-start(f32[64,128]{1,0:T(8,128)S(1)} %shard_map.114.x), channel_id=1, source_target_pairs={{3,4},{4,3},{7,8},{8,7},{11,12},{12,11},{15,16},{16,15},{19,20},{2... | collective-permute-start | bytes 98312 | tf_op jit(solution)/shard_map/ppermute | solution.py:38
  (43 other events, 391.5 us)
where the time goes:
time: 215 us; the launch traced here: 214 us
  waiting for transfers between devices  88.5 us (41%)
  starting transfers between devices  61.5 us (29%)
  Pallas kernels  32.3 us (15%)
  local copies, waits for them, and re-layouts  27.3 us (13%)
  other arithmetic  4.12 us (2%)
    ppermute x45, waiting for transfers between devices, exchange(): return [lax.ppermute(field, AXES, way) for way in ways]  88.5 us
    ppermute x45, starting transfers between devices, exchange(): return [lax.ppermute(field, AXES, way) for way in ways]  61.5 us
    pallas_call x16, Pallas kernels, call(): pl.pallas_call(kernel, out_shape=shapes if len(shapes) > 1 else shapes[0]...  32.3 us
    unnamed x47, local copies, waits for them, and re-layouts  17.3 us
    convert_element_type x2, local copies, waits for them, and re-layouts, shards(): jnp.transpose(coarse_off, (1, 2, 0, 3))  8.78 us
  transfers between devices with their start and end apart: 45, of which 24 were waited for; matrix products, arithmetic and copies ran while one was open for 8% of the time, Pallas kernels for 0%

commit v1 on v0

--- a/solution.py
+++ b/solution.py
@@ -35,7 +35,11 @@
 
 
 def exchange(field, ways):
-    return [lax.ppermute(field, AXES, way) for way in ways]
+    up, down, cross = ways
+    down = lax.ppermute(field, AXES, down)
+    up = lax.ppermute(field, AXES, up)
+    cross = lax.ppermute(field, AXES, cross)
+    return up, down, cross
 
 
 def iota(shape, dim):
@@ -85,17 +89,6 @@
 
 def take_lanes(field, places):
     return jnp.take_along_axis(field, places, axis=1, mode="promise_in_bounds")
-
-
-def apply_fine(blocks, fields, a_block):
-    acc = jnp.zeros((8, 8, LANES), F32)
-    for slot in range(blocks.shape[0]):
-        for g in range(4):
-            piece = blocks[slot, pl.ds(pl.multiple_of(a_block * 8, 8), 8), 16 * g : 16 * g + 16, :].astype(F32)
-            v = fields[slot, 16 * g : 16 * g + 16, :]
-            acc = acc + piece[:, :8] * v[None, :8]
-            acc = acc + piece[:, 8:] * v[None, 8:]
-    return fold_sublanes([acc[i] for i in range(8)])
 
 
 def neighbours(flags, up, down, cross):
@@ -124,46 +117,114 @@
             )
 
 
-def residual_into(res, rhs, diag, off, fields):
+def fold_rows(acc, block):
+    return fold_sublanes([acc[8 * block + i] for i in range(8)])
+
+
+def residual_into(res, rhs, diag, off, fields, acc):
     def body(ab, carry):
-        acc = jnp.zeros((8, 8, LANES), F32)
         rows = pl.ds(pl.multiple_of(ab * 8, 8), 8)
+        total = jnp.zeros((8, 8, LANES), F32)
         for slot in range(fields.shape[0]):
-            for g in range(4):
-                src = diag[rows, 16 * g : 16 * g + 16, :] if slot == 0 else off[slot - 1, rows, 16 * g : 16 * g + 16, :]
-                piece = src.astype(F32)
-                v = fields[slot, 16 * g : 16 * g + 16, :]
-                acc = acc + piece[:, :8] * v[None, :8]
-                acc = acc + piece[:, 8:] * v[None, 8:]
-        res[rows, :] = rhs[rows, :] - fold_sublanes([acc[i] for i in range(8)])
+            for g in range(8):
+                part = slice(8 * g, 8 * g + 8)
+                piece = diag[rows, part, :] if slot == 0 else off[slot - 1, rows, part, :]
+                total = total + piece * fields[slot, part, :][None]
+        acc[rows] = total
         return carry
 
     lax.fori_loop(0, 8, body, 0)
+    for ab in range(8):
+        rows = slice(8 * ab, 8 * ab + 8)
+        res[rows, :] = rhs[rows, :] - fold_rows(acc, ab)
 
 
 def smooth_into(out, x, inv, res):
-    def body(ab, carry):
-        acc = jnp.zeros((8, 8, LANES), F32)
-        rows = pl.ds(pl.multiple_of(ab * 8, 8), 8)
+    for ab in range(8):
+        rows = slice(8 * ab, 8 * ab + 8)
+        total = inv[rows, 0:8, :] * res[0:8, :][None]
+        for g in range(1, 8):
+            part = slice(8 * g, 8 * g + 8)
+            total = total + inv[rows, part, :] * res[part, :][None]
+        out[rows, :] = x[rows, :] + damping * fold_sublanes([total[i] for i in range(8)])
+
+
+def first_kernel(inv, rhs, out, inv_out, rhs_out, held, rhs_sem, sems):
+    copies = [
+        pltpu.make_async_copy(inv.at[pl.ds(8 * k, 8)], held.at[pl.ds(8 * k, 8)], sems.at[k])
+        for k in range(8)
+    ]
+    lead = pltpu.make_async_copy(rhs, rhs_out, rhs_sem)
+    lead.start()
+    for copy in copies:
+        copy.start()
+    lead.wait()
+    for k in range(8):
+        copies[k].wait()
+        rows = slice(8 * k, 8 * k + 8)
+        total = jnp.zeros((8, 8, LANES), F32)
         for g in range(4):
-            piece = inv[rows, 16 * g : 16 * g + 16, :].astype(F32)
-            v = res[16 * g : 16 * g + 16, :]
-            acc = acc + piece[:, :8] * v[None, :8]
-            acc = acc + piece[:, 8:] * v[None, 8:]
-        step = damping * fold_sublanes([acc[i] for i in range(8)])
-        out[rows, :] = step if x is None else x[rows, :] + step
+            piece = held[rows, 16 * g : 16 * g + 16, :].astype(F32)
+            inv_out[rows, 16 * g : 16 * g + 16, :] = piece
+            total = total + piece[:, :8] * rhs_out[16 * g : 16 * g + 8, :][None]
+            total = total + piece[:, 8:] * rhs_out[16 * g + 8 : 16 * g + 16, :][None]
+        out[rows, :] = damping * fold_sublanes([total[i] for i in range(8)])
+
+
+def widen_kernel(diag, off, diag_out, off_out, held, sems):
+    slots = off.shape[0]
+    copies = [pltpu.make_async_copy(diag, held.at[0], sems.at[0])]
+    for s in range(slots):
+        copies.append(pltpu.make_async_copy(off.at[s], held.at[s + 1], sems.at[s + 1]))
+    for copy in copies:
+        copy.start()
+    for s in range(slots + 1):
+        copies[s].wait()
+
+        def body(ab, carry):
+            rows = pl.ds(pl.multiple_of(ab * 8, 8), 8)
+            wide = held[s, rows].astype(F32)
+            if s == 0:
+                diag_out[rows] = wide
+            else:
+                off_out[s - 1, rows] = wide
+            return carry
+
+        lax.fori_loop(0, 8, body, 0)
+
+
+def coarse_prep_kernel(diag, off, inv, diag_out, off_out, inv_out, diag_in, off_in, inv_in, sems):
+    size = diag.shape[0]
+    copies = [
+        pltpu.make_async_copy(inv, inv_in, sems.at[0]),
+        pltpu.make_async_copy(diag, diag_in, sems.at[1]),
+        pltpu.make_async_copy(off, off_in, sems.at[2]),
+    ]
+    for copy in copies:
+        copy.start()
+    eye = jnp.where(iota((size, size), 0) == iota((size, size), 1), 1.0, 0.0).astype(jnp.bfloat16)
+
+    def turned(block):
+        return lax.dot_general(eye, block, (((1,), (1,)), ((), ())), preferred_element_type=F32)
+
+    for copy, src, dst in ((copies[0], inv_in, inv_out), (copies[1], diag_in, diag_out)):
+        copy.wait()
+        for r in range(8):
+            dst[r] = turned(jnp.concatenate([src[8 * h + r] for h in range(8)], axis=0))
+    copies[2].wait()
+
+    def body(a, carry):
+        for k in range(4):
+            block = jnp.concatenate([off_in[s, 4 * a + k] for s in range(off_in.shape[0])], axis=0)
+            off_out[4 * a + k] = turned(block)
         return carry
 
-    lax.fori_loop(0, 8, body, 0)
-
-
-def first_kernel(inv, rhs, out):
-    smooth_into(out, None, inv, rhs)
-
-
-def sweep_kernel(flags, columns, diag, off, inv, rhs, x, up, down, cross, out, fields, res):
+    lax.fori_loop(0, size // 4, body, 0)
+
+
+def sweep_kernel(flags, columns, diag, off, inv, rhs, x, up, down, cross, out, fields, res, acc):
     gather_fine(flags, columns, x, up, down, cross, fields)
-    residual_into(res, rhs, diag, off, fields)
+    residual_into(res, rhs, diag, off, fields, acc)
     smooth_into(out, x, inv, res)
 
 
@@ -175,20 +236,35 @@
     return out
 
 
-def small_apply(blocks, packed, extra=None, fields=None):
+def spread_rows(packed):
+    lane = iota((8, LANES), 1) & 15
+    return [take_lanes(packed, lane + 16 * h) for h in range(8)]
+
+
+def small_apply(blocks, fields):
+    parts = []
+    for r in range(8):
+        acc = blocks[r, 0:8, :] * fields[0]
+        for g in range(1, 8):
+            acc = acc + blocks[r, 8 * g : 8 * g + 8, :] * fields[g]
+        parts.append(acc)
+    return fold_sublanes(parts)
+
+
+def coarse_off_apply(off, fields):
     parts = []
     for ab in range(8):
-        acc = blocks[8 * ab : 8 * ab + 8] * packed[None]
-        if extra is not None:
-            for g in range(8):
-                acc = acc + extra[8 * ab : 8 * ab + 8, 8 * g : 8 * g + 8, :] * fields[g][None]
+        rows = slice(8 * ab, 8 * ab + 8)
+        acc = off[rows, 0:8, :] * fields[0][None]
+        for g in range(1, 8):
+            acc = acc + off[rows, 8 * g : 8 * g + 8, :] * fields[g][None]
         parts.append(fold_sublanes([acc[i] for i in range(8)]))
     return fold_lanes(parts)
 
 
-def restrict_kernel(flags, columns, diag, off, rhs, x, up, down, cross, agg, cinv, coarse_rhs, out, fields, res):
+def restrict_kernel(flags, columns, diag, off, rhs, x, up, down, cross, agg, cinv, coarse_rhs, out, fields, res, acc):
     gather_fine(flags, columns, x, up, down, cross, fields)
-    residual_into(res, rhs, diag, off, fields)
+    residual_into(res, rhs, diag, off, fields, acc)
     r = res[...]
     hi = r.astype(jnp.bfloat16)
     rest = r - hi.astype(F32)
@@ -199,9 +275,8 @@
     select = jnp.where(row_of == (iota((LANES, LANES), 0) & 15), 1.0, 0.0).astype(jnp.bfloat16)
     sums = lax.dot_general(parts, select, (((1,), (1,)), ((), ())), preferred_element_type=F32)
     full = sums[0:64] + (sums[64:128] + sums[128:192])
-    packed = pack_rows(full)
-    coarse_rhs[...] = packed
-    out[...] = damping * small_apply(cinv, packed)
+    coarse_rhs[...] = pack_rows(full)
+    out[...] = damping * small_apply(cinv, [full[8 * g : 8 * g + 8] for g in range(8)])
 
 
 def coarse_step(flags, columns, cdiag, coff, cinv, coarse_rhs, u, up, down, cross):
@@ -219,8 +294,8 @@
                 jnp.where(places < 16, take_lanes(mine, lane), take_lanes(right, lane)),
             )
         )
-    total = small_apply(cdiag, mine, coff, fields)
-    return mine + damping * small_apply(cinv, coarse_rhs[...] - total)
+    total = small_apply(cdiag, spread_rows(mine)) + coarse_off_apply(coff, fields)
+    return mine + damping * small_apply(cinv, spread_rows(coarse_rhs[...] - total))
 
 
 def coarse_kernel(flags, columns, cdiag, coff, cinv, coarse_rhs, u, up, down, cross, out):
@@ -243,22 +318,27 @@
 SM = pl.BlockSpec(memory_space=pltpu.SMEM)
 
 
-def call(kernel, outs, args, scratch=(), smem=False, flops=0, name=None):
+FAR = pl.BlockSpec(memory_space=pltpu.HBM)
+
+
+def call(kernel, outs, args, scratch=(), smem=False, far=False, limit=4, flops=0, moved=0):
     shapes = [pltpu.VMEM(shape, F32) for shape in outs]
-    specs = [VM] * len(args)
+    specs = [FAR if far else VM] * len(args)
     if smem:
         specs[0] = SM
-    args = [a if (smem and i == 0) else in_vmem(a) for i, a in enumerate(args)]
-    result = pl.pallas_call(
+    if far:
+        args = [pltpu.with_memory_space_constraint(a, pltpu.HBM) for a in args]
+    else:
+        args = [a if (smem and i == 0) else in_vmem(a) for i, a in enumerate(args)]
+    return pl.pallas_call(
         kernel,
         out_shape=shapes if len(shapes) > 1 else shapes[0],
         in_specs=specs,
         out_specs=[VM] * len(shapes) if len(shapes) > 1 else VM,
         scratch_shapes=list(scratch),
-        compiler_params=pltpu.CompilerParams(vmem_limit_bytes=4 * 1024 * 1024),
-        name=name,
+        compiler_params=pltpu.CompilerParams(vmem_limit_bytes=limit * 1024 * 1024),
+        cost_estimate=pl.CostEstimate(flops=flops, bytes_accessed=moved, transcendentals=0) if flops else None,
     )(*args)
-    return result
 
 
 def shards(
@@ -291,18 +371,14 @@
     columns = fine_columns - device * rows
     ccolumns = (coarse_columns - device * own_rows).reshape(1, cslots * own_rows)
     agg = aggregate.reshape(1, rows)
-    coff = jnp.transpose(coarse_off, (1, 2, 0, 3)).reshape(size, size, cslots * own_rows).astype(F32)
-
-    def packed_blocks(blocks):
-        split = blocks.reshape(size, 8, 8, own_rows)
-        return jnp.transpose(split, (0, 2, 1, 3)).reshape(size, 8, 8 * own_rows).astype(F32)
-
-    cdiag = packed_blocks(coarse_diag)
-    cinv = packed_blocks(coarse_inv)
-
     full = (size, rows)
     packed = (8, LANES)
-    scratch = [pltpu.VMEM((slots + 1,) + full, F32), pltpu.VMEM(full, F32)]
+    bf16 = jnp.bfloat16
+    scratch = [
+        pltpu.VMEM((slots + 1,) + full, F32),
+        pltpu.VMEM(full, F32),
+        pltpu.VMEM((size, 8, LANES), F32),
+    ]
 
     def sweep(x):
         return call(
@@ -313,7 +389,35 @@
             smem=True,
         )
 
-    x = call(first_kernel, [full], [fine_inv, right_side])
+    x, fine_inv, right_side = call(
+        first_kernel,
+        [full, fine_inv.shape, full],
+        [fine_inv, right_side],
+        [pltpu.VMEM(fine_inv.shape, bf16), pltpu.SemaphoreType.DMA(()), pltpu.SemaphoreType.DMA((8,))],
+        far=True,
+    )
+    fine_diag, fine_off = call(
+        widen_kernel,
+        [fine_diag.shape, fine_off.shape],
+        [fine_diag, fine_off],
+        [pltpu.VMEM((slots + 1, size, size, rows), bf16), pltpu.SemaphoreType.DMA((slots + 1,))],
+        far=True,
+        limit=12,
+    )
+    coarse = [
+        jnp.transpose(coarse_diag, (0, 2, 1)),
+        jnp.transpose(coarse_off, (0, 1, 3, 2)),
+        jnp.transpose(coarse_inv, (0, 2, 1)),
+    ]
+    turned = (8, size, LANES)
+    cdiag, coff, cinv = call(
+        coarse_prep_kernel,
+        [turned, (size, size, LANES), turned],
+        coarse,
+        [pltpu.VMEM(c.shape, bf16) for c in coarse] + [pltpu.SemaphoreType.DMA((3,))],
+        far=True,
+        limit=8,
+    )
     for cycle in range(CYCLES):
         for step in range(SWEEPS):
             if cycle or step:

time: 215 us -> 178 us (0.83)
  the two profiles are of different devices: /device:TPU:6 before, /device:TPU:0 now
where the time goes in v1:
time: 178 us
  waiting for transfers between devices  64.8 us (36%)
  starting transfers between devices  57.1 us (32%)
  Pallas kernels  39.8 us (22%)
  local copies, waits for them, and re-layouts  14.8 us (8%)
    ppermute x15, starting transfers between devices, exchange(): down = lax.ppermute(field, AXES, down)  51.5 us
    pallas_call x18, Pallas kernels, call(): pl.pallas_call(kernel, out_shape=shapes if len(shapes) > 1 else shapes[0]...  39.8 us
    ppermute x15, waiting for transfers between devices, exchange(): up = lax.ppermute(field, AXES, up)  38.8 us
    ppermute x15, waiting for transfers between devices, exchange(): cross = lax.ppermute(field, AXES, cross)  23.1 us
    unnamed x29, local copies, waits for them, and re-layouts  14.7 us
    ppermute x15, starting transfers between devices, exchange(): cross = lax.ppermute(field, AXES, cross)  4.83 us
  transfers between devices with their start and end apart: 45, of which 32 were waited for; matrix products, arithmetic and copies ran while one was open for 0% of the time, Pallas kernels for 5%

profile of v1, /device:TPU:0, one launch (start us, length us, event | category | flops | bytes accessed | tf_op | source)
XLA Modules:
  0.0 177.6 jit_solution(3394999812197327605)
XLA Ops:
  7.9 3.5 %shard_map.100 = (f32[64,64,128]{2,1,0:T(8,128)S(1)}, f32[6,64,64,128]{3,2,1,0:T(8,128)S(1)}) custom-call(bf16[64,64,128]{2,1,0:T(8,128)(2,1)} %diag.1, bf16[6,64,64,128]{3,2,1,0:T(8,128)(2,1)} %off.1), custom_call_target="tpu_custom_call" | custom-call | tf_op jit(solution)/shard_map/pallas_call | solution.py:333
  17.6 4.3 %collective-permute-start.4 = (f32[64,128]{1,0:T(8,128)S(1)}, f32[64,128]{1,0:T(8,128)S(1)}, u32[]{:S(2)}, u32[]{:S(2)}) collective-permute-start(f32[64,128]{1,0:T(8,128)S(1)} %shard_map.103.x), channel_id=1, source_target_pairs={{0,3},{1,0},{2,1},{3,2},{4,7},{5,4},{6,5},{7,6},{8,11},{9,8},{10,9... | collective-permute-start | bytes 98312 | tf_op jit(solution)/shard_map/ppermute | solution.py:39
  21.9 4.9 %shard_map.102 = (f32[8,64,128]{2,1,0:T(8,128)S(1)}, f32[64,64,128]{2,1,0:T(8,128)S(1)}, f32[8,64,128]{2,1,0:T(8,128)S(1)}) custom-call(bf16[64,16,64]{2,1,0:T(8,128)(2,1)} %bitcast.15, bf16[8,64,16,64]{3,2,1,0:T(8,128)(2,1)} %bitcast.14, bf16[64,16,64]{2,1,0:T(8,128)(2,1)} %bitcast.16), custom_call_target="tpu_custom_call" | custom-call | tf_op jit(solution)/shard_map/pallas_call | solution.py:333
  28.2 4.6 %copy-done.1 = f32[6,64,64,128]{3,2,1,0:T(8,128)S(1)} copy-done((f32[6,64,64,128]{3,2,1,0:T(8,128)S(1)}, f32[6,64,64,128]{3,2,1,0:T(8,128)}, u32[]{:S(2)}) %copy-start.1) | copy-done | bytes 12582936
  35.2 4.2 %collective-permute-start.7 = (f32[8,128]{1,0:T(8,128)S(1)}, f32[8,128]{1,0:T(8,128)S(1)}, u32[]{:S(2)}, u32[]{:S(2)}) collective-permute-start(f32[8,128]{1,0:T(8,128)S(1)} %get-tuple-element.26.u), channel_id=1, source_target_pairs={{0,3},{1,0},{2,1},{3,2},{4,7},{5,4},{6,5},{7,6},{8,11},{9,8},{10,9... | collective-permute-start | bytes 12296 | tf_op jit(solution)/shard_map/ppermute | solution.py:39
  40.8 3.5 %collective-permute-done.6.up = f32[8,128]{1,0:T(8,128)S(1)} collective-permute-done((f32[8,128]{1,0:T(8,128)S(1)}, f32[8,128]{1,0:T(8,128)S(1)}, u32[]{:S(2)}, u32[]{:S(2)}) %collective-permute-start.6) | collective-permute-done | bytes 4128 | tf_op jit(solution)/shard_map/ppermute | solution.py:40
  47.1 4.2 %collective-permute-start.10 = (f32[8,128]{1,0:T(8,128)S(1)}, f32[8,128]{1,0:T(8,128)S(1)}, u32[]{:S(2)}, u32[]{:S(2)}) collective-permute-start(f32[8,128]{1,0:T(8,128)S(1)} %shard_map.105.u), channel_id=1, source_target_pairs={{0,3},{1,0},{2,1},{3,2},{4,7},{5,4},{6,5},{7,6},{8,11},{9,8},{10,9... | collective-permute-start | bytes 12296 | tf_op jit(solution)/shard_map/ppermute | solution.py:39
  52.6 3.5 %collective-permute-done.9.up = f32[8,128]{1,0:T(8,128)S(1)} collective-permute-done((f32[8,128]{1,0:T(8,128)S(1)}, f32[8,128]{1,0:T(8,128)S(1)}, u32[]{:S(2)}, u32[]{:S(2)}) %collective-permute-start.9) | collective-permute-done | bytes 4128 | tf_op jit(solution)/shard_map/ppermute | solution.py:40
  57.3 4.3 %collective-permute-start.13 = (f32[8,128]{1,0:T(8,128)S(1)}, f32[8,128]{1,0:T(8,128)S(1)}, u32[]{:S(2)}, u32[]{:S(2)}) collective-permute-start(f32[8,128]{1,0:T(8,128)S(1)} %shard_map.106.u), channel_id=1, source_target_pairs={{0,3},{1,0},{2,1},{3,2},{4,7},{5,4},{6,5},{7,6},{8,11},{9,8},{10,9... | collective-permute-start | bytes 12296 | tf_op jit(solution)/shard_map/ppermute | solution.py:39
  62.9 3.5 %collective-permute-done.12.up = f32[8,128]{1,0:T(8,128)S(1)} collective-permute-done((f32[8,128]{1,0:T(8,128)S(1)}, f32[8,128]{1,0:T(8,128)S(1)}, u32[]{:S(2)}, u32[]{:S(2)}) %collective-permute-start.12) | collective-permute-done | bytes 4128 | tf_op jit(solution)/shard_map/ppermute | solution.py:40
  67.7 3.4 %collective-permute-start.16 = (f32[64,128]{1,0:T(8,128)S(1)}, f32[64,128]{1,0:T(8,128)S(1)}, u32[]{:S(2)}, u32[]{:S(2)}) collective-permute-start(f32[64,128]{1,0:T(8,128)S(1)} %shard_map.107.x), channel_id=1, source_target_pairs={{0,3},{1,0},{2,1},{3,2},{4,7},{5,4},{6,5},{7,6},{8,11},{9,8},{10,9... | collective-permute-start | bytes 98312 | tf_op jit(solution)/shard_map/ppermute | solution.py:39
  73.1 3.1 %collective-permute-done.15.up = f32[64,128]{1,0:T(8,128)S(1)} collective-permute-done((f32[64,128]{1,0:T(8,128)S(1)}, f32[64,128]{1,0:T(8,128)S(1)}, u32[]{:S(2)}, u32[]{:S(2)}) %collective-permute-start.15) | collective-permute-done | bytes 32800 | tf_op jit(solution)/shard_map/ppermute | solution.py:40
  76.2 4.6 %copy-done.2 = f32[6,64,64,128]{3,2,1,0:T(8,128)S(1)} copy-done((f32[6,64,64,128]{3,2,1,0:T(8,128)S(1)}, f32[6,64,64,128]{3,2,1,0:T(8,128)}, u32[]{:S(2)}) %copy-start.2) | copy-done | bytes 12582936
  83.3 3.7 %collective-permute-start.19 = (f32[64,128]{1,0:T(8,128)S(1)}, f32[64,128]{1,0:T(8,128)S(1)}, u32[]{:S(2)}, u32[]{:S(2)}) collective-permute-start(f32[64,128]{1,0:T(8,128)S(1)} %shard_map.108.x), channel_id=1, source_target_pairs={{0,3},{1,0},{2,1},{3,2},{4,7},{5,4},{6,5},{7,6},{8,11},{9,8},{10,9... | collective-permute-start | bytes 98312 | tf_op jit(solution)/shard_map/ppermute | solution.py:39
  88.8 3.3 %collective-permute-done.18.up = f32[64,128]{1,0:T(8,128)S(1)} collective-permute-done((f32[64,128]{1,0:T(8,128)S(1)}, f32[64,128]{1,0:T(8,128)S(1)}, u32[]{:S(2)}, u32[]{:S(2)}) %collective-permute-start.18) | collective-permute-done | bytes 32800 | tf_op jit(solution)/shard_map/ppermute | solution.py:40
  96.9 3.1 %collective-permute-done.23.cross = f32[64,128]{1,0:T(8,128)S(1)} collective-permute-done((f32[64,128]{1,0:T(8,128)S(1)}, f32[64,128]{1,0:T(8,128)S(1)}, u32[]{:S(2)}, u32[]{:S(2)}) %collective-permute-start.23) | collective-permute-done | bytes 32800 | tf_op jit(solution)/shard_map/ppermute | solution.py:41
  124.5 4.8 %collective-permute-start.31 = (f32[8,128]{1,0:T(8,128)S(1)}, f32[8,128]{1,0:T(8,128)S(1)}, u32[]{:S(2)}, u32[]{:S(2)}) collective-permute-start(f32[8,128]{1,0:T(8,128)S(1)} %get-tuple-element.28.u), channel_id=1, source_target_pairs={{0,3},{1,0},{2,1},{3,2},{4,7},{5,4},{6,5},{7,6},{8,11},{9,8},{10,9... | collective-permute-start | bytes 12296 | tf_op jit(solution)/shard_map/ppermute | solution.py:39
  130.6 3.5 %collective-permute-done.30.up = f32[8,128]{1,0:T(8,128)S(1)} collective-permute-done((f32[8,128]{1,0:T(8,128)S(1)}, f32[8,128]{1,0:T(8,128)S(1)}, u32[]{:S(2)}, u32[]{:S(2)}) %collective-permute-start.30) | collective-permute-done | bytes 4128 | tf_op jit(solution)/shard_map/ppermute | solution.py:40
  143.4 3.7 %collective-permute-start.37 = (f32[8,128]{1,0:T(8,128)S(1)}, f32[8,128]{1,0:T(8,128)S(1)}, u32[]{:S(2)}, u32[]{:S(2)}) collective-permute-start(f32[8,128]{1,0:T(8,128)S(1)} %shard_map.114.u), channel_id=1, source_target_pairs={{0,3},{1,0},{2,1},{3,2},{4,7},{5,4},{6,5},{7,6},{8,11},{9,8},{10,9... | collective-permute-start | bytes 12296 | tf_op jit(solution)/shard_map/ppermute | solution.py:39
  148.5 3.4 %collective-permute-done.36.up = f32[8,128]{1,0:T(8,128)S(1)} collective-permute-done((f32[8,128]{1,0:T(8,128)S(1)}, f32[8,128]{1,0:T(8,128)S(1)}, u32[]{:S(2)}, u32[]{:S(2)}) %collective-permute-start.36) | collective-permute-done | bytes 4128 | tf_op jit(solution)/shard_map/ppermute | solution.py:40
  153.2 3.3 %collective-permute-start.40 = (f32[64,128]{1,0:T(8,128)S(1)}, f32[64,128]{1,0:T(8,128)S(1)}, u32[]{:S(2)}, u32[]{:S(2)}) collective-permute-start(f32[64,128]{1,0:T(8,128)S(1)} %shard_map.115.x), channel_id=1, source_target_pairs={{0,3},{1,0},{2,1},{3,2},{4,7},{5,4},{6,5},{7,6},{8,11},{9,8},{10,9... | collective-permute-start | bytes 98312 | tf_op jit(solution)/shard_map/ppermute | solution.py:39
  158.6 3.0 %collective-permute-done.39.up = f32[64,128]{1,0:T(8,128)S(1)} collective-permute-done((f32[64,128]{1,0:T(8,128)S(1)}, f32[64,128]{1,0:T(8,128)S(1)}, u32[]{:S(2)}, u32[]{:S(2)}) %collective-permute-start.39) | collective-permute-done | bytes 32800 | tf_op jit(solution)/shard_map/ppermute | solution.py:40
  164.7 4.2 %collective-permute-start.43 = (f32[64,128]{1,0:T(8,128)S(1)}, f32[64,128]{1,0:T(8,128)S(1)}, u32[]{:S(2)}, u32[]{:S(2)}) collective-permute-start(f32[64,128]{1,0:T(8,128)S(1)} %shard_map.116.x), channel_id=1, source_target_pairs={{0,3},{1,0},{2,1},{3,2},{4,7},{5,4},{6,5},{7,6},{8,11},{9,8},{10,9... | collective-permute-start | bytes 98312 | tf_op jit(solution)/shard_map/ppermute | solution.py:39
  170.5 3.5 %collective-permute-done.42.up = f32[64,128]{1,0:T(8,128)S(1)} collective-permute-done((f32[64,128]{1,0:T(8,128)S(1)}, f32[64,128]{1,0:T(8,128)S(1)}, u32[]{:S(2)}, u32[]{:S(2)}) %collective-permute-start.42) | collective-permute-done | bytes 32800 | tf_op jit(solution)/shard_map/ppermute | solution.py:40
  (118 shorter events, 86.1 us)
Async XLA Ops:
  2.8 8.6 %collective-permute-start.2 = (f32[64,128]{1,0:T(8,128)S(1)}, f32[64,128]{1,0:T(8,128)S(1)}, u32[]{:S(2)}, u32[]{:S(2)}) collective-permute-start(f32[64,128]{1,0:T(8,128)S(1)} %get-tuple-element.24.x), channel_id=1, source_target_pairs={{3,4},{4,3},{7,8},{8,7},{11,12},{12,11},{15,16},{16,15},{19,20},{2... | collective-permute-start | bytes 98312 | tf_op jit(solution)/shard_map/ppermute | solution.py:41
  4.8 6.6 %collective-permute-start.1 = (f32[64,128]{1,0:T(8,128)S(1)}, f32[64,128]{1,0:T(8,128)S(1)}, u32[]{:S(2)}, u32[]{:S(2)}) collective-permute-start(f32[64,128]{1,0:T(8,128)S(1)} %get-tuple-element.24.x), channel_id=1, source_target_pairs={{0,3},{1,0},{2,1},{3,2},{4,7},{5,4},{6,5},{7,6},{8,11},{9,8},{10,9... | collective-permute-start | bytes 98312 | tf_op jit(solution)/shard_map/ppermute | solution.py:39
  16.0 12.2 %collective-permute-start.5 = (f32[64,128]{1,0:T(8,128)S(1)}, f32[64,128]{1,0:T(8,128)S(1)}, u32[]{:S(2)}, u32[]{:S(2)}) collective-permute-start(f32[64,128]{1,0:T(8,128)S(1)} %shard_map.103.x), channel_id=1, source_target_pairs={{3,4},{4,3},{7,8},{8,7},{11,12},{12,11},{15,16},{16,15},{19,20},{2... | collective-permute-start | bytes 98312 | tf_op jit(solution)/shard_map/ppermute | solution.py:41
  17.6 10.6 %collective-permute-start.4 = (f32[64,128]{1,0:T(8,128)S(1)}, f32[64,128]{1,0:T(8,128)S(1)}, u32[]{:S(2)}, u32[]{:S(2)}) collective-permute-start(f32[64,128]{1,0:T(8,128)S(1)} %shard_map.103.x), channel_id=1, source_target_pairs={{0,3},{1,0},{2,1},{3,2},{4,7},{5,4},{6,5},{7,6},{8,11},{9,8},{10,9... | collective-permute-start | bytes 98312 | tf_op jit(solution)/shard_map/ppermute | solution.py:39
  21.9 6.2 %collective-permute-start.3 = (f32[64,128]{1,0:T(8,128)S(1)}, f32[64,128]{1,0:T(8,128)S(1)}, u32[]{:S(2)}, u32[]{:S(2)}) collective-permute-start(f32[64,128]{1,0:T(8,128)S(1)} %shard_map.103.x), channel_id=1, source_target_pairs={{0,1},{1,2},{2,3},{3,0},{4,5},{5,6},{6,7},{7,4},{8,9},{9,10},{10,1... | collective-permute-start | bytes 98312 | tf_op jit(solution)/shard_map/ppermute | solution.py:40
  35.1 5.2 %collective-permute-start.8 = (f32[8,128]{1,0:T(8,128)S(1)}, f32[8,128]{1,0:T(8,128)S(1)}, u32[]{:S(2)}, u32[]{:S(2)}) collective-permute-start(f32[8,128]{1,0:T(8,128)S(1)} %get-tuple-element.26.u), channel_id=1, source_target_pairs={{3,4},{4,3},{7,8},{8,7},{11,12},{12,11},{15,16},{16,15},{19,20},{2... | collective-permute-start | bytes 12296 | tf_op jit(solution)/shard_map/ppermute | solution.py:41
  35.2 5.6 %collective-permute-start.7 = (f32[8,128]{1,0:T(8,128)S(1)}, f32[8,128]{1,0:T(8,128)S(1)}, u32[]{:S(2)}, u32[]{:S(2)}) collective-permute-start(f32[8,128]{1,0:T(8,128)S(1)} %get-tuple-element.26.u), channel_id=1, source_target_pairs={{0,3},{1,0},{2,1},{3,2},{4,7},{5,4},{6,5},{7,6},{8,11},{9,8},{10,9... | collective-permute-start | bytes 12296 | tf_op jit(solution)/shard_map/ppermute | solution.py:39
  47.1 5.5 %collective-permute-start.10 = (f32[8,128]{1,0:T(8,128)S(1)}, f32[8,128]{1,0:T(8,128)S(1)}, u32[]{:S(2)}, u32[]{:S(2)}) collective-permute-start(f32[8,128]{1,0:T(8,128)S(1)} %shard_map.105.u), channel_id=1, source_target_pairs={{0,3},{1,0},{2,1},{3,2},{4,7},{5,4},{6,5},{7,6},{8,11},{9,8},{10,9... | collective-permute-start | bytes 12296 | tf_op jit(solution)/shard_map/ppermute | solution.py:39
  57.3 5.6 %collective-permute-start.13 = (f32[8,128]{1,0:T(8,128)S(1)}, f32[8,128]{1,0:T(8,128)S(1)}, u32[]{:S(2)}, u32[]{:S(2)}) collective-permute-start(f32[8,128]{1,0:T(8,128)S(1)} %shard_map.106.u), channel_id=1, source_target_pairs={{0,3},{1,0},{2,1},{3,2},{4,7},{5,4},{6,5},{7,6},{8,11},{9,8},{10,9... | collective-permute-start | bytes 12296 | tf_op jit(solution)/shard_map/ppermute | solution.py:39
  67.6 5.5 %collective-permute-start.17 = (f32[64,128]{1,0:T(8,128)S(1)}, f32[64,128]{1,0:T(8,128)S(1)}, u32[]{:S(2)}, u32[]{:S(2)}) collective-permute-start(f32[64,128]{1,0:T(8,128)S(1)} %shard_map.107.x), channel_id=1, source_target_pairs={{3,4},{4,3},{7,8},{8,7},{11,12},{12,11},{15,16},{16,15},{19,20},{2... | collective-permute-start | bytes 98312 | tf_op jit(solution)/shard_map/ppermute | solution.py:41
  67.7 5.4 %collective-permute-start.16 = (f32[64,128]{1,0:T(8,128)S(1)}, f32[64,128]{1,0:T(8,128)S(1)}, u32[]{:S(2)}, u32[]{:S(2)}) collective-permute-start(f32[64,128]{1,0:T(8,128)S(1)} %shard_map.107.x), channel_id=1, source_target_pairs={{0,3},{1,0},{2,1},{3,2},{4,7},{5,4},{6,5},{7,6},{8,11},{9,8},{10,9... | collective-permute-start | bytes 98312 | tf_op jit(solution)/shard_map/ppermute | solution.py:39
  83.2 5.6 %collective-permute-start.20 = (f32[64,128]{1,0:T(8,128)S(1)}, f32[64,128]{1,0:T(8,128)S(1)}, u32[]{:S(2)}, u32[]{:S(2)}) collective-permute-start(f32[64,128]{1,0:T(8,128)S(1)} %shard_map.108.x), channel_id=1, source_target_pairs={{3,4},{4,3},{7,8},{8,7},{11,12},{12,11},{15,16},{16,15},{19,20},{2... | collective-permute-start | bytes 98312 | tf_op jit(solution)/shard_map/ppermute | solution.py:41
  83.3 5.5 %collective-permute-start.19 = (f32[64,128]{1,0:T(8,128)S(1)}, f32[64,128]{1,0:T(8,128)S(1)}, u32[]{:S(2)}, u32[]{:S(2)}) collective-permute-start(f32[64,128]{1,0:T(8,128)S(1)} %shard_map.108.x), channel_id=1, source_target_pairs={{0,3},{1,0},{2,1},{3,2},{4,7},{5,4},{6,5},{7,6},{8,11},{9,8},{10,9... | collective-permute-start | bytes 98312 | tf_op jit(solution)/shard_map/ppermute | solution.py:39
  94.5 5.5 %collective-permute-start.23 = (f32[64,128]{1,0:T(8,128)S(1)}, f32[64,128]{1,0:T(8,128)S(1)}, u32[]{:S(2)}, u32[]{:S(2)}) collective-permute-start(f32[64,128]{1,0:T(8,128)S(1)} %shard_map.109.x), channel_id=1, source_target_pairs={{3,4},{4,3},{7,8},{8,7},{11,12},{12,11},{15,16},{16,15},{19,20},{2... | collective-permute-start | bytes 98312 | tf_op jit(solution)/shard_map/ppermute | solution.py:41
  94.6 5.4 %collective-permute-start.22 = (f32[64,128]{1,0:T(8,128)S(1)}, f32[64,128]{1,0:T(8,128)S(1)}, u32[]{:S(2)}, u32[]{:S(2)}) collective-permute-start(f32[64,128]{1,0:T(8,128)S(1)} %shard_map.109.x), channel_id=1, source_target_pairs={{0,3},{1,0},{2,1},{3,2},{4,7},{5,4},{6,5},{7,6},{8,11},{9,8},{10,9... | collective-permute-start | bytes 98312 | tf_op jit(solution)/shard_map/ppermute | solution.py:39
  103.7 5.5 %collective-permute-start.26 = (f32[64,128]{1,0:T(8,128)S(1)}, f32[64,128]{1,0:T(8,128)S(1)}, u32[]{:S(2)}, u32[]{:S(2)}) collective-permute-start(f32[64,128]{1,0:T(8,128)S(1)} %shard_map.110.x), channel_id=1, source_target_pairs={{3,4},{4,3},{7,8},{8,7},{11,12},{12,11},{15,16},{16,15},{19,20},{2... | collective-permute-start | bytes 98312 | tf_op jit(solution)/shard_map/ppermute | solution.py:41
  103.8 5.4 %collective-permute-start.25 = (f32[64,128]{1,0:T(8,128)S(1)}, f32[64,128]{1,0:T(8,128)S(1)}, u32[]{:S(2)}, u32[]{:S(2)}) collective-permute-start(f32[64,128]{1,0:T(8,128)S(1)} %shard_map.110.x), channel_id=1, source_target_pairs={{0,3},{1,0},{2,1},{3,2},{4,7},{5,4},{6,5},{7,6},{8,11},{9,8},{10,9... | collective-permute-start | bytes 98312 | tf_op jit(solution)/shard_map/ppermute | solution.py:39
  113.9 5.8 %collective-permute-start.29 = (f32[64,128]{1,0:T(8,128)S(1)}, f32[64,128]{1,0:T(8,128)S(1)}, u32[]{:S(2)}, u32[]{:S(2)}) collective-permute-start(f32[64,128]{1,0:T(8,128)S(1)} %shard_map.111.x), channel_id=1, source_target_pairs={{3,4},{4,3},{7,8},{8,7},{11,12},{12,11},{15,16},{16,15},{19,20},{2... | collective-permute-start | bytes 98312 | tf_op jit(solution)/shard_map/ppermute | solution.py:41
  114.0 5.7 %collective-permute-start.28 = (f32[64,128]{1,0:T(8,128)S(1)}, f32[64,128]{1,0:T(8,128)S(1)}, u32[]{:S(2)}, u32[]{:S(2)}) collective-permute-start(f32[64,128]{1,0:T(8,128)S(1)} %shard_map.111.x), channel_id=1, source_target_pairs={{0,3},{1,0},{2,1},{3,2},{4,7},{5,4},{6,5},{7,6},{8,11},{9,8},{10,9... | collective-permute-start | bytes 98312 | tf_op jit(solution)/shard_map/ppermute | solution.py:39
  124.5 6.1 %collective-permute-start.31 = (f32[8,128]{1,0:T(8,128)S(1)}, f32[8,128]{1,0:T(8,128)S(1)}, u32[]{:S(2)}, u32[]{:S(2)}) collective-permute-start(f32[8,128]{1,0:T(8,128)S(1)} %get-tuple-element.28.u), channel_id=1, source_target_pairs={{0,3},{1,0},{2,1},{3,2},{4,7},{5,4},{6,5},{7,6},{8,11},{9,8},{10,9... | collective-permute-start | bytes 12296 | tf_op jit(solution)/shard_map/ppermute | solution.py:39
  153.1 5.5 %collective-permute-start.41 = (f32[64,128]{1,0:T(8,128)S(1)}, f32[64,128]{1,0:T(8,128)S(1)}, u32[]{:S(2)}, u32[]{:S(2)}) collective-permute-start(f32[64,128]{1,0:T(8,128)S(1)} %shard_map.115.x), channel_id=1, source_target_pairs={{3,4},{4,3},{7,8},{8,7},{11,12},{12,11},{15,16},{16,15},{19,20},{2... | collective-permute-start | bytes 98312 | tf_op jit(solution)/shard_map/ppermute | solution.py:41
  153.2 5.4 %collective-permute-start.40 = (f32[64,128]{1,0:T(8,128)S(1)}, f32[64,128]{1,0:T(8,128)S(1)}, u32[]{:S(2)}, u32[]{:S(2)}) collective-permute-start(f32[64,128]{1,0:T(8,128)S(1)} %shard_map.115.x), channel_id=1, source_target_pairs={{0,3},{1,0},{2,1},{3,2},{4,7},{5,4},{6,5},{7,6},{8,11},{9,8},{10,9... | collective-permute-start | bytes 98312 | tf_op jit(solution)/shard_map/ppermute | solution.py:39
  164.6 5.5 %collective-permute-start.44 = (f32[64,128]{1,0:T(8,128)S(1)}, f32[64,128]{1,0:T(8,128)S(1)}, u32[]{:S(2)}, u32[]{:S(2)}) collective-permute-start(f32[64,128]{1,0:T(8,128)S(1)} %shard_map.116.x), channel_id=1, source_target_pairs={{3,4},{4,3},{7,8},{8,7},{11,12},{12,11},{15,16},{16,15},{19,20},{2... | collective-permute-start | bytes 98312 | tf_op jit(solution)/shard_map/ppermute | solution.py:41
  164.7 5.8 %collective-permute-start.43 = (f32[64,128]{1,0:T(8,128)S(1)}, f32[64,128]{1,0:T(8,128)S(1)}, u32[]{:S(2)}, u32[]{:S(2)}) collective-permute-start(f32[64,128]{1,0:T(8,128)S(1)} %shard_map.116.x), channel_id=1, source_target_pairs={{0,3},{1,0},{2,1},{3,2},{4,7},{5,4},{6,5},{7,6},{8,11},{9,8},{10,9... | collective-permute-start | bytes 98312 | tf_op jit(solution)/shard_map/ppermute | solution.py:39
  (35 other events, 303.6 us)

commit v2 on v0

v2 whole, which is shorter than its diff:
```python
import jax
import jax.numpy as jnp
from jax import lax
from jax.experimental import pallas as pl
from jax.experimental.pallas import tpu as pltpu
from jax.sharding import PartitionSpec as P

SWEEPS = 2
CSWEEPS = 4
CYCLES = 2
AXES = ("brick", "group")
LINE = 4

damping = 0.7
LANES = 128
F32 = jnp.float32


def routes(count):
    lines = count // LINE
    cross, down, up = [], [], []
    for i in range(count):
        base = i - i % LINE
        up.append((i, base + (i + 1) % LINE))
        down.append((i, base + (i - 1) % LINE))
    for k in range(lines - 1):
        a, b = LINE * k + LINE - 1, LINE * k + LINE
        cross += [(a, b), (b, a)]
    for k in range(1, lines - 1):
        a, b = LINE * k + 1, LINE * k + 2
        cross += [(a, b), (b, a)]
    last = count - 1
    cross += [(0, 1), (1, 2), (2, 0), (last - 2, last - 1), (last - 1, last), (last, last - 2)]
    return cross, down, up


def exchange(field, ways):
    cross, down, up = ways
    cross = lax.ppermute(field, AXES, cross)
    down = lax.ppermute(field, AXES, down)
    up = lax.ppermute(field, AXES, up)
    return cross, down, up


def iota(shape, dim):
    return lax.broadcasted_iota(jnp.int32, shape, dim)


def fold_sublanes(parts):
    rows = iota(parts[0].shape, 0)
    shift = 4
    while shift:
        low = (rows & shift) == 0
        parts = [
            jnp.where(low, a, b) + pltpu.roll(jnp.where(low, b, a), 4 if shift == 4 else (8 - shift), 0)
            if shift == 4
            else fold_pair(a, b, low, shift, 0)
            for a, b in zip(parts[:shift], parts[shift:])
        ]
        shift //= 2
    return parts[0]


def fold_pair(a, b, low, shift, axis):
    size = a.shape[axis]
    own = jnp.where(low, a, b)
    other = jnp.where(low, b, a)
    return own + jnp.where(
        low, pltpu.roll(other, size - shift, axis), pltpu.roll(other, shift, axis)
    )


def fold_lanes(parts):
    lanes = iota(parts[0].shape, 1)
    shift, half = 64, 4
    while half:
        low = (lanes & shift) == 0
        if shift == 64:
            parts = [
                jnp.where(low, a, b) + pltpu.roll(jnp.where(low, b, a), 64, 1)
                for a, b in zip(parts[:half], parts[half:])
            ]
        else:
            parts = [fold_pair(a, b, low, shift, 1) for a, b in zip(parts[:half], parts[half:])]
        shift //= 2
        half //= 2
    return parts[0]


def take_lanes(field, places):
    return jnp.take_along_axis(field, places, axis=1, mode="promise_in_bounds")


def place_on_line():
    return lax.axis_index(AXES), lax.axis_size(AXES)


def neighbours(cross, down, up):
    device, count = place_on_line()
    spot = lax.rem(device, LINE)
    left = jnp.where(spot == 0, cross, up)
    right = jnp.where(spot == LINE - 1, cross, down)
    left = jnp.where(device == 0, 0.0, left)
    right = jnp.where(device == count - 1, 0.0, right)
    return left, right


def outer_lanes(shape):
    lanes = iota(shape, len(shape) - 1)
    return (lanes < 32) | (lanes >= 96)


def split_field(top, bottom):
    outer = outer_lanes(top.shape)
    turned = pltpu.roll(bottom, 64, top.ndim - 1)
    return jnp.where(outer, top, turned), jnp.where(outer, turned, top)


def join_field(rim, core):
    outer = outer_lanes(rim.shape)
    return jnp.where(outer, rim, core), pltpu.roll(jnp.where(outer, core, rim), 64, 1)


def pack_halves(top, bottom, outer):
    return jnp.where(outer, top, bottom) + pltpu.roll(jnp.where(outer, bottom, top), 64, 1)


def fold_all(acc, outer):
    rows = [fold_sublanes([acc[8 * k + i] for i in range(8)]) for k in range(8)]
    return [pack_halves(rows[k], rows[k + 4], outer) for k in range(4)]


def apply_slots(blocks, fields, acc):
    step = 16

    def body(ab, carry):
        rows = pl.ds(pl.multiple_of(ab * step, step), step)
        total = jnp.zeros((step, 8, LANES), F32)
        for slot in range(fields.shape[0]):
            for g in range(4):
                part = slice(8 * g, 8 * g + 8)
                total = total + blocks[slot, rows, part, :] * fields[slot, part, :][None]
        acc[rows] = total
        return carry

    lax.fori_loop(0, 64 // step, body, 0)


def apply_one(blocks, parts, outer):
    out = []
    for k in range(8):
        rows = slice(8 * k, 8 * k + 8)
        total = blocks[rows, 0:8, :] * parts[0][None]
        for g in range(1, 4):
            total = total + blocks[rows, 8 * g : 8 * g + 8, :] * parts[g][None]
        out.append(fold_sublanes([total[i] for i in range(8)]))
    return [pack_halves(out[k], out[k + 4], outer) for k in range(4)]


def home_lanes(is_rim):
    outer = outer_lanes((8, LANES))
    return outer if is_rim else jnp.logical_not(outer)


def gather_fields(columns, own, rim, core, outside, fields):
    is_rim = outside is not None
    home = home_lanes(is_rim)
    slots = fields.shape[0] - 1
    places = [jnp.broadcast_to(columns[s : s + 1, :], (8, LANES)) for s in range(slots)]
    lane = [jnp.where(home, p, p + 64) & (LANES - 1) for p in places]
    inner = [((p + 32) & 64) != 0 for p in places]
    inside = [(p >= 0) & (p < LANES) for p in places]
    for g in range(4):
        part = slice(8 * g, 8 * g + 8)
        fields[0, part, :] = own[part, :]
        if outside is not None:
            left, right = neighbours(*[o[part, :] for o in outside])
            beyond = jnp.where((iota((8, LANES), 1) & 32) == 0, right, left)
        for s in range(slots):
            edge = take_lanes(rim[part, :], lane[s])
            if outside is not None:
                edge = jnp.where(inside[s], edge, take_lanes(beyond, lane[s]))
            middle = take_lanes(core[part, :], lane[s])
            fields[s + 1, part, :] = jnp.where(inner[s], middle, edge)


def part_residual(columns, blocks, rhs, own, rim, core, outside, fields, acc):
    gather_fields(columns, own, rim, core, outside, fields)
    apply_slots(blocks, fields, acc)
    total = fold_all(acc, home_lanes(outside is not None))
    return [rhs[8 * g : 8 * g + 8, :] - total[g] for g in range(4)]


def part_sweep(columns, blocks, inv, rhs, own, rim, core, outside, fields, acc):
    res = part_residual(columns, blocks, rhs, own, rim, core, outside, fields, acc)
    step = apply_one(inv, res, home_lanes(outside is not None))
    return [own[8 * g : 8 * g + 8, :] + damping * step[g] for g in range(4)]


def rim_kernel(columns, blocks, inv, rhs, rim, core, cross, down, up, out, fields, acc):
    new = part_sweep(columns, blocks, inv, rhs, rim, rim, core, (cross, down, up), fields, acc)
    for g in range(4):
        out[8 * g : 8 * g + 8, :] = new[g]


def core_kernel(columns, blocks, inv, rhs, rim, core, out, fields, acc):
    new = part_sweep(columns, blocks, inv, rhs, core, rim, core, None, fields, acc)
    for g in range(4):
        out[8 * g : 8 * g + 8, :] = new[g]


def core_residual_kernel(columns, blocks, rhs, rim, core, out, fields, acc):
    res = part_residual(columns, blocks, rhs, core, rim, core, None, fields, acc)
    for g in range(4):
        out[8 * g : 8 * g + 8, :] = res[g]


def last_kernel(columns, blocks, inv, rhs, rim, core, cross, down, up, new_core, out, fields, acc, held, sem):
    new = part_sweep(columns, blocks, inv, rhs, rim, rim, core, (cross, down, up), fields, acc)
    for g in range(4):
        part = slice(8 * g, 8 * g + 8)
        top, bottom = join_field(new[g], new_core[part, :])
        held[part, :] = top
        held[32 + 8 * g : 40 + 8 * g, :] = bottom
    copy = pltpu.make_async_copy(held, out, sem)
    copy.start()
    copy.wait()


def first_kernel(
    inv, rhs, columns, agg, ccolumns,
    rim, core, rim_inv, core_inv, rim_rhs, core_rhs, rim_columns, core_columns, near,
    held, rhs_in, col_in, agg_in, ccol_in, sems,
):
    device, _ = place_on_line()
    copies = [pltpu.make_async_copy(rhs, rhs_in, sems.at[8])] + [
        pltpu.make_async_copy(inv.at[pl.ds(8 * k, 8)], held.at[pl.ds(8 * k, 8)], sems.at[k])
        for k in range(8)
    ]
    small = [
        pltpu.make_async_copy(columns, col_in, sems.at[9]),
        pltpu.make_async_copy(agg, agg_in, sems.at[10]),
        pltpu.make_async_copy(ccolumns, ccol_in, sems.at[11]),
    ]
    for copy in copies + small:
        copy.start()
    copies[0].wait()
    own = ([], [])
    for g in range(4):
        part = slice(8 * g, 8 * g + 8)
        edge, middle = split_field(rhs_in[part, :], rhs_in[32 + 8 * g : 40 + 8 * g, :])
        rim_rhs[part, :] = edge
        core_rhs[part, :] = middle
        own[0].append(edge)
        own[1].append(middle)
    sums = ([], [])
    for k in range(8):
        copies[k + 1].wait()
        rows = slice(8 * k, 8 * k + 8)
        wide = held[rows].astype(F32)
        both = split_field(wide[:, :32], wide[:, 32:])
        for blocks, piece, parts, kept in zip((rim_inv, core_inv), both, own, sums):
            blocks[rows] = piece
            total = piece[:, 0:8] * parts[0][None]
            for g in range(1, 4):
                total = total + piece[:, 8 * g : 8 * g + 8] * parts[g][None]
            kept.append(fold_sublanes([total[i] for i in range(8)]))
    for out, kept, home in ((rim, sums[0], True), (core, sums[1], False)):
        for g in range(4):
            total = pack_halves(kept[g], kept[g + 4], home_lanes(home))
            out[8 * g : 8 * g + 8, :] = damping * total
    for copy in small:
        copy.wait()
    slots = columns.shape[0]
    rows = iota((8, LANES), 0)
    table = jnp.broadcast_to(agg_in[...], (8, LANES))
    for s in range(slots):
        table = jnp.where(
            rows == s, jnp.broadcast_to(col_in[s : s + 1, :] - device * LANES, (8, LANES)), table
        )
    turned = pltpu.roll(table, 64, 1)
    outer = outer_lanes((8, LANES))
    rim_columns[...] = jnp.where(outer, table, turned)
    core_columns[...] = jnp.where(outer, turned, table)
    count = ccol_in.shape[1]
    tiled = jnp.concatenate([ccol_in[...]] * (LANES // count), axis=1)
    chosen = jnp.where(rows == iota((8, LANES), 1) // count, tiled - device * count, 0)
    near[...] = jnp.broadcast_to(jnp.sum(chosen, axis=0, keepdims=True), (8, LANES))


def widen_kernel(diag, off, rim_out, core_out, held, sems):
    slots = off.shape[0] + 1
    copies = [pltpu.make_async_copy(diag, held.at[0], sems.at[0])]
    for s in range(1, slots):
        copies.append(pltpu.make_async_copy(off.at[s - 1], held.at[s], sems.at[s]))
    for copy in copies:
        copy.start()
    for s in range(slots):
        copies[s].wait()

        def body(ab, carry):
            rows = pl.ds(pl.multiple_of(ab * 8, 8), 8)
            wide = held[s, rows].astype(F32)
            rim_out[s, rows], core_out[s, rows] = split_field(wide[:, :32], wide[:, 32:])
            return carry

        lax.fori_loop(0, 8, body, 0)


def turn(block):
    return jnp.transpose(block.astype(F32), (1, 0))


def coarse_ends_kernel(diag, inv, diag_out, inv_out):
    for src, dst in ((inv, inv_out), (diag, diag_out)):
        for r in range(8):
            dst[r] = turn(jnp.concatenate([src[8 * h + r] for h in range(8)], axis=0))


def coarse_off_kernel(off, off_out):
    slots, size = off.shape[:2]

    def body(i, carry):
        for j in range(8):
            a = 8 * i + j
            off_out[a] = turn(jnp.concatenate([off[s, a] for s in range(slots)], axis=0))
        return carry

    lax.fori_loop(0, size // 8, body, 0)


def pack_rows(full):
    group = iota((8, LANES), 1) // 16
    out = full[0:8, :]
    for g in range(1, 8):
        out = jnp.where(group == g, full[8 * g : 8 * g + 8, :], out)
    return out


def spread_rows(packed):
    lane = iota((8, LANES), 1) & 15
    return [take_lanes(packed, lane + 16 * h) for h in range(8)]


def small_apply(blocks, fields):
    parts = []
    for r in range(8):
        acc = blocks[r, 0:8, :] * fields[0]
        for g in range(1, 8):
            acc = acc + blocks[r, 8 * g : 8 * g + 8, :] * fields[g]
        parts.append(acc)
    return fold_sublanes(parts)


def coarse_off_apply(off, fields):
    parts = []
    for ab in range(8):
        rows = slice(8 * ab, 8 * ab + 8)
        acc = off[rows, 0:8, :] * fields[0][None]
        for g in range(1, 8):
            acc = acc + off[rows, 8 * g : 8 * g + 8, :] * fields[g][None]
        parts.append(fold_sublanes([acc[i] for i in range(8)]))
    return fold_lanes(parts)


def restrict_kernel(
    columns, blocks, rhs, rim, core, core_res, cross, down, up, core_columns, cinv,
    coarse_rhs, out, fields, acc,
):
    res = part_residual(columns, blocks, rhs, rim, rim, core, (cross, down, up), fields, acc)
    inner = core_res[...]
    edge = jnp.concatenate(res, axis=0)
    r = jnp.concatenate(join_field(edge, inner), axis=0)
    hi = r.astype(jnp.bfloat16)
    rest = r - hi.astype(F32)
    mid = rest.astype(jnp.bfloat16)
    last = (rest - mid.astype(F32)).astype(jnp.bfloat16)
    parts = jnp.concatenate([hi, mid, last], axis=0)
    slots = fields.shape[0] - 1
    agg = jnp.where(
        outer_lanes((1, LANES)), columns[slots : slots + 1, :], core_columns[slots : slots + 1, :]
    )
    row_of = jnp.broadcast_to(agg, (LANES, LANES))
    select = jnp.where(row_of == (iota((LANES, LANES), 0) & 15), 1.0, 0.0).astype(jnp.bfloat16)
    sums = lax.dot_general(parts, select, (((1,), (1,)), ((), ())), preferred_element_type=F32)
    full = sums[0:64] + (sums[64:128] + sums[128:192])
    coarse_rhs[...] = pack_rows(full)
    out[...] = damping * small_apply(cinv, [full[8 * g : 8 * g + 8] for g in range(8)])


def coarse_step(places, cdiag, coff, cinv, coarse_rhs, u, cross, down, up):
    left, right = neighbours(cross[...], down[...], up[...])
    places = places[...]
    inner = places & 15
    mine = u[...]
    fields = []
    for g in range(8):
        lane = inner + 16 * g
        fields.append(
            jnp.where(
                places < 0,
                take_lanes(left, lane),
                jnp.where(places < 16, take_lanes(mine, lane), take_lanes(right, lane)),
            )
        )
    total = small_apply(cdiag, spread_rows(mine)) + coarse_off_apply(coff, fields)
    return mine + damping * small_apply(cinv, spread_rows(coarse_rhs[...] - total))


def coarse_kernel(places, cdiag, coff, cinv, coarse_rhs, u, cross, down, up, out):
    out[...] = coarse_step(places, cdiag, coff, cinv, coarse_rhs, u, cross, down, up)


def prolong_kernel(
    places, cdiag, coff, cinv, coarse_rhs, u, cross, down, up, rim_columns, core_columns, rim, core,
    rim_out, core_out,
):
    last = coarse_step(places, cdiag, coff, cinv, coarse_rhs, u, cross, down, up)
    row = 6
    tables = ((rim_columns, rim, rim_out, True), (core_columns, core, core_out, False))
    for table, old, out, is_rim in tables:
        lane = jnp.broadcast_to(table[row : row + 1, :], (8, LANES))
        lane = jnp.where(home_lanes(is_rim), lane, lane + 64)
        for g in range(4):
            part = slice(8 * g, 8 * g + 8)
            out[part, :] = old[part, :] + take_lanes(last, lane + 16 * g)


def in_vmem(array):
    return pltpu.with_memory_space_constraint(array, pltpu.VMEM)


VM = pl.BlockSpec(memory_space=pltpu.VMEM)
FAR = pl.BlockSpec(memory_space=pltpu.HBM)


def call(kernel, outs, args, scratch=(), far=False, limit=4, flops=0, moved=0):
    shapes = [pltpu.VMEM(o[0], o[1]) if isinstance(o[0], tuple) else pltpu.VMEM(o, F32) for o in outs]
    place = pltpu.HBM if far else pltpu.VMEM
    return pl.pallas_call(
        kernel,
        out_shape=shapes if len(shapes) > 1 else shapes[0],
        in_specs=[pl.BlockSpec(memory_space=place)] * len(args),
        out_specs=[VM] * len(shapes) if len(shapes) > 1 else VM,
        scratch_shapes=list(scratch),
        compiler_params=pltpu.CompilerParams(vmem_limit_bytes=limit * 1024 * 1024),
    )(*[pltpu.with_memory_space_constraint(a, place) for a in args])


def shards(
    right_side,
    fine_diag,
    fine_off,
    fine_inv,
    fine_columns,
    aggregate,
    coarse_diag,
    coarse_off,
    coarse_inv,
    coarse_columns,
):
    size, rows = right_side.shape
    slots = fine_off.shape[0]
    own_rows = coarse_diag.shape[2]
    ways = routes(lax.axis_size(AXES))
    bf16 = jnp.bfloat16
    i32 = jnp.int32
    full = (size, rows)
    half = (size // 2, rows)
    packed = (8, LANES)
    table = ((8, LANES), i32)
    blocks = (slots + 1, size, size // 2, rows)
    turned = (8, size, LANES)
    sem = pltpu.SemaphoreType.DMA
    work = [pltpu.VMEM((slots + 1,) + half, F32), pltpu.VMEM((size, 8, LANES), F32)]

    rim, core, rim_inv, core_inv, rim_rhs, core_rhs, rim_cols, core_cols, near = call(
        first_kernel,
        [half, half, blocks[1:], blocks[1:], half, half, table, table, table],
        [fine_inv, right_side, fine_columns, aggregate.reshape(1, rows), coarse_columns],
        [
            pltpu.VMEM(fine_inv.shape, bf16),
            pltpu.VMEM(full, F32),
            pltpu.VMEM((slots, rows), i32),
            pltpu.VMEM((1, rows), i32),
            pltpu.VMEM(coarse_columns.shape, i32),
            sem((12,)),
        ],
        far=True,
    )
    sent = exchange(rim, ways)
    rim_blocks, core_blocks = call(
        widen_kernel,
        [blocks, blocks],
        [fine_diag, fine_off],
        [pltpu.VMEM((slots + 1, size, size, rows), bf16), sem((slots + 1,))],
        far=True,
        limit=12,
    )
    ends = [jnp.transpose(coarse_diag, (0, 2, 1)), jnp.transpose(coarse_inv, (0, 2, 1))]
    cdiag, cinv = call(coarse_ends_kernel, [turned, turned], ends)
    others = jnp.transpose(coarse_off, (0, 1, 3, 2))
    coff = call(coarse_off_kernel, [(size, size, LANES)], [others])

    def sweep_core(rim, core):
        return call(core_kernel, [half], [core_cols, core_blocks, core_inv, core_rhs, rim, core], work)

    def sweep_rim(rim, core, sent):
        args = [rim_cols, rim_blocks, rim_inv, rim_rhs, rim, core, *sent]
        return call(rim_kernel, [half], args, work)

    for cycle in range(CYCLES):
        for step in range(SWEEPS):
            if cycle or step:
                rim, core = sweep_rim(rim, core, sent), sweep_core(rim, core)
                sent = exchange(rim, ways)
        core_res = call(
            core_residual_kernel, [half], [core_cols, core_blocks, core_rhs, rim, core], work
        )
        crhs, u = call(
            restrict_kernel,
            [packed, packed],
            [rim_cols, rim_blocks, rim_rhs, rim, core, core_res, *sent, core_cols, cinv],
            work,
        )
        for step in range(1, CSWEEPS):
            base = [near, cdiag, coff, cinv, crhs, u, *exchange(u, ways)]
            if step < CSWEEPS - 1:
                u = call(coarse_kernel, [packed], base)
            else:
                rim, core = call(prolong_kernel, [half, half], base + [rim_cols, core_cols, rim, core])
        sent = exchange(rim, ways)
        for step in range(SWEEPS):
            if cycle == CYCLES - 1 and step == SWEEPS - 1:
                break
            rim, core = sweep_rim(rim, core, sent), sweep_core(rim, core)
            sent = exchange(rim, ways)
    args = [rim_cols, rim_blocks, rim_inv, rim_rhs, rim, core, *sent, sweep_core(rim, core)]
    return pl.pallas_call(
        last_kernel,
        out_shape=pltpu.HBM(full, F32),
        in_specs=[VM] * len(args),
        out_specs=FAR,
        scratch_shapes=work + [pltpu.VMEM(full, F32), sem(())],
        compiler_params=pltpu.CompilerParams(vmem_limit_bytes=4 * 1024 * 1024),
    )(*[in_vmem(a) for a in args])


def solution(mesh):
    placed = (
        P(None, AXES),
        P(None, None, AXES),
        P(None, None, None, AXES),
        P(None, None, AXES),
        P(None, AXES),
        P(AXES),
        P(None, None, AXES),
        P(None, None, None, AXES),
        P(None, None, AXES),
        P(None, AXES),
    )
    return jax.shard_map(
        shards, mesh=mesh, in_specs=placed, out_specs=P(None, AXES), check_vma=False
    )
```

time: 215 us -> 146 us (0.68)
  the two profiles are of different devices: /device:TPU:6 before, /device:TPU:25 now
where the time goes in v2:
time: 146 us
  starting transfers between devices  70.4 us (48%)
  waiting for transfers between devices  41.9 us (29%)
  Pallas kernels  33 us (23%)
    ppermute x15, starting transfers between devices, exchange(): down = lax.ppermute(field, AXES, down)  61.9 us
    ppermute x15, waiting for transfers between devices, exchange(): up = lax.ppermute(field, AXES, up)  35.9 us
    pallas_call x27, Pallas kernels, call(): pl.pallas_call(kernel, out_shape=shapes if len(shapes) > 1 else shapes[0]...  31.3 us
    ppermute x15, starting transfers between devices, exchange(): cross = lax.ppermute(field, AXES, cross)  6.95 us
    ppermute x15, waiting for transfers between devices, exchange(): down = lax.ppermute(field, AXES, down)  4.74 us
  transfers between devices with their start and end apart: 45, of which 22 were waited for; matrix products, arithmetic and copies ran while one was open for 0% of the time, Pallas kernels for 12%

profile of v2, /device:TPU:25, one launch (start us, length us, event | category | flops | bytes accessed | tf_op | source)
XLA Modules:
  0.0 145.8 jit_solution(12937203006515212405)
XLA Ops:
  2.2 4.0 %collective-permute-start = (f32[32,128]{1,0:T(8,128)S(1)}, f32[32,128]{1,0:T(8,128)S(1)}, u32[]{:S(2)}, u32[]{:S(2)}) collective-permute-start(f32[32,128]{1,0:T(8,128)S(1)} %get-tuple-element.33.rim), channel_id=1, source_target_pairs={{3,4},{4,3},{7,8},{8,7},{11,12},{12,11},{15,16},{16,15},{19,20},{2... | collective-permute-start | bytes 49160 | tf_op jit(solution)/shard_map/ppermute | solution.py:39
  7.6 6.2 %shard_map.101 = (f32[7,64,32,128]{3,2,1,0:T(8,128)S(1)}, f32[7,64,32,128]{3,2,1,0:T(8,128)S(1)}) custom-call(bf16[64,64,128]{2,1,0:T(8,128)(2,1)} %diag.1, bf16[6,64,64,128]{3,2,1,0:T(8,128)(2,1)} %off.1), custom_call_target="tpu_custom_call" | custom-call | tf_op jit(solution)/shard_map/pallas_call | solution.py:440
  16.3 5.1 %collective-permute-start.4 = (f32[32,128]{1,0:T(8,128)S(1)}, f32[32,128]{1,0:T(8,128)S(1)}, u32[]{:S(2)}, u32[]{:S(2)}) collective-permute-start(f32[32,128]{1,0:T(8,128)S(1)} %shard_map.104.rim), channel_id=1, source_target_pairs={{0,3},{1,0},{2,1},{3,2},{4,7},{5,4},{6,5},{7,6},{8,11},{9,8},{10,9... | collective-permute-start | bytes 49160 | tf_op jit(solution)/shard_map/ppermute | solution.py:40
  26.8 3.2 %collective-permute-start.7 = (f32[8,128]{1,0:T(8,128)S(1)}, f32[8,128]{1,0:T(8,128)S(1)}, u32[]{:S(2)}, u32[]{:S(2)}) collective-permute-start(f32[8,128]{1,0:T(8,128)S(1)} %get-tuple-element.40.u), channel_id=1, source_target_pairs={{0,3},{1,0},{2,1},{3,2},{4,7},{5,4},{6,5},{7,6},{8,11},{9,8},{10,9... | collective-permute-start | bytes 12296 | tf_op jit(solution)/shard_map/ppermute | solution.py:40
  34.7 4.9 %collective-permute-start.10 = (f32[8,128]{1,0:T(8,128)S(1)}, f32[8,128]{1,0:T(8,128)S(1)}, u32[]{:S(2)}, u32[]{:S(2)}) collective-permute-start(f32[8,128]{1,0:T(8,128)S(1)} %shard_map.108.u), channel_id=1, source_target_pairs={{0,3},{1,0},{2,1},{3,2},{4,7},{5,4},{6,5},{7,6},{8,11},{9,8},{10,9... | collective-permute-start | bytes 12296 | tf_op jit(solution)/shard_map/ppermute | solution.py:40
  40.3 2.9 %collective-permute-done.11.up = f32[8,128]{1,0:T(8,128)S(1)} collective-permute-done((f32[8,128]{1,0:T(8,128)S(1)}, f32[8,128]{1,0:T(8,128)S(1)}, u32[]{:S(2)}, u32[]{:S(2)}) %collective-permute-start.11) | collective-permute-done | bytes 4128 | tf_op jit(solution)/shard_map/ppermute | solution.py:41
  43.8 5.4 %collective-permute-start.13 = (f32[8,128]{1,0:T(8,128)S(1)}, f32[8,128]{1,0:T(8,128)S(1)}, u32[]{:S(2)}, u32[]{:S(2)}) collective-permute-start(f32[8,128]{1,0:T(8,128)S(1)} %shard_map.109.u), channel_id=1, source_target_pairs={{0,3},{1,0},{2,1},{3,2},{4,7},{5,4},{6,5},{7,6},{8,11},{9,8},{10,9... | collective-permute-start | bytes 12296 | tf_op jit(solution)/shard_map/ppermute | solution.py:40
  50.0 2.9 %collective-permute-done.14.up = f32[8,128]{1,0:T(8,128)S(1)} collective-permute-done((f32[8,128]{1,0:T(8,128)S(1)}, f32[8,128]{1,0:T(8,128)S(1)}, u32[]{:S(2)}, u32[]{:S(2)}) %collective-permute-start.14) | collective-permute-done | bytes 4128 | tf_op jit(solution)/shard_map/ppermute | solution.py:41
  53.6 5.6 %collective-permute-start.16 = (f32[32,128]{1,0:T(8,128)S(1)}, f32[32,128]{1,0:T(8,128)S(1)}, u32[]{:S(2)}, u32[]{:S(2)}) collective-permute-start(f32[32,128]{1,0:T(8,128)S(1)} %get-tuple-element.41.rim), channel_id=1, source_target_pairs={{0,3},{1,0},{2,1},{3,2},{4,7},{5,4},{6,5},{7,6},{8,11},{9,8},{10,9... | collective-permute-start | bytes 49160 | tf_op jit(solution)/shard_map/ppermute | solution.py:40
  60.1 2.9 %collective-permute-done.17.up = f32[32,128]{1,0:T(8,128)S(1)} collective-permute-done((f32[32,128]{1,0:T(8,128)S(1)}, f32[32,128]{1,0:T(8,128)S(1)}, u32[]{:S(2)}, u32[]{:S(2)}) %collective-permute-start.17) | collective-permute-done | bytes 16416 | tf_op jit(solution)/shard_map/ppermute | solution.py:41
  64.1 3.6 %collective-permute-start.19 = (f32[32,128]{1,0:T(8,128)S(1)}, f32[32,128]{1,0:T(8,128)S(1)}, u32[]{:S(2)}, u32[]{:S(2)}) collective-permute-start(f32[32,128]{1,0:T(8,128)S(1)} %shard_map.111.rim), channel_id=1, source_target_pairs={{0,3},{1,0},{2,1},{3,2},{4,7},{5,4},{6,5},{7,6},{8,11},{9,8},{10,9... | collective-permute-start | bytes 49160 | tf_op jit(solution)/shard_map/ppermute | solution.py:40
  68.9 2.7 %collective-permute-done.20.up = f32[32,128]{1,0:T(8,128)S(1)} collective-permute-done((f32[32,128]{1,0:T(8,128)S(1)}, f32[32,128]{1,0:T(8,128)S(1)}, u32[]{:S(2)}, u32[]{:S(2)}) %collective-permute-start.20) | collective-permute-done | bytes 16416 | tf_op jit(solution)/shard_map/ppermute | solution.py:41
  72.6 3.7 %collective-permute-start.22 = (f32[32,128]{1,0:T(8,128)S(1)}, f32[32,128]{1,0:T(8,128)S(1)}, u32[]{:S(2)}, u32[]{:S(2)}) collective-permute-start(f32[32,128]{1,0:T(8,128)S(1)} %shard_map.113.rim), channel_id=1, source_target_pairs={{0,3},{1,0},{2,1},{3,2},{4,7},{5,4},{6,5},{7,6},{8,11},{9,8},{10,9... | collective-permute-start | bytes 49160 | tf_op jit(solution)/shard_map/ppermute | solution.py:40
  81.2 3.8 %collective-permute-start.25 = (f32[32,128]{1,0:T(8,128)S(1)}, f32[32,128]{1,0:T(8,128)S(1)}, u32[]{:S(2)}, u32[]{:S(2)}) collective-permute-start(f32[32,128]{1,0:T(8,128)S(1)} %shard_map.115.rim), channel_id=1, source_target_pairs={{0,3},{1,0},{2,1},{3,2},{4,7},{5,4},{6,5},{7,6},{8,11},{9,8},{10,9... | collective-permute-start | bytes 49160 | tf_op jit(solution)/shard_map/ppermute | solution.py:40
  89.9 3.9 %collective-permute-start.28 = (f32[32,128]{1,0:T(8,128)S(1)}, f32[32,128]{1,0:T(8,128)S(1)}, u32[]{:S(2)}, u32[]{:S(2)}) collective-permute-start(f32[32,128]{1,0:T(8,128)S(1)} %shard_map.117.rim), channel_id=1, source_target_pairs={{0,3},{1,0},{2,1},{3,2},{4,7},{5,4},{6,5},{7,6},{8,11},{9,8},{10,9... | collective-permute-start | bytes 49160 | tf_op jit(solution)/shard_map/ppermute | solution.py:40
  99.4 3.0 %collective-permute-start.31 = (f32[8,128]{1,0:T(8,128)S(1)}, f32[8,128]{1,0:T(8,128)S(1)}, u32[]{:S(2)}, u32[]{:S(2)}) collective-permute-start(f32[8,128]{1,0:T(8,128)S(1)} %get-tuple-element.44.u), channel_id=1, source_target_pairs={{0,3},{1,0},{2,1},{3,2},{4,7},{5,4},{6,5},{7,6},{8,11},{9,8},{10,9... | collective-permute-start | bytes 12296 | tf_op jit(solution)/shard_map/ppermute | solution.py:40
  103.3 2.7 %collective-permute-done.32.up = f32[8,128]{1,0:T(8,128)S(1)} collective-permute-done((f32[8,128]{1,0:T(8,128)S(1)}, f32[8,128]{1,0:T(8,128)S(1)}, u32[]{:S(2)}, u32[]{:S(2)}) %collective-permute-start.32) | collective-permute-done | bytes 4128 | tf_op jit(solution)/shard_map/ppermute | solution.py:41
  106.7 4.6 %collective-permute-start.34 = (f32[8,128]{1,0:T(8,128)S(1)}, f32[8,128]{1,0:T(8,128)S(1)}, u32[]{:S(2)}, u32[]{:S(2)}) collective-permute-start(f32[8,128]{1,0:T(8,128)S(1)} %shard_map.121.u), channel_id=1, source_target_pairs={{0,3},{1,0},{2,1},{3,2},{4,7},{5,4},{6,5},{7,6},{8,11},{9,8},{10,9... | collective-permute-start | bytes 12296 | tf_op jit(solution)/shard_map/ppermute | solution.py:40
  112.1 2.9 %collective-permute-done.35.up = f32[8,128]{1,0:T(8,128)S(1)} collective-permute-done((f32[8,128]{1,0:T(8,128)S(1)}, f32[8,128]{1,0:T(8,128)S(1)}, u32[]{:S(2)}, u32[]{:S(2)}) %collective-permute-start.35) | collective-permute-done | bytes 4128 | tf_op jit(solution)/shard_map/ppermute | solution.py:41
  115.6 5.1 %collective-permute-start.37 = (f32[8,128]{1,0:T(8,128)S(1)}, f32[8,128]{1,0:T(8,128)S(1)}, u32[]{:S(2)}, u32[]{:S(2)}) collective-permute-start(f32[8,128]{1,0:T(8,128)S(1)} %shard_map.122.u), channel_id=1, source_target_pairs={{0,3},{1,0},{2,1},{3,2},{4,7},{5,4},{6,5},{7,6},{8,11},{9,8},{10,9... | collective-permute-start | bytes 12296 | tf_op jit(solution)/shard_map/ppermute | solution.py:40
  121.5 2.9 %collective-permute-done.38.up = f32[8,128]{1,0:T(8,128)S(1)} collective-permute-done((f32[8,128]{1,0:T(8,128)S(1)}, f32[8,128]{1,0:T(8,128)S(1)}, u32[]{:S(2)}, u32[]{:S(2)}) %collective-permute-start.38) | collective-permute-done | bytes 4128 | tf_op jit(solution)/shard_map/ppermute | solution.py:41
  125.1 6.4 %collective-permute-start.40 = (f32[32,128]{1,0:T(8,128)S(1)}, f32[32,128]{1,0:T(8,128)S(1)}, u32[]{:S(2)}, u32[]{:S(2)}) collective-permute-start(f32[32,128]{1,0:T(8,128)S(1)} %get-tuple-element.45.rim), channel_id=1, source_target_pairs={{0,3},{1,0},{2,1},{3,2},{4,7},{5,4},{6,5},{7,6},{8,11},{9,8},{10,9... | collective-permute-start | bytes 49160 | tf_op jit(solution)/shard_map/ppermute | solution.py:40
  132.4 2.9 %collective-permute-done.41.up = f32[32,128]{1,0:T(8,128)S(1)} collective-permute-done((f32[32,128]{1,0:T(8,128)S(1)}, f32[32,128]{1,0:T(8,128)S(1)}, u32[]{:S(2)}, u32[]{:S(2)}) %collective-permute-start.41) | collective-permute-done | bytes 16416 | tf_op jit(solution)/shard_map/ppermute | solution.py:41
  136.4 3.6 %collective-permute-start.43 = (f32[32,128]{1,0:T(8,128)S(1)}, f32[32,128]{1,0:T(8,128)S(1)}, u32[]{:S(2)}, u32[]{:S(2)}) collective-permute-start(f32[32,128]{1,0:T(8,128)S(1)} %shard_map.124.rim), channel_id=1, source_target_pairs={{0,3},{1,0},{2,1},{3,2},{4,7},{5,4},{6,5},{7,6},{8,11},{9,8},{10,9... | collective-permute-start | bytes 49160 | tf_op jit(solution)/shard_map/ppermute | solution.py:40
  (100 shorter events, 50.2 us)
Async XLA Ops:
  2.2 11.7 %collective-permute-start = (f32[32,128]{1,0:T(8,128)S(1)}, f32[32,128]{1,0:T(8,128)S(1)}, u32[]{:S(2)}, u32[]{:S(2)}) collective-permute-start(f32[32,128]{1,0:T(8,128)S(1)} %get-tuple-element.33.rim), channel_id=1, source_target_pairs={{3,4},{4,3},{7,8},{8,7},{11,12},{12,11},{15,16},{16,15},{19,20},{2... | collective-permute-start | bytes 49160 | tf_op jit(solution)/shard_map/ppermute | solution.py:39
  6.2 7.7 %collective-permute-start.1 = (f32[32,128]{1,0:T(8,128)S(1)}, f32[32,128]{1,0:T(8,128)S(1)}, u32[]{:S(2)}, u32[]{:S(2)}) collective-permute-start(f32[32,128]{1,0:T(8,128)S(1)} %get-tuple-element.33.rim), channel_id=1, source_target_pairs={{0,3},{1,0},{2,1},{3,2},{4,7},{5,4},{6,5},{7,6},{8,11},{9,8},{10,9... | collective-permute-start | bytes 49160 | tf_op jit(solution)/shard_map/ppermute | solution.py:40
  6.2 7.7 %collective-permute-start.2 = (f32[32,128]{1,0:T(8,128)S(1)}, f32[32,128]{1,0:T(8,128)S(1)}, u32[]{:S(2)}, u32[]{:S(2)}) collective-permute-start(f32[32,128]{1,0:T(8,128)S(1)} %get-tuple-element.33.rim), channel_id=1, source_target_pairs={{0,1},{1,2},{2,3},{3,0},{4,5},{5,6},{6,7},{7,4},{8,9},{9,10},{10,1... | collective-permute-start | bytes 49160 | tf_op jit(solution)/shard_map/ppermute | solution.py:41
  15.0 8.7 %collective-permute-start.3 = (f32[32,128]{1,0:T(8,128)S(1)}, f32[32,128]{1,0:T(8,128)S(1)}, u32[]{:S(2)}, u32[]{:S(2)}) collective-permute-start(f32[32,128]{1,0:T(8,128)S(1)} %shard_map.104.rim), channel_id=1, source_target_pairs={{3,4},{4,3},{7,8},{8,7},{11,12},{12,11},{15,16},{16,15},{19,20},{2... | collective-permute-start | bytes 49160 | tf_op jit(solution)/shard_map/ppermute | solution.py:39
  16.3 7.3 %collective-permute-start.4 = (f32[32,128]{1,0:T(8,128)S(1)}, f32[32,128]{1,0:T(8,128)S(1)}, u32[]{:S(2)}, u32[]{:S(2)}) collective-permute-start(f32[32,128]{1,0:T(8,128)S(1)} %shard_map.104.rim), channel_id=1, source_target_pairs={{0,3},{1,0},{2,1},{3,2},{4,7},{5,4},{6,5},{7,6},{8,11},{9,8},{10,9... | collective-permute-start | bytes 49160 | tf_op jit(solution)/shard_map/ppermute | solution.py:40
  34.2 5.3 %collective-permute-start.9 = (f32[8,128]{1,0:T(8,128)S(1)}, f32[8,128]{1,0:T(8,128)S(1)}, u32[]{:S(2)}, u32[]{:S(2)}) collective-permute-start(f32[8,128]{1,0:T(8,128)S(1)} %shard_map.108.u), channel_id=1, source_target_pairs={{3,4},{4,3},{7,8},{8,7},{11,12},{12,11},{15,16},{16,15},{19,20},{2... | collective-permute-start | bytes 12296 | tf_op jit(solution)/shard_map/ppermute | solution.py:39
  34.7 5.6 %collective-permute-start.10 = (f32[8,128]{1,0:T(8,128)S(1)}, f32[8,128]{1,0:T(8,128)S(1)}, u32[]{:S(2)}, u32[]{:S(2)}) collective-permute-start(f32[8,128]{1,0:T(8,128)S(1)} %shard_map.108.u), channel_id=1, source_target_pairs={{0,3},{1,0},{2,1},{3,2},{4,7},{5,4},{6,5},{7,6},{8,11},{9,8},{10,9... | collective-permute-start | bytes 12296 | tf_op jit(solution)/shard_map/ppermute | solution.py:40
  43.8 5.5 %collective-permute-start.12 = (f32[8,128]{1,0:T(8,128)S(1)}, f32[8,128]{1,0:T(8,128)S(1)}, u32[]{:S(2)}, u32[]{:S(2)}) collective-permute-start(f32[8,128]{1,0:T(8,128)S(1)} %shard_map.109.u), channel_id=1, source_target_pairs={{3,4},{4,3},{7,8},{8,7},{11,12},{12,11},{15,16},{16,15},{19,20},{2... | collective-permute-start | bytes 12296 | tf_op jit(solution)/shard_map/ppermute | solution.py:39
  43.8 6.1 %collective-permute-start.13 = (f32[8,128]{1,0:T(8,128)S(1)}, f32[8,128]{1,0:T(8,128)S(1)}, u32[]{:S(2)}, u32[]{:S(2)}) collective-permute-start(f32[8,128]{1,0:T(8,128)S(1)} %shard_map.109.u), channel_id=1, source_target_pairs={{0,3},{1,0},{2,1},{3,2},{4,7},{5,4},{6,5},{7,6},{8,11},{9,8},{10,9... | collective-permute-start | bytes 12296 | tf_op jit(solution)/shard_map/ppermute | solution.py:40
  53.5 5.7 %collective-permute-start.15 = (f32[32,128]{1,0:T(8,128)S(1)}, f32[32,128]{1,0:T(8,128)S(1)}, u32[]{:S(2)}, u32[]{:S(2)}) collective-permute-start(f32[32,128]{1,0:T(8,128)S(1)} %get-tuple-element.41.rim), channel_id=1, source_target_pairs={{3,4},{4,3},{7,8},{8,7},{11,12},{12,11},{15,16},{16,15},{19,20},{2... | collective-permute-start | bytes 49160 | tf_op jit(solution)/shard_map/ppermute | solution.py:39
  53.6 6.5 %collective-permute-start.16 = (f32[32,128]{1,0:T(8,128)S(1)}, f32[32,128]{1,0:T(8,128)S(1)}, u32[]{:S(2)}, u32[]{:S(2)}) collective-permute-start(f32[32,128]{1,0:T(8,128)S(1)} %get-tuple-element.41.rim), channel_id=1, source_target_pairs={{0,3},{1,0},{2,1},{3,2},{4,7},{5,4},{6,5},{7,6},{8,11},{9,8},{10,9... | collective-permute-start | bytes 49160 | tf_op jit(solution)/shard_map/ppermute | solution.py:40
  72.6 4.9 %collective-permute-start.21 = (f32[32,128]{1,0:T(8,128)S(1)}, f32[32,128]{1,0:T(8,128)S(1)}, u32[]{:S(2)}, u32[]{:S(2)}) collective-permute-start(f32[32,128]{1,0:T(8,128)S(1)} %shard_map.113.rim), channel_id=1, source_target_pairs={{3,4},{4,3},{7,8},{8,7},{11,12},{12,11},{15,16},{16,15},{19,20},{2... | collective-permute-start | bytes 49160 | tf_op jit(solution)/shard_map/ppermute | solution.py:39
  72.6 4.8 %collective-permute-start.22 = (f32[32,128]{1,0:T(8,128)S(1)}, f32[32,128]{1,0:T(8,128)S(1)}, u32[]{:S(2)}, u32[]{:S(2)}) collective-permute-start(f32[32,128]{1,0:T(8,128)S(1)} %shard_map.113.rim), channel_id=1, source_target_pairs={{0,3},{1,0},{2,1},{3,2},{4,7},{5,4},{6,5},{7,6},{8,11},{9,8},{10,9... | collective-permute-start | bytes 49160 | tf_op jit(solution)/shard_map/ppermute | solution.py:40
  81.2 4.9 %collective-permute-start.24 = (f32[32,128]{1,0:T(8,128)S(1)}, f32[32,128]{1,0:T(8,128)S(1)}, u32[]{:S(2)}, u32[]{:S(2)}) collective-permute-start(f32[32,128]{1,0:T(8,128)S(1)} %shard_map.115.rim), channel_id=1, source_target_pairs={{3,4},{4,3},{7,8},{8,7},{11,12},{12,11},{15,16},{16,15},{19,20},{2... | collective-permute-start | bytes 49160 | tf_op jit(solution)/shard_map/ppermute | solution.py:39
  81.2 4.9 %collective-permute-start.25 = (f32[32,128]{1,0:T(8,128)S(1)}, f32[32,128]{1,0:T(8,128)S(1)}, u32[]{:S(2)}, u32[]{:S(2)}) collective-permute-start(f32[32,128]{1,0:T(8,128)S(1)} %shard_map.115.rim), channel_id=1, source_target_pairs={{0,3},{1,0},{2,1},{3,2},{4,7},{5,4},{6,5},{7,6},{8,11},{9,8},{10,9... | collective-permute-start | bytes 49160 | tf_op jit(solution)/shard_map/ppermute | solution.py:40
  89.8 6.0 %collective-permute-start.27 = (f32[32,128]{1,0:T(8,128)S(1)}, f32[32,128]{1,0:T(8,128)S(1)}, u32[]{:S(2)}, u32[]{:S(2)}) collective-permute-start(f32[32,128]{1,0:T(8,128)S(1)} %shard_map.117.rim), channel_id=1, source_target_pairs={{3,4},{4,3},{7,8},{8,7},{11,12},{12,11},{15,16},{16,15},{19,20},{2... | collective-permute-start | bytes 49160 | tf_op jit(solution)/shard_map/ppermute | solution.py:39
  89.9 5.9 %collective-permute-start.28 = (f32[32,128]{1,0:T(8,128)S(1)}, f32[32,128]{1,0:T(8,128)S(1)}, u32[]{:S(2)}, u32[]{:S(2)}) collective-permute-start(f32[32,128]{1,0:T(8,128)S(1)} %shard_map.117.rim), channel_id=1, source_target_pairs={{0,3},{1,0},{2,1},{3,2},{4,7},{5,4},{6,5},{7,6},{8,11},{9,8},{10,9... | collective-permute-start | bytes 49160 | tf_op jit(solution)/shard_map/ppermute | solution.py:40
  106.7 5.4 %collective-permute-start.34 = (f32[8,128]{1,0:T(8,128)S(1)}, f32[8,128]{1,0:T(8,128)S(1)}, u32[]{:S(2)}, u32[]{:S(2)}) collective-permute-start(f32[8,128]{1,0:T(8,128)S(1)} %shard_map.121.u), channel_id=1, source_target_pairs={{0,3},{1,0},{2,1},{3,2},{4,7},{5,4},{6,5},{7,6},{8,11},{9,8},{10,9... | collective-permute-start | bytes 12296 | tf_op jit(solution)/shard_map/ppermute | solution.py:40
  115.5 5.2 %collective-permute-start.36 = (f32[8,128]{1,0:T(8,128)S(1)}, f32[8,128]{1,0:T(8,128)S(1)}, u32[]{:S(2)}, u32[]{:S(2)}) collective-permute-start(f32[8,128]{1,0:T(8,128)S(1)} %shard_map.122.u), channel_id=1, source_target_pairs={{3,4},{4,3},{7,8},{8,7},{11,12},{12,11},{15,16},{16,15},{19,20},{2... | collective-permute-start | bytes 12296 | tf_op jit(solution)/shard_map/ppermute | solution.py:39
  115.6 5.9 %collective-permute-start.37 = (f32[8,128]{1,0:T(8,128)S(1)}, f32[8,128]{1,0:T(8,128)S(1)}, u32[]{:S(2)}, u32[]{:S(2)}) collective-permute-start(f32[8,128]{1,0:T(8,128)S(1)} %shard_map.122.u), channel_id=1, source_target_pairs={{0,3},{1,0},{2,1},{3,2},{4,7},{5,4},{6,5},{7,6},{8,11},{9,8},{10,9... | collective-permute-start | bytes 12296 | tf_op jit(solution)/shard_map/ppermute | solution.py:40
  125.1 6.5 %collective-permute-start.39 = (f32[32,128]{1,0:T(8,128)S(1)}, f32[32,128]{1,0:T(8,128)S(1)}, u32[]{:S(2)}, u32[]{:S(2)}) collective-permute-start(f32[32,128]{1,0:T(8,128)S(1)} %get-tuple-element.45.rim), channel_id=1, source_target_pairs={{3,4},{4,3},{7,8},{8,7},{11,12},{12,11},{15,16},{16,15},{19,20},{2... | collective-permute-start | bytes 49160 | tf_op jit(solution)/shard_map/ppermute | solution.py:39
  125.1 7.3 %collective-permute-start.40 = (f32[32,128]{1,0:T(8,128)S(1)}, f32[32,128]{1,0:T(8,128)S(1)}, u32[]{:S(2)}, u32[]{:S(2)}) collective-permute-start(f32[32,128]{1,0:T(8,128)S(1)} %get-tuple-element.45.rim), channel_id=1, source_target_pairs={{0,3},{1,0},{2,1},{3,2},{4,7},{5,4},{6,5},{7,6},{8,11},{9,8},{10,9... | collective-permute-start | bytes 49160 | tf_op jit(solution)/shard_map/ppermute | solution.py:40
  136.4 5.9 %collective-permute-start.42 = (f32[32,128]{1,0:T(8,128)S(1)}, f32[32,128]{1,0:T(8,128)S(1)}, u32[]{:S(2)}, u32[]{:S(2)}) collective-permute-start(f32[32,128]{1,0:T(8,128)S(1)} %shard_map.124.rim), channel_id=1, source_target_pairs={{3,4},{4,3},{7,8},{8,7},{11,12},{12,11},{15,16},{16,15},{19,20},{2... | collective-permute-start | bytes 49160 | tf_op jit(solution)/shard_map/ppermute | solution.py:39
  136.4 5.8 %collective-permute-start.43 = (f32[32,128]{1,0:T(8,128)S(1)}, f32[32,128]{1,0:T(8,128)S(1)}, u32[]{:S(2)}, u32[]{:S(2)}) collective-permute-start(f32[32,128]{1,0:T(8,128)S(1)} %shard_map.124.rim), channel_id=1, source_target_pairs={{0,3},{1,0},{2,1},{3,2},{4,7},{5,4},{6,5},{7,6},{8,11},{9,8},{10,9... | collective-permute-start | bytes 49160 | tf_op jit(solution)/shard_map/ppermute | solution.py:40
  (24 other events, 130.5 us)

commit v3 on v2

--- a/solution.py
+++ b/solution.py
@@ -17,29 +17,29 @@
 
 
 def routes(count):
-    lines = count // LINE
-    cross, down, up = [], [], []
+    last = count - 1
+    cross = []
+    for i in range(3, last, 2):
+        if i + 1 < last - 1:
+            cross += [(i, i + 1), (i + 1, i)]
+    cross += [(0, 1), (1, 2), (2, 0), (last - 2, last - 1), (last - 1, last), (last, last - 2)]
+    pair = [(i, i ^ 1) for i in range(count)]
+    mend = []
     for i in range(count):
-        base = i - i % LINE
-        up.append((i, base + (i + 1) % LINE))
-        down.append((i, base + (i - 1) % LINE))
-    for k in range(lines - 1):
-        a, b = LINE * k + LINE - 1, LINE * k + LINE
-        cross += [(a, b), (b, a)]
-    for k in range(1, lines - 1):
-        a, b = LINE * k + 1, LINE * k + 2
-        cross += [(a, b), (b, a)]
-    last = count - 1
-    cross += [(0, 1), (1, 2), (2, 0), (last - 2, last - 1), (last - 1, last), (last, last - 2)]
-    return cross, down, up
+        spot = i % LINE
+        if spot in (0, LINE - 1):
+            mend.append((i, i ^ LINE))
+        else:
+            low = (i // LINE) % LINE in (0, LINE - 1)
+            back = spot == 2
+            mend.append((i, i - 1 if low and back else i + 1 if not low and not back else i ^ LINE))
+    for way in (mend, pair, cross):
+        assert sorted(t for _, t in way) == sorted(f for f, _ in way) == list(range(count))
+    return mend, pair, cross
 
 
 def exchange(field, ways):
-    cross, down, up = ways
-    cross = lax.ppermute(field, AXES, cross)
-    down = lax.ppermute(field, AXES, down)
-    up = lax.ppermute(field, AXES, up)
-    return cross, down, up
+    return [lax.ppermute(field, AXES, way) for way in ways]
 
 
 def iota(shape, dim):
@@ -70,23 +70,6 @@
     )
 
 
-def fold_lanes(parts):
-    lanes = iota(parts[0].shape, 1)
-    shift, half = 64, 4
-    while half:
-        low = (lanes & shift) == 0
-        if shift == 64:
-            parts = [
-                jnp.where(low, a, b) + pltpu.roll(jnp.where(low, b, a), 64, 1)
-                for a, b in zip(parts[:half], parts[half:])
-            ]
-        else:
-            parts = [fold_pair(a, b, low, shift, 1) for a, b in zip(parts[:half], parts[half:])]
-        shift //= 2
-        half //= 2
-    return parts[0]
-
-
 def take_lanes(field, places):
     return jnp.take_along_axis(field, places, axis=1, mode="promise_in_bounds")
 
@@ -95,11 +78,12 @@
     return lax.axis_index(AXES), lax.axis_size(AXES)
 
 
-def neighbours(cross, down, up):
+def neighbours(mend, pair, cross):
     device, count = place_on_line()
-    spot = lax.rem(device, LINE)
-    left = jnp.where(spot == 0, cross, up)
-    right = jnp.where(spot == LINE - 1, cross, down)
+    even = lax.rem(device, 2) == 0
+    ends = (device == 1) | (device == count - 3)
+    left = jnp.where(even, cross, pair)
+    right = jnp.where(even, pair, jnp.where(ends, mend, cross))
     left = jnp.where(device == 0, 0.0, left)
     right = jnp.where(device == count - 1, 0.0, right)
     return left, right
@@ -130,16 +114,18 @@
     return [pack_halves(rows[k], rows[k + 4], outer) for k in range(4)]
 
 
-def apply_slots(blocks, fields, acc):
-    step = 16
+def apply_slots(blocks, fields, acc, lead=None):
+    step = 16 if blocks.dtype == jnp.bfloat16 else 32
+    skip = 0 if lead is None else 1
 
     def body(ab, carry):
         rows = pl.ds(pl.multiple_of(ab * step, step), step)
-        total = jnp.zeros((step, 8, LANES), F32)
+        total = jnp.zeros((step, 8, LANES), F32) if lead is None else lead[rows]
         for slot in range(fields.shape[0]):
-            for g in range(4):
-                part = slice(8 * g, 8 * g + 8)
-                total = total + blocks[slot, rows, part, :] * fields[slot, part, :][None]
+            for g in range(2):
+                piece = blocks[slot + skip, rows, 16 * g : 16 * g + 16, :].astype(F32)
+                total = total + piece[:, :8] * fields[slot, 16 * g : 16 * g + 8, :][None]
+                total = total + piece[:, 8:] * fields[slot, 16 * g + 8 : 16 * g + 16, :][None]
         acc[rows] = total
         return carry
 
@@ -150,9 +136,11 @@
     out = []
     for k in range(8):
         rows = slice(8 * k, 8 * k + 8)
-        total = blocks[rows, 0:8, :] * parts[0][None]
-        for g in range(1, 4):
-            total = total + blocks[rows, 8 * g : 8 * g + 8, :] * parts[g][None]
+        total = jnp.zeros((8, 8, LANES), F32)
+        for g in range(2):
+            piece = blocks[rows, 16 * g : 16 * g + 16, :].astype(F32)
+            total = total + piece[:, :8] * parts[2 * g][None]
+            total = total + piece[:, 8:] * parts[2 * g + 1][None]
         out.append(fold_sublanes([total[i] for i in range(8)]))
     return [pack_halves(out[k], out[k + 4], outer) for k in range(4)]
 
@@ -162,61 +150,100 @@
     return outer if is_rim else jnp.logical_not(outer)
 
 
-def gather_fields(columns, own, rim, core, outside, fields):
-    is_rim = outside is not None
+def lanes_of(columns, slots, is_rim):
     home = home_lanes(is_rim)
-    slots = fields.shape[0] - 1
     places = [jnp.broadcast_to(columns[s : s + 1, :], (8, LANES)) for s in range(slots)]
-    lane = [jnp.where(home, p, p + 64) & (LANES - 1) for p in places]
+    return places, [jnp.where(home, p, p + 64) & (LANES - 1) for p in places]
+
+
+def gather_inside(columns, slots, is_rim, rim, core, fields, first):
+    places, lane = lanes_of(columns, slots, is_rim)
     inner = [((p + 32) & 64) != 0 for p in places]
-    inside = [(p >= 0) & (p < LANES) for p in places]
     for g in range(4):
         part = slice(8 * g, 8 * g + 8)
-        fields[0, part, :] = own[part, :]
-        if outside is not None:
-            left, right = neighbours(*[o[part, :] for o in outside])
-            beyond = jnp.where((iota((8, LANES), 1) & 32) == 0, right, left)
         for s in range(slots):
             edge = take_lanes(rim[part, :], lane[s])
-            if outside is not None:
-                edge = jnp.where(inside[s], edge, take_lanes(beyond, lane[s]))
             middle = take_lanes(core[part, :], lane[s])
-            fields[s + 1, part, :] = jnp.where(inner[s], middle, edge)
-
-
-def part_residual(columns, blocks, rhs, own, rim, core, outside, fields, acc):
-    gather_fields(columns, own, rim, core, outside, fields)
-    apply_slots(blocks, fields, acc)
-    total = fold_all(acc, home_lanes(outside is not None))
+            fields[first + s, part, :] = jnp.where(inner[s], middle, edge)
+
+
+def gather_outside(columns, sent, inside, fields):
+    slots = fields.shape[0]
+    places, lane = lanes_of(columns, slots, True)
+    own = [(p >= 0) & (p < LANES) for p in places]
+    for g in range(4):
+        part = slice(8 * g, 8 * g + 8)
+        left, right = neighbours(*[o[part, :] for o in sent])
+        beyond = jnp.where((iota((8, LANES), 1) & 32) == 0, right, left)
+        for s in range(slots):
+            fields[s, part, :] = jnp.where(own[s], inside[s, part, :], take_lanes(beyond, lane[s]))
+
+
+def rim_residual(columns, blocks, rhs, inside, lead, sent, fields, acc):
+    gather_outside(columns, sent, inside, fields)
+    apply_slots(blocks, fields, acc, lead)
+    total = fold_all(acc, home_lanes(True))
     return [rhs[8 * g : 8 * g + 8, :] - total[g] for g in range(4)]
 
 
-def part_sweep(columns, blocks, inv, rhs, own, rim, core, outside, fields, acc):
-    res = part_residual(columns, blocks, rhs, own, rim, core, outside, fields, acc)
-    step = apply_one(inv, res, home_lanes(outside is not None))
-    return [own[8 * g : 8 * g + 8, :] + damping * step[g] for g in range(4)]
-
-
-def rim_kernel(columns, blocks, inv, rhs, rim, core, cross, down, up, out, fields, acc):
-    new = part_sweep(columns, blocks, inv, rhs, rim, rim, core, (cross, down, up), fields, acc)
+def rim_sweep(columns, blocks, inv, rhs, rim, inside, lead, sent, fields, acc):
+    res = rim_residual(columns, blocks, rhs, inside, lead, sent, fields, acc)
+    step = apply_one(inv, res, home_lanes(True))
+    return [rim[8 * g : 8 * g + 8, :] + damping * step[g] for g in range(4)]
+
+
+def rim_kernel(columns, blocks, inv, rhs, rim, inside, lead, mend, pair, cross, out, fields, acc):
+    sent = (mend, pair, cross)
+    new = rim_sweep(columns, blocks, inv, rhs, rim, inside, lead, sent, fields, acc)
     for g in range(4):
         out[8 * g : 8 * g + 8, :] = new[g]
 
 
-def core_kernel(columns, blocks, inv, rhs, rim, core, out, fields, acc):
-    new = part_sweep(columns, blocks, inv, rhs, core, rim, core, None, fields, acc)
+def core_residual(columns, blocks, rhs, rim, core, rim_columns, rim_blocks, inside, lead, fields, acc):
+    slots = inside.shape[0]
+    gather_inside(rim_columns, slots, True, rim, core, inside, 0)
+    for k in range(8):
+        rows = slice(8 * k, 8 * k + 8)
+        total = rim_blocks[0, rows, 0:8, :] * rim[0:8, :][None]
+        for g in range(1, 4):
+            part = slice(8 * g, 8 * g + 8)
+            total = total + rim_blocks[0, rows, part, :] * rim[part, :][None]
+        lead[rows] = total
+    fields[0] = core[...]
+    gather_inside(columns, slots, False, rim, core, fields, 1)
+    apply_slots(blocks, fields, acc)
+    total = fold_all(acc, home_lanes(False))
+    return [rhs[8 * g : 8 * g + 8, :] - total[g] for g in range(4)]
+
+
+def core_kernel(
+    columns, blocks, rhs, rim, core, rim_columns, rim_blocks, inv, out, inside, lead, fields, acc
+):
+    res = core_residual(
+        columns, blocks, rhs, rim, core, rim_columns, rim_blocks, inside, lead, fields, acc
+    )
+    step = apply_one(inv, res, home_lanes(False))
     for g in range(4):
-        out[8 * g : 8 * g + 8, :] = new[g]
-
-
-def core_residual_kernel(columns, blocks, rhs, rim, core, out, fields, acc):
-    res = part_residual(columns, blocks, rhs, core, rim, core, None, fields, acc)
+        part = slice(8 * g, 8 * g + 8)
+        out[part, :] = core[part, :] + damping * step[g]
+
+
+def core_residual_kernel(
+    columns, blocks, rhs, rim, core, rim_columns, rim_blocks, out, inside, lead, fields, acc
+):
+    res = core_residual(
+        columns, blocks, rhs, rim, core, rim_columns, rim_blocks, inside, lead, fields, acc
+    )
     for g in range(4):
         out[8 * g : 8 * g + 8, :] = res[g]
 
 
-def last_kernel(columns, blocks, inv, rhs, rim, core, cross, down, up, new_core, out, fields, acc, held, sem):
-    new = part_sweep(columns, blocks, inv, rhs, rim, rim, core, (cross, down, up), fields, acc)
+def last_kernel(
+    columns, blocks, inv, rhs, rim, inside, lead, mend, pair, cross, new_core,
+    out, fields, acc, held, sem,
+):
+    sent = (mend, pair, cross)
+    new = rim_sweep(columns, blocks, inv, rhs, rim, inside, lead, sent, fields, acc)
     for g in range(4):
         part = slice(8 * g, 8 * g + 8)
         top, bottom = join_field(new[g], new_core[part, :])
@@ -257,10 +284,11 @@
     for k in range(8):
         copies[k + 1].wait()
         rows = slice(8 * k, 8 * k + 8)
-        wide = held[rows].astype(F32)
-        both = split_field(wide[:, :32], wide[:, 32:])
-        for blocks, piece, parts, kept in zip((rim_inv, core_inv), both, own, sums):
-            blocks[rows] = piece
+        both = split_field(held[rows, :32, :], held[rows, 32:, :])
+        core_inv[rows] = both[1]
+        both = [piece.astype(F32) for piece in both]
+        rim_inv[rows] = both[0]
+        for piece, parts, kept in zip(both, own, sums):
             total = piece[:, 0:8] * parts[0][None]
             for g in range(1, 4):
                 total = total + piece[:, 8 * g : 8 * g + 8] * parts[g][None]
@@ -290,21 +318,25 @@
 
 def widen_kernel(diag, off, rim_out, core_out, held, sems):
     slots = off.shape[0] + 1
-    copies = [pltpu.make_async_copy(diag, held.at[0], sems.at[0])]
-    for s in range(1, slots):
-        copies.append(pltpu.make_async_copy(off.at[s - 1], held.at[s], sems.at[s]))
-    for copy in copies:
+    parts, ahead = 4, 6
+    each = diag.shape[0] // parts
+    copies = []
+    for s in range(slots):
+        src = diag if s == 0 else off.at[s - 1]
+        for k in range(parts):
+            rows = pl.ds(each * k, each)
+            copies.append(pltpu.make_async_copy(src.at[rows], held.at[s, rows], sems.at[s, k]))
+    for copy in copies[:ahead]:
         copy.start()
-    for s in range(slots):
-        copies[s].wait()
-
-        def body(ab, carry):
-            rows = pl.ds(pl.multiple_of(ab * 8, 8), 8)
-            wide = held[s, rows].astype(F32)
-            rim_out[s, rows], core_out[s, rows] = split_field(wide[:, :32], wide[:, 32:])
-            return carry
-
-        lax.fori_loop(0, 8, body, 0)
+    for i, copy in enumerate(copies):
+        copy.wait()
+        if i + ahead < len(copies):
+            copies[i + ahead].start()
+        s, k = divmod(i, parts)
+        rows = pl.ds(each * k, each)
+        rim, core = split_field(held[s, rows, :32, :], held[s, rows, 32:, :])
+        rim_out[s, rows] = rim.astype(F32)
+        core_out[s, rows] = core
 
 
 def turn(block):
@@ -359,15 +391,18 @@
         acc = off[rows, 0:8, :] * fields[0][None]
         for g in range(1, 8):
             acc = acc + off[rows, 8 * g : 8 * g + 8, :] * fields[g][None]
-        parts.append(fold_sublanes([acc[i] for i in range(8)]))
-    return fold_lanes(parts)
+        total = fold_sublanes([acc[i] for i in range(8)])
+        for shift in (64, 32, 16):
+            total = total + pltpu.roll(total, shift, 1)
+        parts.append(total)
+    return parts
 
 
 def restrict_kernel(
-    columns, blocks, rhs, rim, core, core_res, cross, down, up, core_columns, cinv,
+    columns, blocks, rhs, core_res, inside, lead, mend, pair, cross, core_columns, cinv,
     coarse_rhs, out, fields, acc,
 ):
-    res = part_residual(columns, blocks, rhs, rim, rim, core, (cross, down, up), fields, acc)
+    res = rim_residual(columns, blocks, rhs, inside, lead, (mend, pair, cross), fields, acc)
     inner = core_res[...]
     edge = jnp.concatenate(res, axis=0)
     r = jnp.concatenate(join_field(edge, inner), axis=0)
@@ -376,7 +411,7 @@
     mid = rest.astype(jnp.bfloat16)
     last = (rest - mid.astype(F32)).astype(jnp.bfloat16)
     parts = jnp.concatenate([hi, mid, last], axis=0)
-    slots = fields.shape[0] - 1
+    slots = fields.shape[0]
     agg = jnp.where(
         outer_lanes((1, LANES)), columns[slots : slots + 1, :], core_columns[slots : slots + 1, :]
     )
@@ -388,8 +423,8 @@
     out[...] = damping * small_apply(cinv, [full[8 * g : 8 * g + 8] for g in range(8)])
 
 
-def coarse_step(places, cdiag, coff, cinv, coarse_rhs, u, cross, down, up):
-    left, right = neighbours(cross[...], down[...], up[...])
+def coarse_step(places, cdiag, coff, cinv, coarse_rhs, u, mend, pair, cross):
+    left, right = neighbours(mend[...], pair[...], cross[...])
     places = places[...]
     inner = places & 15
     mine = u[...]
@@ -403,19 +438,20 @@
                 jnp.where(places < 16, take_lanes(mine, lane), take_lanes(right, lane)),
             )
         )
-    total = small_apply(cdiag, spread_rows(mine)) + coarse_off_apply(coff, fields)
-    return mine + damping * small_apply(cinv, spread_rows(coarse_rhs[...] - total))
-
-
-def coarse_kernel(places, cdiag, coff, cinv, coarse_rhs, u, cross, down, up, out):
-    out[...] = coarse_step(places, cdiag, coff, cinv, coarse_rhs, u, cross, down, up)
+    base = spread_rows(coarse_rhs[...] - small_apply(cdiag, spread_rows(mine)))
+    total = coarse_off_apply(coff, fields)
+    return mine + damping * small_apply(cinv, [a - b for a, b in zip(base, total)])
+
+
+def coarse_kernel(places, cdiag, coff, cinv, coarse_rhs, u, mend, pair, cross, out):
+    out[...] = coarse_step(places, cdiag, coff, cinv, coarse_rhs, u, mend, pair, cross)
 
 
 def prolong_kernel(
-    places, cdiag, coff, cinv, coarse_rhs, u, cross, down, up, rim_columns, core_columns, rim, core,
+    places, cdiag, coff, cinv, coarse_rhs, u, mend, pair, cross, rim_columns, core_columns, rim, core,
     rim_out, core_out,
 ):
-    last = coarse_step(places, cdiag, coff, cinv, coarse_rhs, u, cross, down, up)
+    last = coarse_step(places, cdiag, coff, cinv, coarse_rhs, u, mend, pair, cross)
     row = 6
     tables = ((rim_columns, rim, rim_out, True), (core_columns, core, core_out, False))
     for table, old, out, is_rim in tables:
@@ -476,7 +512,7 @@
 
     rim, core, rim_inv, core_inv, rim_rhs, core_rhs, rim_cols, core_cols, near = call(
         first_kernel,
-        [half, half, blocks[1:], blocks[1:], half, half, table, table, table],
+        [half, half, blocks[1:], (blocks[1:], bf16), half, half, table, table, table],
         [fine_inv, right_side, fine_columns, aggregate.reshape(1, rows), coarse_columns],
         [
             pltpu.VMEM(fine_inv.shape, bf16),
@@ -488,12 +524,11 @@
         ],
         far=True,
     )
-    sent = exchange(rim, ways)
     rim_blocks, core_blocks = call(
         widen_kernel,
-        [blocks, blocks],
+        [blocks, (blocks, bf16)],
         [fine_diag, fine_off],
-        [pltpu.VMEM((slots + 1, size, size, rows), bf16), sem((slots + 1,))],
+        [pltpu.VMEM((slots + 1, size, size, rows), bf16), sem((slots + 1, 4))],
         far=True,
         limit=12,
     )
@@ -502,26 +537,34 @@
     others = jnp.transpose(coarse_off, (0, 1, 3, 2))
     coff = call(coarse_off_kernel, [(size, size, LANES)], [others])
 
+    rim_work = [pltpu.VMEM((slots,) + half, F32), work[1]]
+    ready = [half, (slots,) + half, (size, 8, LANES)]
+
+    def core_args(rim, core):
+        return [core_cols, core_blocks, core_rhs, rim, core, rim_cols, rim_blocks]
+
     def sweep_core(rim, core):
-        return call(core_kernel, [half], [core_cols, core_blocks, core_inv, core_rhs, rim, core], work)
-
-    def sweep_rim(rim, core, sent):
-        args = [rim_cols, rim_blocks, rim_inv, rim_rhs, rim, core, *sent]
-        return call(rim_kernel, [half], args, work)
+        return call(core_kernel, ready, core_args(rim, core) + [core_inv], work)
+
+    def rim_args(rim, inside, lead, sent):
+        return [rim_cols, rim_blocks, rim_inv, rim_rhs, rim, inside, lead, *sent]
+
+    def sweep(rim, core):
+        sent = exchange(rim, ways)
+        core, inside, lead = sweep_core(rim, core)
+        return call(rim_kernel, [half], rim_args(rim, inside, lead, sent), rim_work), core
 
     for cycle in range(CYCLES):
         for step in range(SWEEPS):
             if cycle or step:
-                rim, core = sweep_rim(rim, core, sent), sweep_core(rim, core)
-                sent = exchange(rim, ways)
-        core_res = call(
-            core_residual_kernel, [half], [core_cols, core_blocks, core_rhs, rim, core], work
-        )
+                rim, core = sweep(rim, core)
+        sent = exchange(rim, ways)
+        core_res, inside, lead = call(core_residual_kernel, ready, core_args(rim, core), work)
         crhs, u = call(
             restrict_kernel,
             [packed, packed],
-            [rim_cols, rim_blocks, rim_rhs, rim, core, core_res, *sent, core_cols, cinv],
-            work,
+            [rim_cols, rim_blocks, rim_rhs, core_res, inside, lead, *sent, core_cols, cinv],
+            rim_work,
         )
         for step in range(1, CSWEEPS):
             base = [near, cdiag, coff, cinv, crhs, u, *exchange(u, ways)]
@@ -529,19 +572,17 @@
                 u = call(coarse_kernel, [packed], base)
             else:
                 rim, core = call(prolong_kernel, [half, half], base + [rim_cols, core_cols, rim, core])
-        sent = exchange(rim, ways)
-        for step in range(SWEEPS):
-            if cycle == CYCLES - 1 and step == SWEEPS - 1:
-                break
-            rim, core = sweep_rim(rim, core, sent), sweep_core(rim, core)
-            sent = exchange(rim, ways)
-    args = [rim_cols, rim_blocks, rim_inv, rim_rhs, rim, core, *sent, sweep_core(rim, core)]
+        for step in range(SWEEPS - (cycle == CYCLES - 1)):
+            rim, core = sweep(rim, core)
+    sent = exchange(rim, ways)
+    core, inside, lead = sweep_core(rim, core)
+    args = rim_args(rim, inside, lead, sent) + [core]
     return pl.pallas_call(
         last_kernel,
         out_shape=pltpu.HBM(full, F32),
         in_specs=[VM] * len(args),
         out_specs=FAR,
-        scratch_shapes=work + [pltpu.VMEM(full, F32), sem(())],
+        scratch_shapes=rim_work + [pltpu.VMEM(full, F32), sem(())],
         compiler_params=pltpu.CompilerParams(vmem_limit_bytes=4 * 1024 * 1024),
     )(*[in_vmem(a) for a in args])
 

time: 146 us -> 132 us (0.904)
  the two profiles are of different devices: /device:TPU:25 before, /device:TPU:6 now
where the time goes in v3:
time: 132 us
  waiting for transfers between devices  68.6 us (52%)
  Pallas kernels  33.3 us (25%)
  starting transfers between devices  29.5 us (22%)
    ppermute x45, waiting for transfers between devices, exchange(): return [lax.ppermute(field, AXES, way) for way in ways]  68.6 us
    pallas_call x27, Pallas kernels, call(): pl.pallas_call(kernel, out_shape=shapes if len(shapes) > 1 else shapes[0]...  31.7 us
    ppermute x45, starting transfers between devices, exchange(): return [lax.ppermute(field, AXES, way) for way in ways]  29.5 us
  transfers between devices with their start and end apart: 45, of which 15 were waited for; matrix products, arithmetic and copies ran while one was open for 0% of the time, Pallas kernels for 15%

profile of v3, /device:TPU:6, one launch (start us, length us, event | category | flops | bytes accessed | tf_op | source)
XLA Modules:
  0.0 131.7 jit_solution(14390083980778515768)
XLA Ops:
  0.0 2.2 %shard_map.100 = (f32[32,128]{1,0:T(8,128)S(1)}, f32[32,128]{1,0:T(8,128)S(1)}, f32[64,32,128]{2,1,0:T(8,128)S(1)}, bf16[64,32,128]{2,1,0:T(8,128)(2,1)S(1)}, f3...) custom-call(bf16[64,64,128]{2,1,0:T(8,128)(2,1)} %inv.1, ...), custom_call_target="tpu_custom_call" | custom-call | tf_op jit(solution)/shard_map/pallas_call | solution.py:476
  2.2 6.3 %collective-permute-start.2 = (f32[32,128]{1,0:T(8,128)S(1)}, f32[32,128]{1,0:T(8,128)S(1)}, u32[]{:S(2)}, u32[]{:S(2)}) collective-permute-start(f32[32,128]{1,0:T(8,128)S(1)} %get-tuple-element.63.rim), channel_id=1, source_target_pairs={{3,4},{4,3},{5,6},{6,5},{7,8},{8,7},{9,10},{10,9},{11,12},{12,11},... | collective-permute-start | bytes 49160 | tf_op jit(solution)/shard_map/ppermute | solution.py:42
  8.5 5.9 %shard_map.101 = (f32[7,64,32,128]{3,2,1,0:T(8,128)S(1)}, bf16[7,64,32,128]{3,2,1,0:T(8,128)(2,1)S(1)}) custom-call(bf16[64,64,128]{2,1,0:T(8,128)(2,1)} %diag.1, bf16[6,64,64,128]{3,2,1,0:T(8,128)(2,1)} %off.1), custom_call_target="tpu_custom_call" | custom-call | tf_op jit(solution)/shard_map/pallas_call | solution.py:476
  17.3 3.4 %collective-permute-start.4 = (f32[32,128]{1,0:T(8,128)S(1)}, f32[32,128]{1,0:T(8,128)S(1)}, u32[]{:S(2)}, u32[]{:S(2)}) collective-permute-start(f32[32,128]{1,0:T(8,128)S(1)} %shard_map.105.rim), channel_id=1, source_target_pairs={{0,1},{1,0},{2,3},{3,2},{4,5},{5,4},{6,7},{7,6},{8,9},{9,8},{10,11... | collective-permute-start | bytes 49160 | tf_op jit(solution)/shard_map/ppermute | solution.py:42
  22.1 1.9 %collective-permute-done.5.cross = f32[32,128]{1,0:T(8,128)S(1)} collective-permute-done((f32[32,128]{1,0:T(8,128)S(1)}, f32[32,128]{1,0:T(8,128)S(1)}, u32[]{:S(2)}, u32[]{:S(2)}) %collective-permute-start.5) | collective-permute-done | bytes 16416 | tf_op jit(solution)/shard_map/ppermute | solution.py:42
  28.9 3.8 %collective-permute-done.8.cross = f32[8,128]{1,0:T(8,128)S(1)} collective-permute-done((f32[8,128]{1,0:T(8,128)S(1)}, f32[8,128]{1,0:T(8,128)S(1)}, u32[]{:S(2)}, u32[]{:S(2)}) %collective-permute-start.8) | collective-permute-done | bytes 4128 | tf_op jit(solution)/shard_map/ppermute | solution.py:42
  34.5 6.1 %collective-permute-done.11.cross = f32[8,128]{1,0:T(8,128)S(1)} collective-permute-done((f32[8,128]{1,0:T(8,128)S(1)}, f32[8,128]{1,0:T(8,128)S(1)}, u32[]{:S(2)}, u32[]{:S(2)}) %collective-permute-start.11) | collective-permute-done | bytes 4128 | tf_op jit(solution)/shard_map/ppermute | solution.py:42
  42.3 6.1 %collective-permute-done.14.cross = f32[8,128]{1,0:T(8,128)S(1)} collective-permute-done((f32[8,128]{1,0:T(8,128)S(1)}, f32[8,128]{1,0:T(8,128)S(1)}, u32[]{:S(2)}, u32[]{:S(2)}) %collective-permute-start.14) | collective-permute-done | bytes 4128 | tf_op jit(solution)/shard_map/ppermute | solution.py:42
  51.6 4.8 %collective-permute-done.17.cross = f32[32,128]{1,0:T(8,128)S(1)} collective-permute-done((f32[32,128]{1,0:T(8,128)S(1)}, f32[32,128]{1,0:T(8,128)S(1)}, u32[]{:S(2)}, u32[]{:S(2)}) %collective-permute-start.17) | collective-permute-done | bytes 16416 | tf_op jit(solution)/shard_map/ppermute | solution.py:42
  59.9 4.8 %collective-permute-done.20.cross = f32[32,128]{1,0:T(8,128)S(1)} collective-permute-done((f32[32,128]{1,0:T(8,128)S(1)}, f32[32,128]{1,0:T(8,128)S(1)}, u32[]{:S(2)}, u32[]{:S(2)}) %collective-permute-start.20) | collective-permute-done | bytes 16416 | tf_op jit(solution)/shard_map/ppermute | solution.py:42
  68.2 4.8 %collective-permute-done.23.cross = f32[32,128]{1,0:T(8,128)S(1)} collective-permute-done((f32[32,128]{1,0:T(8,128)S(1)}, f32[32,128]{1,0:T(8,128)S(1)}, u32[]{:S(2)}, u32[]{:S(2)}) %collective-permute-start.23) | collective-permute-done | bytes 16416 | tf_op jit(solution)/shard_map/ppermute | solution.py:42
  76.6 4.8 %collective-permute-done.26.cross = f32[32,128]{1,0:T(8,128)S(1)} collective-permute-done((f32[32,128]{1,0:T(8,128)S(1)}, f32[32,128]{1,0:T(8,128)S(1)}, u32[]{:S(2)}, u32[]{:S(2)}) %collective-permute-start.26) | collective-permute-done | bytes 16416 | tf_op jit(solution)/shard_map/ppermute | solution.py:42
  82.3 1.5 %collective-permute-start.29 = (f32[32,128]{1,0:T(8,128)S(1)}, f32[32,128]{1,0:T(8,128)S(1)}, u32[]{:S(2)}, u32[]{:S(2)}) collective-permute-start(f32[32,128]{1,0:T(8,128)S(1)} %shard_map.118.rim), channel_id=1, source_target_pairs={{3,4},{4,3},{5,6},{6,5},{7,8},{8,7},{9,10},{10,9},{11,12},{12,11},... | collective-permute-start | bytes 49160 | tf_op jit(solution)/shard_map/ppermute | solution.py:42
  85.0 4.7 %collective-permute-done.29.cross = f32[32,128]{1,0:T(8,128)S(1)} collective-permute-done((f32[32,128]{1,0:T(8,128)S(1)}, f32[32,128]{1,0:T(8,128)S(1)}, u32[]{:S(2)}, u32[]{:S(2)}) %collective-permute-start.29) | collective-permute-done | bytes 16416 | tf_op jit(solution)/shard_map/ppermute | solution.py:42
  90.6 1.6 %collective-permute-start.32 = (f32[8,128]{1,0:T(8,128)S(1)}, f32[8,128]{1,0:T(8,128)S(1)}, u32[]{:S(2)}, u32[]{:S(2)}) collective-permute-start(f32[8,128]{1,0:T(8,128)S(1)} %get-tuple-element.92.u), channel_id=1, source_target_pairs={{3,4},{4,3},{5,6},{6,5},{7,8},{8,7},{9,10},{10,9},{11,12},{12,11},... | collective-permute-start | bytes 12296 | tf_op jit(solution)/shard_map/ppermute | solution.py:42
  92.2 5.8 %collective-permute-done.32.cross = f32[8,128]{1,0:T(8,128)S(1)} collective-permute-done((f32[8,128]{1,0:T(8,128)S(1)}, f32[8,128]{1,0:T(8,128)S(1)}, u32[]{:S(2)}, u32[]{:S(2)}) %collective-permute-start.32) | collective-permute-done | bytes 4128 | tf_op jit(solution)/shard_map/ppermute | solution.py:42
  98.5 1.6 %collective-permute-start.35 = (f32[8,128]{1,0:T(8,128)S(1)}, f32[8,128]{1,0:T(8,128)S(1)}, u32[]{:S(2)}, u32[]{:S(2)}) collective-permute-start(f32[8,128]{1,0:T(8,128)S(1)} %shard_map.121.u), channel_id=1, source_target_pairs={{3,4},{4,3},{5,6},{6,5},{7,8},{8,7},{9,10},{10,9},{11,12},{12,11},... | collective-permute-start | bytes 12296 | tf_op jit(solution)/shard_map/ppermute | solution.py:42
  100.0 5.8 %collective-permute-done.35.cross = f32[8,128]{1,0:T(8,128)S(1)} collective-permute-done((f32[8,128]{1,0:T(8,128)S(1)}, f32[8,128]{1,0:T(8,128)S(1)}, u32[]{:S(2)}, u32[]{:S(2)}) %collective-permute-start.35) | collective-permute-done | bytes 4128 | tf_op jit(solution)/shard_map/ppermute | solution.py:42
  106.3 1.6 %collective-permute-start.38 = (f32[8,128]{1,0:T(8,128)S(1)}, f32[8,128]{1,0:T(8,128)S(1)}, u32[]{:S(2)}, u32[]{:S(2)}) collective-permute-start(f32[8,128]{1,0:T(8,128)S(1)} %shard_map.122.u), channel_id=1, source_target_pairs={{3,4},{4,3},{5,6},{6,5},{7,8},{8,7},{9,10},{10,9},{11,12},{12,11},... | collective-permute-start | bytes 12296 | tf_op jit(solution)/shard_map/ppermute | solution.py:42
  107.9 5.8 %collective-permute-done.38.cross = f32[8,128]{1,0:T(8,128)S(1)} collective-permute-done((f32[8,128]{1,0:T(8,128)S(1)}, f32[8,128]{1,0:T(8,128)S(1)}, u32[]{:S(2)}, u32[]{:S(2)}) %collective-permute-start.38) | collective-permute-done | bytes 4128 | tf_op jit(solution)/shard_map/ppermute | solution.py:42
  117.1 4.5 %collective-permute-done.41.cross = f32[32,128]{1,0:T(8,128)S(1)} collective-permute-done((f32[32,128]{1,0:T(8,128)S(1)}, f32[32,128]{1,0:T(8,128)S(1)}, u32[]{:S(2)}, u32[]{:S(2)}) %collective-permute-start.41) | collective-permute-done | bytes 16416 | tf_op jit(solution)/shard_map/ppermute | solution.py:42
  122.5 1.5 %collective-permute-start.44 = (f32[32,128]{1,0:T(8,128)S(1)}, f32[32,128]{1,0:T(8,128)S(1)}, u32[]{:S(2)}, u32[]{:S(2)}) collective-permute-start(f32[32,128]{1,0:T(8,128)S(1)} %shard_map.125.rim), channel_id=1, source_target_pairs={{3,4},{4,3},{5,6},{6,5},{7,8},{8,7},{9,10},{10,9},{11,12},{12,11},... | collective-permute-start | bytes 49160 | tf_op jit(solution)/shard_map/ppermute | solution.py:42
  125.5 4.5 %collective-permute-done.44.cross = f32[32,128]{1,0:T(8,128)S(1)} collective-permute-done((f32[32,128]{1,0:T(8,128)S(1)}, f32[32,128]{1,0:T(8,128)S(1)}, u32[]{:S(2)}, u32[]{:S(2)}) %collective-permute-start.44) | collective-permute-done | bytes 16416 | tf_op jit(solution)/shard_map/ppermute | solution.py:42
  130.0 1.6 %shard_map.127 = f32[64,128]{1,0:T(8,128)} custom-call(s32[8,128]{1,0:T(8,128)S(1)} %get-tuple-element.53.rim_columns.columns, f32[7,64,32,128]{3,2,1,0:T(8,128)S(1)} %get-tuple-element.54.rim_blocks.blocks, f32[64,32,128]{2,1,0:T(8,128)S(1)} %get-tuple-element.55.inv, f32[32,128]{1,0:T(8,128)S(1)} %get-tuple-element.56.rhs, f32[32,128]{1,0:T(8,128)S(1)} %shard_map.125.rim, ...), custom_call_target="tpu_custom_call" | custom-call | tf_op jit(solution)/shard_map/pallas_call | solution.py:580
  (100 shorter events, 36.3 us)
Async XLA Ops:
  2.2 13.6 %collective-permute-start.2 = (f32[32,128]{1,0:T(8,128)S(1)}, f32[32,128]{1,0:T(8,128)S(1)}, u32[]{:S(2)}, u32[]{:S(2)}) collective-permute-start(f32[32,128]{1,0:T(8,128)S(1)} %get-tuple-element.63.rim), channel_id=1, source_target_pairs={{3,4},{4,3},{5,6},{6,5},{7,8},{8,7},{9,10},{10,9},{11,12},{12,11},... | collective-permute-start | bytes 49160 | tf_op jit(solution)/shard_map/ppermute | solution.py:42
  8.4 7.3 %collective-permute-start.1 = (f32[32,128]{1,0:T(8,128)S(1)}, f32[32,128]{1,0:T(8,128)S(1)}, u32[]{:S(2)}, u32[]{:S(2)}) collective-permute-start(f32[32,128]{1,0:T(8,128)S(1)} %get-tuple-element.63.rim), channel_id=1, source_target_pairs={{0,1},{1,0},{2,3},{3,2},{4,5},{5,4},{6,7},{7,6},{8,9},{9,8},{10,11... | collective-permute-start | bytes 49160 | tf_op jit(solution)/shard_map/ppermute | solution.py:42
  8.5 7.3 %collective-permute-start = (f32[32,128]{1,0:T(8,128)S(1)}, f32[32,128]{1,0:T(8,128)S(1)}, u32[]{:S(2)}, u32[]{:S(2)}) collective-permute-start(f32[32,128]{1,0:T(8,128)S(1)} %get-tuple-element.63.rim), channel_id=1, source_target_pairs={{0,4},{1,5},{2,1},{3,7},{4,0},{5,6},{6,2},{7,3},{8,12},{9,10},{10,... | collective-permute-start | bytes 49160 | tf_op jit(solution)/shard_map/ppermute | solution.py:42
  16.7 7.4 %collective-permute-start.5 = (f32[32,128]{1,0:T(8,128)S(1)}, f32[32,128]{1,0:T(8,128)S(1)}, u32[]{:S(2)}, u32[]{:S(2)}) collective-permute-start(f32[32,128]{1,0:T(8,128)S(1)} %shard_map.105.rim), channel_id=1, source_target_pairs={{3,4},{4,3},{5,6},{6,5},{7,8},{8,7},{9,10},{10,9},{11,12},{12,11},... | collective-permute-start | bytes 49160 | tf_op jit(solution)/shard_map/ppermute | solution.py:42
  17.3 6.7 %collective-permute-start.4 = (f32[32,128]{1,0:T(8,128)S(1)}, f32[32,128]{1,0:T(8,128)S(1)}, u32[]{:S(2)}, u32[]{:S(2)}) collective-permute-start(f32[32,128]{1,0:T(8,128)S(1)} %shard_map.105.rim), channel_id=1, source_target_pairs={{0,1},{1,0},{2,3},{3,2},{4,5},{5,4},{6,7},{7,6},{8,9},{9,8},{10,11... | collective-permute-start | bytes 49160 | tf_op jit(solution)/shard_map/ppermute | solution.py:42
  25.4 7.3 %collective-permute-start.8 = (f32[8,128]{1,0:T(8,128)S(1)}, f32[8,128]{1,0:T(8,128)S(1)}, u32[]{:S(2)}, u32[]{:S(2)}) collective-permute-start(f32[8,128]{1,0:T(8,128)S(1)} %get-tuple-element.73.u), channel_id=1, source_target_pairs={{3,4},{4,3},{5,6},{6,5},{7,8},{8,7},{9,10},{10,9},{11,12},{12,11},... | collective-permute-start | bytes 12296 | tf_op jit(solution)/shard_map/ppermute | solution.py:42
  26.3 6.5 %collective-permute-start.7 = (f32[8,128]{1,0:T(8,128)S(1)}, f32[8,128]{1,0:T(8,128)S(1)}, u32[]{:S(2)}, u32[]{:S(2)}) collective-permute-start(f32[8,128]{1,0:T(8,128)S(1)} %get-tuple-element.73.u), channel_id=1, source_target_pairs={{0,1},{1,0},{2,3},{3,2},{4,5},{5,4},{6,7},{7,6},{8,9},{9,8},{10,11... | collective-permute-start | bytes 12296 | tf_op jit(solution)/shard_map/ppermute | solution.py:42
  33.2 7.3 %collective-permute-start.11 = (f32[8,128]{1,0:T(8,128)S(1)}, f32[8,128]{1,0:T(8,128)S(1)}, u32[]{:S(2)}, u32[]{:S(2)}) collective-permute-start(f32[8,128]{1,0:T(8,128)S(1)} %shard_map.108.u), channel_id=1, source_target_pairs={{3,4},{4,3},{5,6},{6,5},{7,8},{8,7},{9,10},{10,9},{11,12},{12,11},... | collective-permute-start | bytes 12296 | tf_op jit(solution)/shard_map/ppermute | solution.py:42
  41.1 7.3 %collective-permute-start.14 = (f32[8,128]{1,0:T(8,128)S(1)}, f32[8,128]{1,0:T(8,128)S(1)}, u32[]{:S(2)}, u32[]{:S(2)}) collective-permute-start(f32[8,128]{1,0:T(8,128)S(1)} %shard_map.109.u), channel_id=1, source_target_pairs={{3,4},{4,3},{5,6},{6,5},{7,8},{8,7},{9,10},{10,9},{11,12},{12,11},... | collective-permute-start | bytes 12296 | tf_op jit(solution)/shard_map/ppermute | solution.py:42
  49.0 7.4 %collective-permute-start.17 = (f32[32,128]{1,0:T(8,128)S(1)}, f32[32,128]{1,0:T(8,128)S(1)}, u32[]{:S(2)}, u32[]{:S(2)}) collective-permute-start(f32[32,128]{1,0:T(8,128)S(1)} %get-tuple-element.74.rim), channel_id=1, source_target_pairs={{3,4},{4,3},{5,6},{6,5},{7,8},{8,7},{9,10},{10,9},{11,12},{12,11},... | collective-permute-start | bytes 49160 | tf_op jit(solution)/shard_map/ppermute | solution.py:42
  50.2 6.2 %collective-permute-start.16 = (f32[32,128]{1,0:T(8,128)S(1)}, f32[32,128]{1,0:T(8,128)S(1)}, u32[]{:S(2)}, u32[]{:S(2)}) collective-permute-start(f32[32,128]{1,0:T(8,128)S(1)} %get-tuple-element.74.rim), channel_id=1, source_target_pairs={{0,1},{1,0},{2,3},{3,2},{4,5},{5,4},{6,7},{7,6},{8,9},{9,8},{10,11... | collective-permute-start | bytes 49160 | tf_op jit(solution)/shard_map/ppermute | solution.py:42
  50.2 6.2 %collective-permute-start.15 = (f32[32,128]{1,0:T(8,128)S(1)}, f32[32,128]{1,0:T(8,128)S(1)}, u32[]{:S(2)}, u32[]{:S(2)}) collective-permute-start(f32[32,128]{1,0:T(8,128)S(1)} %get-tuple-element.74.rim), channel_id=1, source_target_pairs={{0,4},{1,5},{2,1},{3,7},{4,0},{5,6},{6,2},{7,3},{8,12},{9,10},{10,... | collective-permute-start | bytes 49160 | tf_op jit(solution)/shard_map/ppermute | solution.py:42
  57.3 7.4 %collective-permute-start.20 = (f32[32,128]{1,0:T(8,128)S(1)}, f32[32,128]{1,0:T(8,128)S(1)}, u32[]{:S(2)}, u32[]{:S(2)}) collective-permute-start(f32[32,128]{1,0:T(8,128)S(1)} %shard_map.112.rim), channel_id=1, source_target_pairs={{3,4},{4,3},{5,6},{6,5},{7,8},{8,7},{9,10},{10,9},{11,12},{12,11},... | collective-permute-start | bytes 49160 | tf_op jit(solution)/shard_map/ppermute | solution.py:42
  58.5 6.2 %collective-permute-start.19 = (f32[32,128]{1,0:T(8,128)S(1)}, f32[32,128]{1,0:T(8,128)S(1)}, u32[]{:S(2)}, u32[]{:S(2)}) collective-permute-start(f32[32,128]{1,0:T(8,128)S(1)} %shard_map.112.rim), channel_id=1, source_target_pairs={{0,1},{1,0},{2,3},{3,2},{4,5},{5,4},{6,7},{7,6},{8,9},{9,8},{10,11... | collective-permute-start | bytes 49160 | tf_op jit(solution)/shard_map/ppermute | solution.py:42
  58.5 6.2 %collective-permute-start.18 = (f32[32,128]{1,0:T(8,128)S(1)}, f32[32,128]{1,0:T(8,128)S(1)}, u32[]{:S(2)}, u32[]{:S(2)}) collective-permute-start(f32[32,128]{1,0:T(8,128)S(1)} %shard_map.112.rim), channel_id=1, source_target_pairs={{0,4},{1,5},{2,1},{3,7},{4,0},{5,6},{6,2},{7,3},{8,12},{9,10},{10,... | collective-permute-start | bytes 49160 | tf_op jit(solution)/shard_map/ppermute | solution.py:42
  65.6 7.4 %collective-permute-start.23 = (f32[32,128]{1,0:T(8,128)S(1)}, f32[32,128]{1,0:T(8,128)S(1)}, u32[]{:S(2)}, u32[]{:S(2)}) collective-permute-start(f32[32,128]{1,0:T(8,128)S(1)} %shard_map.114.rim), channel_id=1, source_target_pairs={{3,4},{4,3},{5,6},{6,5},{7,8},{8,7},{9,10},{10,9},{11,12},{12,11},... | collective-permute-start | bytes 49160 | tf_op jit(solution)/shard_map/ppermute | solution.py:42
  66.8 6.2 %collective-permute-start.22 = (f32[32,128]{1,0:T(8,128)S(1)}, f32[32,128]{1,0:T(8,128)S(1)}, u32[]{:S(2)}, u32[]{:S(2)}) collective-permute-start(f32[32,128]{1,0:T(8,128)S(1)} %shard_map.114.rim), channel_id=1, source_target_pairs={{0,1},{1,0},{2,3},{3,2},{4,5},{5,4},{6,7},{7,6},{8,9},{9,8},{10,11... | collective-permute-start | bytes 49160 | tf_op jit(solution)/shard_map/ppermute | solution.py:42
  73.9 7.4 %collective-permute-start.26 = (f32[32,128]{1,0:T(8,128)S(1)}, f32[32,128]{1,0:T(8,128)S(1)}, u32[]{:S(2)}, u32[]{:S(2)}) collective-permute-start(f32[32,128]{1,0:T(8,128)S(1)} %shard_map.116.rim), channel_id=1, source_target_pairs={{3,4},{4,3},{5,6},{6,5},{7,8},{8,7},{9,10},{10,9},{11,12},{12,11},... | collective-permute-start | bytes 49160 | tf_op jit(solution)/shard_map/ppermute | solution.py:42
  82.3 7.4 %collective-permute-start.29 = (f32[32,128]{1,0:T(8,128)S(1)}, f32[32,128]{1,0:T(8,128)S(1)}, u32[]{:S(2)}, u32[]{:S(2)}) collective-permute-start(f32[32,128]{1,0:T(8,128)S(1)} %shard_map.118.rim), channel_id=1, source_target_pairs={{3,4},{4,3},{5,6},{6,5},{7,8},{8,7},{9,10},{10,9},{11,12},{12,11},... | collective-permute-start | bytes 49160 | tf_op jit(solution)/shard_map/ppermute | solution.py:42
  90.6 7.3 %collective-permute-start.32 = (f32[8,128]{1,0:T(8,128)S(1)}, f32[8,128]{1,0:T(8,128)S(1)}, u32[]{:S(2)}, u32[]{:S(2)}) collective-permute-start(f32[8,128]{1,0:T(8,128)S(1)} %get-tuple-element.92.u), channel_id=1, source_target_pairs={{3,4},{4,3},{5,6},{6,5},{7,8},{8,7},{9,10},{10,9},{11,12},{12,11},... | collective-permute-start | bytes 12296 | tf_op jit(solution)/shard_map/ppermute | solution.py:42
  98.5 7.3 %collective-permute-start.35 = (f32[8,128]{1,0:T(8,128)S(1)}, f32[8,128]{1,0:T(8,128)S(1)}, u32[]{:S(2)}, u32[]{:S(2)}) collective-permute-start(f32[8,128]{1,0:T(8,128)S(1)} %shard_map.121.u), channel_id=1, source_target_pairs={{3,4},{4,3},{5,6},{6,5},{7,8},{8,7},{9,10},{10,9},{11,12},{12,11},... | collective-permute-start | bytes 12296 | tf_op jit(solution)/shard_map/ppermute | solution.py:42
  106.3 7.3 %collective-permute-start.38 = (f32[8,128]{1,0:T(8,128)S(1)}, f32[8,128]{1,0:T(8,128)S(1)}, u32[]{:S(2)}, u32[]{:S(2)}) collective-permute-start(f32[8,128]{1,0:T(8,128)S(1)} %shard_map.122.u), channel_id=1, source_target_pairs={{3,4},{4,3},{5,6},{6,5},{7,8},{8,7},{9,10},{10,9},{11,12},{12,11},... | collective-permute-start | bytes 12296 | tf_op jit(solution)/shard_map/ppermute | solution.py:42
  114.2 7.4 %collective-permute-start.41 = (f32[32,128]{1,0:T(8,128)S(1)}, f32[32,128]{1,0:T(8,128)S(1)}, u32[]{:S(2)}, u32[]{:S(2)}) collective-permute-start(f32[32,128]{1,0:T(8,128)S(1)} %get-tuple-element.93.rim), channel_id=1, source_target_pairs={{3,4},{4,3},{5,6},{6,5},{7,8},{8,7},{9,10},{10,9},{11,12},{12,11},... | collective-permute-start | bytes 49160 | tf_op jit(solution)/shard_map/ppermute | solution.py:42
  122.5 7.4 %collective-permute-start.44 = (f32[32,128]{1,0:T(8,128)S(1)}, f32[32,128]{1,0:T(8,128)S(1)}, u32[]{:S(2)}, u32[]{:S(2)}) collective-permute-start(f32[32,128]{1,0:T(8,128)S(1)} %shard_map.125.rim), channel_id=1, source_target_pairs={{3,4},{4,3},{5,6},{6,5},{7,8},{8,7},{9,10},{10,9},{11,12},{12,11},... | collective-permute-start | bytes 49160 | tf_op jit(solution)/shard_map/ppermute | solution.py:42
  (24 other events, 135.6 us)

commit v4 on v3

--- a/solution.py
+++ b/solution.py
@@ -199,9 +199,8 @@
         out[8 * g : 8 * g + 8, :] = new[g]
 
 
-def core_residual(columns, blocks, rhs, rim, core, rim_columns, rim_blocks, inside, lead, fields, acc):
-    slots = inside.shape[0]
-    gather_inside(rim_columns, slots, True, rim, core, inside, 0)
+def rim_lead(rim, core, rim_columns, rim_blocks, inside, lead):
+    gather_inside(rim_columns, inside.shape[0], True, rim, core, inside, 0)
     for k in range(8):
         rows = slice(8 * k, 8 * k + 8)
         total = rim_blocks[0, rows, 0:8, :] * rim[0:8, :][None]
@@ -209,19 +208,32 @@
             part = slice(8 * g, 8 * g + 8)
             total = total + rim_blocks[0, rows, part, :] * rim[part, :][None]
         lead[rows] = total
+
+
+def lead_kernel(rim, core, rim_columns, rim_blocks, inside, lead):
+    rim_lead(rim, core, rim_columns, rim_blocks, inside, lead)
+
+
+def core_residual(columns, blocks, rhs, rim, core, fields, acc):
     fields[0] = core[...]
-    gather_inside(columns, slots, False, rim, core, fields, 1)
+    gather_inside(columns, fields.shape[0] - 1, False, rim, core, fields, 1)
     apply_slots(blocks, fields, acc)
     total = fold_all(acc, home_lanes(False))
     return [rhs[8 * g : 8 * g + 8, :] - total[g] for g in range(4)]
 
 
+def core_alone_kernel(columns, blocks, rhs, rim, core, inv, out, fields, acc):
+    step = apply_one(inv, core_residual(columns, blocks, rhs, rim, core, fields, acc), home_lanes(False))
+    for g in range(4):
+        part = slice(8 * g, 8 * g + 8)
+        out[part, :] = core[part, :] + damping * step[g]
+
+
 def core_kernel(
     columns, blocks, rhs, rim, core, rim_columns, rim_blocks, inv, out, inside, lead, fields, acc
 ):
-    res = core_residual(
-        columns, blocks, rhs, rim, core, rim_columns, rim_blocks, inside, lead, fields, acc
-    )
+    rim_lead(rim, core, rim_columns, rim_blocks, inside, lead)
+    res = core_residual(columns, blocks, rhs, rim, core, fields, acc)
     step = apply_one(inv, res, home_lanes(False))
     for g in range(4):
         part = slice(8 * g, 8 * g + 8)
@@ -231,9 +243,8 @@
 def core_residual_kernel(
     columns, blocks, rhs, rim, core, rim_columns, rim_blocks, out, inside, lead, fields, acc
 ):
-    res = core_residual(
-        columns, blocks, rhs, rim, core, rim_columns, rim_blocks, inside, lead, fields, acc
-    )
+    rim_lead(rim, core, rim_columns, rim_blocks, inside, lead)
+    res = core_residual(columns, blocks, rhs, rim, core, fields, acc)
     for g in range(4):
         out[8 * g : 8 * g + 8, :] = res[g]
 
@@ -318,7 +329,7 @@
 
 def widen_kernel(diag, off, rim_out, core_out, held, sems):
     slots = off.shape[0] + 1
-    parts, ahead = 4, 6
+    parts, ahead = 4, 14
     each = diag.shape[0] // parts
     copies = []
     for s in range(slots):
@@ -556,8 +567,15 @@
 
     for cycle in range(CYCLES):
         for step in range(SWEEPS):
-            if cycle or step:
+            if cycle:
                 rim, core = sweep(rim, core)
+            elif step:
+                sent = exchange(rim, ways)
+                inside, lead = call(lead_kernel, ready[1:], [rim, core, rim_cols, rim_blocks])
+                args = [core_cols, core_blocks, core_rhs, rim, core, core_inv]
+                new_core = call(core_alone_kernel, [half], args, work)
+                rim = call(rim_kernel, [half], rim_args(rim, inside, lead, sent), rim_work)
+                core = new_core
         sent = exchange(rim, ways)
         core_res, inside, lead = call(core_residual_kernel, ready, core_args(rim, core), work)
         crhs, u = call(

time: 132 us -> 129 us (0.977)
  waiting for transfers between devices: 68.6 us -> 56.1 us
  starting transfers between devices: 29.5 us -> 40.7 us
    ppermute x45, waiting for transfers between devices: 68.6 us -> 56.1 us  [exchange(): return [lax.ppermute(field, AXES, way) for way in ways]]
    ppermute x45, starting transfers between devices: 29.5 us -> 40.7 us  [exchange(): return [lax.ppermute(field, AXES, way) for way in ways]]
    pallas_call x27 -> x28, Pallas kernels: 31.7 us -> 30.4 us  [call(): pl.pallas_call(kernel, out_shape=shapes if len(shapes) > 1 else shapes[0]...]
  transfers between devices with their start and end apart: 45 -> 45, of which waited for: 15 -> 15; matrix products, arithmetic and copies ran while one was open for 0% -> 0% of each run, Pallas kernels for 15% -> 14%
where the time goes in v4:
time: 129 us
  waiting for transfers between devices  56.1 us (43%)
  starting transfers between devices  40.7 us (32%)
  Pallas kernels  32 us (25%)
    ppermute x45, waiting for transfers between devices, exchange(): return [lax.ppermute(field, AXES, way) for way in ways]  56.1 us
    ppermute x45, starting transfers between devices, exchange(): return [lax.ppermute(field, AXES, way) for way in ways]  40.7 us
    pallas_call x28, Pallas kernels, call(): pl.pallas_call(kernel, out_shape=shapes if len(shapes) > 1 else shapes[0]...  30.4 us
  transfers between devices with their start and end apart: 45, of which 15 were waited for; matrix products, arithmetic and copies ran while one was open for 0% of the time, Pallas kernels for 14%

profile of v4, /device:TPU:6, one launch (start us, length us, event | category | flops | bytes accessed | tf_op | source)
XLA Modules:
  0.0 129.2 jit_solution(16775066165829955294)
XLA Ops:
  2.2 6.3 %collective-permute-start.2 = (f32[32,128]{1,0:T(8,128)S(1)}, f32[32,128]{1,0:T(8,128)S(1)}, u32[]{:S(2)}, u32[]{:S(2)}) collective-permute-start(f32[32,128]{1,0:T(8,128)S(1)} %get-tuple-element.62.rim), channel_id=1, source_target_pairs={{3,4},{4,3},{5,6},{6,5},{7,8},{8,7},{9,10},{10,9},{11,12},{12,11},... | collective-permute-start | bytes 49160 | tf_op jit(solution)/shard_map/ppermute | solution.py:42
  8.5 4.5 %shard_map.101 = (f32[7,64,32,128]{3,2,1,0:T(8,128)S(1)}, bf16[7,64,32,128]{3,2,1,0:T(8,128)(2,1)S(1)}) custom-call(bf16[64,64,128]{2,1,0:T(8,128)(2,1)} %diag.1, bf16[6,64,64,128]{3,2,1,0:T(8,128)(2,1)} %off.1), custom_call_target="tpu_custom_call" | custom-call | tf_op jit(solution)/shard_map/pallas_call | solution.py:487
  14.1 2.6 %collective-permute-start.5 = (f32[32,128]{1,0:T(8,128)S(1)}, f32[32,128]{1,0:T(8,128)S(1)}, u32[]{:S(2)}, u32[]{:S(2)}) collective-permute-start(f32[32,128]{1,0:T(8,128)S(1)} %shard_map.105.rim), channel_id=1, source_target_pairs={{3,4},{4,3},{5,6},{6,5},{7,8},{8,7},{9,10},{10,9},{11,12},{12,11},... | collective-permute-start | bytes 49160 | tf_op jit(solution)/shard_map/ppermute | solution.py:42
  22.9 2.3 %collective-permute-start.8 = (f32[8,128]{1,0:T(8,128)S(1)}, f32[8,128]{1,0:T(8,128)S(1)}, u32[]{:S(2)}, u32[]{:S(2)}) collective-permute-start(f32[8,128]{1,0:T(8,128)S(1)} %get-tuple-element.71.u), channel_id=1, source_target_pairs={{3,4},{4,3},{5,6},{6,5},{7,8},{8,7},{9,10},{10,9},{11,12},{12,11},... | collective-permute-start | bytes 12296 | tf_op jit(solution)/shard_map/ppermute | solution.py:42
  27.0 3.2 %collective-permute-done.8.cross = f32[8,128]{1,0:T(8,128)S(1)} collective-permute-done((f32[8,128]{1,0:T(8,128)S(1)}, f32[8,128]{1,0:T(8,128)S(1)}, u32[]{:S(2)}, u32[]{:S(2)}) %collective-permute-start.8) | collective-permute-done | bytes 4128 | tf_op jit(solution)/shard_map/ppermute | solution.py:42
  30.7 2.3 %collective-permute-start.11 = (f32[8,128]{1,0:T(8,128)S(1)}, f32[8,128]{1,0:T(8,128)S(1)}, u32[]{:S(2)}, u32[]{:S(2)}) collective-permute-start(f32[8,128]{1,0:T(8,128)S(1)} %shard_map.109.u), channel_id=1, source_target_pairs={{3,4},{4,3},{5,6},{6,5},{7,8},{8,7},{9,10},{10,9},{11,12},{12,11},... | collective-permute-start | bytes 12296 | tf_op jit(solution)/shard_map/ppermute | solution.py:42
  33.0 5.0 %collective-permute-done.11.cross = f32[8,128]{1,0:T(8,128)S(1)} collective-permute-done((f32[8,128]{1,0:T(8,128)S(1)}, f32[8,128]{1,0:T(8,128)S(1)}, u32[]{:S(2)}, u32[]{:S(2)}) %collective-permute-start.11) | collective-permute-done | bytes 4128 | tf_op jit(solution)/shard_map/ppermute | solution.py:42
  38.5 2.3 %collective-permute-start.14 = (f32[8,128]{1,0:T(8,128)S(1)}, f32[8,128]{1,0:T(8,128)S(1)}, u32[]{:S(2)}, u32[]{:S(2)}) collective-permute-start(f32[8,128]{1,0:T(8,128)S(1)} %shard_map.110.u), channel_id=1, source_target_pairs={{3,4},{4,3},{5,6},{6,5},{7,8},{8,7},{9,10},{10,9},{11,12},{12,11},... | collective-permute-start | bytes 12296 | tf_op jit(solution)/shard_map/ppermute | solution.py:42
  40.9 5.0 %collective-permute-done.14.cross = f32[8,128]{1,0:T(8,128)S(1)} collective-permute-done((f32[8,128]{1,0:T(8,128)S(1)}, f32[8,128]{1,0:T(8,128)S(1)}, u32[]{:S(2)}, u32[]{:S(2)}) %collective-permute-start.14) | collective-permute-done | bytes 4128 | tf_op jit(solution)/shard_map/ppermute | solution.py:42
  46.5 2.3 %collective-permute-start.17 = (f32[32,128]{1,0:T(8,128)S(1)}, f32[32,128]{1,0:T(8,128)S(1)}, u32[]{:S(2)}, u32[]{:S(2)}) collective-permute-start(f32[32,128]{1,0:T(8,128)S(1)} %get-tuple-element.72.rim), channel_id=1, source_target_pairs={{3,4},{4,3},{5,6},{6,5},{7,8},{8,7},{9,10},{10,9},{11,12},{12,11},... | collective-permute-start | bytes 49160 | tf_op jit(solution)/shard_map/ppermute | solution.py:42
  50.1 3.8 %collective-permute-done.17.cross = f32[32,128]{1,0:T(8,128)S(1)} collective-permute-done((f32[32,128]{1,0:T(8,128)S(1)}, f32[32,128]{1,0:T(8,128)S(1)}, u32[]{:S(2)}, u32[]{:S(2)}) %collective-permute-start.17) | collective-permute-done | bytes 16416 | tf_op jit(solution)/shard_map/ppermute | solution.py:42
  54.8 2.3 %collective-permute-start.20 = (f32[32,128]{1,0:T(8,128)S(1)}, f32[32,128]{1,0:T(8,128)S(1)}, u32[]{:S(2)}, u32[]{:S(2)}) collective-permute-start(f32[32,128]{1,0:T(8,128)S(1)} %shard_map.113.rim), channel_id=1, source_target_pairs={{3,4},{4,3},{5,6},{6,5},{7,8},{8,7},{9,10},{10,9},{11,12},{12,11},... | collective-permute-start | bytes 49160 | tf_op jit(solution)/shard_map/ppermute | solution.py:42
  58.4 3.8 %collective-permute-done.20.cross = f32[32,128]{1,0:T(8,128)S(1)} collective-permute-done((f32[32,128]{1,0:T(8,128)S(1)}, f32[32,128]{1,0:T(8,128)S(1)}, u32[]{:S(2)}, u32[]{:S(2)}) %collective-permute-start.20) | collective-permute-done | bytes 16416 | tf_op jit(solution)/shard_map/ppermute | solution.py:42
  66.8 3.8 %collective-permute-done.23.cross = f32[32,128]{1,0:T(8,128)S(1)} collective-permute-done((f32[32,128]{1,0:T(8,128)S(1)}, f32[32,128]{1,0:T(8,128)S(1)}, u32[]{:S(2)}, u32[]{:S(2)}) %collective-permute-start.23) | collective-permute-done | bytes 16416 | tf_op jit(solution)/shard_map/ppermute | solution.py:42
  75.1 3.8 %collective-permute-done.26.cross = f32[32,128]{1,0:T(8,128)S(1)} collective-permute-done((f32[32,128]{1,0:T(8,128)S(1)}, f32[32,128]{1,0:T(8,128)S(1)}, u32[]{:S(2)}, u32[]{:S(2)}) %collective-permute-start.26) | collective-permute-done | bytes 16416 | tf_op jit(solution)/shard_map/ppermute | solution.py:42
  83.2 4.0 %collective-permute-done.29.cross = f32[32,128]{1,0:T(8,128)S(1)} collective-permute-done((f32[32,128]{1,0:T(8,128)S(1)}, f32[32,128]{1,0:T(8,128)S(1)}, u32[]{:S(2)}, u32[]{:S(2)}) %collective-permute-start.29) | collective-permute-done | bytes 16416 | tf_op jit(solution)/shard_map/ppermute | solution.py:42
  88.1 2.3 %collective-permute-start.32 = (f32[8,128]{1,0:T(8,128)S(1)}, f32[8,128]{1,0:T(8,128)S(1)}, u32[]{:S(2)}, u32[]{:S(2)}) collective-permute-start(f32[8,128]{1,0:T(8,128)S(1)} %get-tuple-element.90.u), channel_id=1, source_target_pairs={{3,4},{4,3},{5,6},{6,5},{7,8},{8,7},{9,10},{10,9},{11,12},{12,11},... | collective-permute-start | bytes 12296 | tf_op jit(solution)/shard_map/ppermute | solution.py:42
  90.4 5.1 %collective-permute-done.32.cross = f32[8,128]{1,0:T(8,128)S(1)} collective-permute-done((f32[8,128]{1,0:T(8,128)S(1)}, f32[8,128]{1,0:T(8,128)S(1)}, u32[]{:S(2)}, u32[]{:S(2)}) %collective-permute-start.32) | collective-permute-done | bytes 4128 | tf_op jit(solution)/shard_map/ppermute | solution.py:42
  95.9 2.3 %collective-permute-start.35 = (f32[8,128]{1,0:T(8,128)S(1)}, f32[8,128]{1,0:T(8,128)S(1)}, u32[]{:S(2)}, u32[]{:S(2)}) collective-permute-start(f32[8,128]{1,0:T(8,128)S(1)} %shard_map.122.u), channel_id=1, source_target_pairs={{3,4},{4,3},{5,6},{6,5},{7,8},{8,7},{9,10},{10,9},{11,12},{12,11},... | collective-permute-start | bytes 12296 | tf_op jit(solution)/shard_map/ppermute | solution.py:42
  98.2 5.1 %collective-permute-done.35.cross = f32[8,128]{1,0:T(8,128)S(1)} collective-permute-done((f32[8,128]{1,0:T(8,128)S(1)}, f32[8,128]{1,0:T(8,128)S(1)}, u32[]{:S(2)}, u32[]{:S(2)}) %collective-permute-start.35) | collective-permute-done | bytes 4128 | tf_op jit(solution)/shard_map/ppermute | solution.py:42
  103.8 2.3 %collective-permute-start.38 = (f32[8,128]{1,0:T(8,128)S(1)}, f32[8,128]{1,0:T(8,128)S(1)}, u32[]{:S(2)}, u32[]{:S(2)}) collective-permute-start(f32[8,128]{1,0:T(8,128)S(1)} %shard_map.123.u), channel_id=1, source_target_pairs={{3,4},{4,3},{5,6},{6,5},{7,8},{8,7},{9,10},{10,9},{11,12},{12,11},... | collective-permute-start | bytes 12296 | tf_op jit(solution)/shard_map/ppermute | solution.py:42
  106.0 5.1 %collective-permute-done.38.cross = f32[8,128]{1,0:T(8,128)S(1)} collective-permute-done((f32[8,128]{1,0:T(8,128)S(1)}, f32[8,128]{1,0:T(8,128)S(1)}, u32[]{:S(2)}, u32[]{:S(2)}) %collective-permute-start.38) | collective-permute-done | bytes 4128 | tf_op jit(solution)/shard_map/ppermute | solution.py:42
  115.3 3.8 %collective-permute-done.41.cross = f32[32,128]{1,0:T(8,128)S(1)} collective-permute-done((f32[32,128]{1,0:T(8,128)S(1)}, f32[32,128]{1,0:T(8,128)S(1)}, u32[]{:S(2)}, u32[]{:S(2)}) %collective-permute-start.41) | collective-permute-done | bytes 16416 | tf_op jit(solution)/shard_map/ppermute | solution.py:42
  123.6 3.8 %collective-permute-done.44.cross = f32[32,128]{1,0:T(8,128)S(1)} collective-permute-done((f32[32,128]{1,0:T(8,128)S(1)}, f32[32,128]{1,0:T(8,128)S(1)}, u32[]{:S(2)}, u32[]{:S(2)}) %collective-permute-start.44) | collective-permute-done | bytes 16416 | tf_op jit(solution)/shard_map/ppermute | solution.py:42
  (101 shorter events, 42.1 us)
Async XLA Ops:
  2.2 11.0 %collective-permute-start.2 = (f32[32,128]{1,0:T(8,128)S(1)}, f32[32,128]{1,0:T(8,128)S(1)}, u32[]{:S(2)}, u32[]{:S(2)}) collective-permute-start(f32[32,128]{1,0:T(8,128)S(1)} %get-tuple-element.62.rim), channel_id=1, source_target_pairs={{3,4},{4,3},{5,6},{6,5},{7,8},{8,7},{9,10},{10,9},{11,12},{12,11},... | collective-permute-start | bytes 49160 | tf_op jit(solution)/shard_map/ppermute | solution.py:42
  14.1 7.4 %collective-permute-start.5 = (f32[32,128]{1,0:T(8,128)S(1)}, f32[32,128]{1,0:T(8,128)S(1)}, u32[]{:S(2)}, u32[]{:S(2)}) collective-permute-start(f32[32,128]{1,0:T(8,128)S(1)} %shard_map.105.rim), channel_id=1, source_target_pairs={{3,4},{4,3},{5,6},{6,5},{7,8},{8,7},{9,10},{10,9},{11,12},{12,11},... | collective-permute-start | bytes 49160 | tf_op jit(solution)/shard_map/ppermute | solution.py:42
  22.9 7.3 %collective-permute-start.8 = (f32[8,128]{1,0:T(8,128)S(1)}, f32[8,128]{1,0:T(8,128)S(1)}, u32[]{:S(2)}, u32[]{:S(2)}) collective-permute-start(f32[8,128]{1,0:T(8,128)S(1)} %get-tuple-element.71.u), channel_id=1, source_target_pairs={{3,4},{4,3},{5,6},{6,5},{7,8},{8,7},{9,10},{10,9},{11,12},{12,11},... | collective-permute-start | bytes 12296 | tf_op jit(solution)/shard_map/ppermute | solution.py:42
  30.7 7.3 %collective-permute-start.11 = (f32[8,128]{1,0:T(8,128)S(1)}, f32[8,128]{1,0:T(8,128)S(1)}, u32[]{:S(2)}, u32[]{:S(2)}) collective-permute-start(f32[8,128]{1,0:T(8,128)S(1)} %shard_map.109.u), channel_id=1, source_target_pairs={{3,4},{4,3},{5,6},{6,5},{7,8},{8,7},{9,10},{10,9},{11,12},{12,11},... | collective-permute-start | bytes 12296 | tf_op jit(solution)/shard_map/ppermute | solution.py:42
  38.5 7.3 %collective-permute-start.14 = (f32[8,128]{1,0:T(8,128)S(1)}, f32[8,128]{1,0:T(8,128)S(1)}, u32[]{:S(2)}, u32[]{:S(2)}) collective-permute-start(f32[8,128]{1,0:T(8,128)S(1)} %shard_map.110.u), channel_id=1, source_target_pairs={{3,4},{4,3},{5,6},{6,5},{7,8},{8,7},{9,10},{10,9},{11,12},{12,11},... | collective-permute-start | bytes 12296 | tf_op jit(solution)/shard_map/ppermute | solution.py:42
  46.5 7.4 %collective-permute-start.17 = (f32[32,128]{1,0:T(8,128)S(1)}, f32[32,128]{1,0:T(8,128)S(1)}, u32[]{:S(2)}, u32[]{:S(2)}) collective-permute-start(f32[32,128]{1,0:T(8,128)S(1)} %get-tuple-element.72.rim), channel_id=1, source_target_pairs={{3,4},{4,3},{5,6},{6,5},{7,8},{8,7},{9,10},{10,9},{11,12},{12,11},... | collective-permute-start | bytes 49160 | tf_op jit(solution)/shard_map/ppermute | solution.py:42
  54.8 7.4 %collective-permute-start.20 = (f32[32,128]{1,0:T(8,128)S(1)}, f32[32,128]{1,0:T(8,128)S(1)}, u32[]{:S(2)}, u32[]{:S(2)}) collective-permute-start(f32[32,128]{1,0:T(8,128)S(1)} %shard_map.113.rim), channel_id=1, source_target_pairs={{3,4},{4,3},{5,6},{6,5},{7,8},{8,7},{9,10},{10,9},{11,12},{12,11},... | collective-permute-start | bytes 49160 | tf_op jit(solution)/shard_map/ppermute | solution.py:42
  63.1 7.4 %collective-permute-start.23 = (f32[32,128]{1,0:T(8,128)S(1)}, f32[32,128]{1,0:T(8,128)S(1)}, u32[]{:S(2)}, u32[]{:S(2)}) collective-permute-start(f32[32,128]{1,0:T(8,128)S(1)} %shard_map.115.rim), channel_id=1, source_target_pairs={{3,4},{4,3},{5,6},{6,5},{7,8},{8,7},{9,10},{10,9},{11,12},{12,11},... | collective-permute-start | bytes 49160 | tf_op jit(solution)/shard_map/ppermute | solution.py:42
  65.3 5.2 %collective-permute-start.22 = (f32[32,128]{1,0:T(8,128)S(1)}, f32[32,128]{1,0:T(8,128)S(1)}, u32[]{:S(2)}, u32[]{:S(2)}) collective-permute-start(f32[32,128]{1,0:T(8,128)S(1)} %shard_map.115.rim), channel_id=1, source_target_pairs={{0,1},{1,0},{2,3},{3,2},{4,5},{5,4},{6,7},{7,6},{8,9},{9,8},{10,11... | collective-permute-start | bytes 49160 | tf_op jit(solution)/shard_map/ppermute | solution.py:42
  71.4 7.4 %collective-permute-start.26 = (f32[32,128]{1,0:T(8,128)S(1)}, f32[32,128]{1,0:T(8,128)S(1)}, u32[]{:S(2)}, u32[]{:S(2)}) collective-permute-start(f32[32,128]{1,0:T(8,128)S(1)} %shard_map.117.rim), channel_id=1, source_target_pairs={{3,4},{4,3},{5,6},{6,5},{7,8},{8,7},{9,10},{10,9},{11,12},{12,11},... | collective-permute-start | bytes 49160 | tf_op jit(solution)/shard_map/ppermute | solution.py:42
  73.7 5.2 %collective-permute-start.25 = (f32[32,128]{1,0:T(8,128)S(1)}, f32[32,128]{1,0:T(8,128)S(1)}, u32[]{:S(2)}, u32[]{:S(2)}) collective-permute-start(f32[32,128]{1,0:T(8,128)S(1)} %shard_map.117.rim), channel_id=1, source_target_pairs={{0,1},{1,0},{2,3},{3,2},{4,5},{5,4},{6,7},{7,6},{8,9},{9,8},{10,11... | collective-permute-start | bytes 49160 | tf_op jit(solution)/shard_map/ppermute | solution.py:42
  73.7 5.2 %collective-permute-start.24 = (f32[32,128]{1,0:T(8,128)S(1)}, f32[32,128]{1,0:T(8,128)S(1)}, u32[]{:S(2)}, u32[]{:S(2)}) collective-permute-start(f32[32,128]{1,0:T(8,128)S(1)} %shard_map.117.rim), channel_id=1, source_target_pairs={{0,4},{1,5},{2,1},{3,7},{4,0},{5,6},{6,2},{7,3},{8,12},{9,10},{10,... | collective-permute-start | bytes 49160 | tf_op jit(solution)/shard_map/ppermute | solution.py:42
  79.7 7.4 %collective-permute-start.29 = (f32[32,128]{1,0:T(8,128)S(1)}, f32[32,128]{1,0:T(8,128)S(1)}, u32[]{:S(2)}, u32[]{:S(2)}) collective-permute-start(f32[32,128]{1,0:T(8,128)S(1)} %shard_map.119.rim), channel_id=1, source_target_pairs={{3,4},{4,3},{5,6},{6,5},{7,8},{8,7},{9,10},{10,9},{11,12},{12,11},... | collective-permute-start | bytes 49160 | tf_op jit(solution)/shard_map/ppermute | solution.py:42
  82.0 5.2 %collective-permute-start.28 = (f32[32,128]{1,0:T(8,128)S(1)}, f32[32,128]{1,0:T(8,128)S(1)}, u32[]{:S(2)}, u32[]{:S(2)}) collective-permute-start(f32[32,128]{1,0:T(8,128)S(1)} %shard_map.119.rim), channel_id=1, source_target_pairs={{0,1},{1,0},{2,3},{3,2},{4,5},{5,4},{6,7},{7,6},{8,9},{9,8},{10,11... | collective-permute-start | bytes 49160 | tf_op jit(solution)/shard_map/ppermute | solution.py:42
  82.0 5.2 %collective-permute-start.27 = (f32[32,128]{1,0:T(8,128)S(1)}, f32[32,128]{1,0:T(8,128)S(1)}, u32[]{:S(2)}, u32[]{:S(2)}) collective-permute-start(f32[32,128]{1,0:T(8,128)S(1)} %shard_map.119.rim), channel_id=1, source_target_pairs={{0,4},{1,5},{2,1},{3,7},{4,0},{5,6},{6,2},{7,3},{8,12},{9,10},{10,... | collective-permute-start | bytes 49160 | tf_op jit(solution)/shard_map/ppermute | solution.py:42
  88.1 7.3 %collective-permute-start.32 = (f32[8,128]{1,0:T(8,128)S(1)}, f32[8,128]{1,0:T(8,128)S(1)}, u32[]{:S(2)}, u32[]{:S(2)}) collective-permute-start(f32[8,128]{1,0:T(8,128)S(1)} %get-tuple-element.90.u), channel_id=1, source_target_pairs={{3,4},{4,3},{5,6},{6,5},{7,8},{8,7},{9,10},{10,9},{11,12},{12,11},... | collective-permute-start | bytes 12296 | tf_op jit(solution)/shard_map/ppermute | solution.py:42
  95.9 7.3 %collective-permute-start.35 = (f32[8,128]{1,0:T(8,128)S(1)}, f32[8,128]{1,0:T(8,128)S(1)}, u32[]{:S(2)}, u32[]{:S(2)}) collective-permute-start(f32[8,128]{1,0:T(8,128)S(1)} %shard_map.122.u), channel_id=1, source_target_pairs={{3,4},{4,3},{5,6},{6,5},{7,8},{8,7},{9,10},{10,9},{11,12},{12,11},... | collective-permute-start | bytes 12296 | tf_op jit(solution)/shard_map/ppermute | solution.py:42
  103.8 7.3 %collective-permute-start.38 = (f32[8,128]{1,0:T(8,128)S(1)}, f32[8,128]{1,0:T(8,128)S(1)}, u32[]{:S(2)}, u32[]{:S(2)}) collective-permute-start(f32[8,128]{1,0:T(8,128)S(1)} %shard_map.123.u), channel_id=1, source_target_pairs={{3,4},{4,3},{5,6},{6,5},{7,8},{8,7},{9,10},{10,9},{11,12},{12,11},... | collective-permute-start | bytes 12296 | tf_op jit(solution)/shard_map/ppermute | solution.py:42
  111.7 7.4 %collective-permute-start.41 = (f32[32,128]{1,0:T(8,128)S(1)}, f32[32,128]{1,0:T(8,128)S(1)}, u32[]{:S(2)}, u32[]{:S(2)}) collective-permute-start(f32[32,128]{1,0:T(8,128)S(1)} %get-tuple-element.91.rim), channel_id=1, source_target_pairs={{3,4},{4,3},{5,6},{6,5},{7,8},{8,7},{9,10},{10,9},{11,12},{12,11},... | collective-permute-start | bytes 49160 | tf_op jit(solution)/shard_map/ppermute | solution.py:42
  113.9 5.2 %collective-permute-start.40 = (f32[32,128]{1,0:T(8,128)S(1)}, f32[32,128]{1,0:T(8,128)S(1)}, u32[]{:S(2)}, u32[]{:S(2)}) collective-permute-start(f32[32,128]{1,0:T(8,128)S(1)} %get-tuple-element.91.rim), channel_id=1, source_target_pairs={{0,1},{1,0},{2,3},{3,2},{4,5},{5,4},{6,7},{7,6},{8,9},{9,8},{10,11... | collective-permute-start | bytes 49160 | tf_op jit(solution)/shard_map/ppermute | solution.py:42
  113.9 5.2 %collective-permute-start.39 = (f32[32,128]{1,0:T(8,128)S(1)}, f32[32,128]{1,0:T(8,128)S(1)}, u32[]{:S(2)}, u32[]{:S(2)}) collective-permute-start(f32[32,128]{1,0:T(8,128)S(1)} %get-tuple-element.91.rim), channel_id=1, source_target_pairs={{0,4},{1,5},{2,1},{3,7},{4,0},{5,6},{6,2},{7,3},{8,12},{9,10},{10,... | collective-permute-start | bytes 49160 | tf_op jit(solution)/shard_map/ppermute | solution.py:42
  120.0 7.4 %collective-permute-start.44 = (f32[32,128]{1,0:T(8,128)S(1)}, f32[32,128]{1,0:T(8,128)S(1)}, u32[]{:S(2)}, u32[]{:S(2)}) collective-permute-start(f32[32,128]{1,0:T(8,128)S(1)} %shard_map.126.rim), channel_id=1, source_target_pairs={{3,4},{4,3},{5,6},{6,5},{7,8},{8,7},{9,10},{10,9},{11,12},{12,11},... | collective-permute-start | bytes 49160 | tf_op jit(solution)/shard_map/ppermute | solution.py:42
  122.2 5.2 %collective-permute-start.43 = (f32[32,128]{1,0:T(8,128)S(1)}, f32[32,128]{1,0:T(8,128)S(1)}, u32[]{:S(2)}, u32[]{:S(2)}) collective-permute-start(f32[32,128]{1,0:T(8,128)S(1)} %shard_map.126.rim), channel_id=1, source_target_pairs={{0,1},{1,0},{2,3},{3,2},{4,5},{5,4},{6,7},{7,6},{8,9},{9,8},{10,11... | collective-permute-start | bytes 49160 | tf_op jit(solution)/shard_map/ppermute | solution.py:42
  122.2 5.2 %collective-permute-start.42 = (f32[32,128]{1,0:T(8,128)S(1)}, f32[32,128]{1,0:T(8,128)S(1)}, u32[]{:S(2)}, u32[]{:S(2)}) collective-permute-start(f32[32,128]{1,0:T(8,128)S(1)} %shard_map.126.rim), channel_id=1, source_target_pairs={{0,4},{1,5},{2,1},{3,7},{4,0},{5,6},{6,2},{7,3},{8,12},{9,10},{10,... | collective-permute-start | bytes 49160 | tf_op jit(solution)/shard_map/ppermute | solution.py:42
  (24 other events, 118.5 us)

commit v5 on v4

--- a/solution.py
+++ b/solution.py
@@ -251,18 +251,22 @@
 
 def last_kernel(
     columns, blocks, inv, rhs, rim, inside, lead, mend, pair, cross, new_core,
-    out, fields, acc, held, sem,
+    out, fields, acc, held, sems,
 ):
     sent = (mend, pair, cross)
     new = rim_sweep(columns, blocks, inv, rhs, rim, inside, lead, sent, fields, acc)
+    copies = []
     for g in range(4):
         part = slice(8 * g, 8 * g + 8)
         top, bottom = join_field(new[g], new_core[part, :])
         held[part, :] = top
-        held[32 + 8 * g : 40 + 8 * g, :] = bottom
-    copy = pltpu.make_async_copy(held, out, sem)
-    copy.start()
-    copy.wait()
+        below = slice(32 + 8 * g, 40 + 8 * g)
+        held[below, :] = bottom
+        for i, rows in enumerate((part, below)):
+            copies.append(pltpu.make_async_copy(held.at[rows], out.at[rows], sems.at[g, i]))
+            copies[-1].start()
+    for copy in copies:
+        copy.wait()
 
 
 def first_kernel(
@@ -329,7 +333,7 @@
 
 def widen_kernel(diag, off, rim_out, core_out, held, sems):
     slots = off.shape[0] + 1
-    parts, ahead = 4, 14
+    parts, ahead = 4, 22
     each = diag.shape[0] // parts
     copies = []
     for s in range(slots):
@@ -600,7 +604,7 @@
         out_shape=pltpu.HBM(full, F32),
         in_specs=[VM] * len(args),
         out_specs=FAR,
-        scratch_shapes=rim_work + [pltpu.VMEM(full, F32), sem(())],
+        scratch_shapes=rim_work + [pltpu.VMEM(full, F32), sem((4, 2))],
         compiler_params=pltpu.CompilerParams(vmem_limit_bytes=4 * 1024 * 1024),
     )(*[in_vmem(a) for a in args])
 

time: 129 us -> 129 us (level)
  no operation moved by 1% of the time
where the time goes in v5:
time: 129 us
  waiting for transfers between devices  56 us (43%)
  starting transfers between devices  40.8 us (32%)
  Pallas kernels  32 us (25%)
    ppermute x45, waiting for transfers between devices, exchange(): return [lax.ppermute(field, AXES, way) for way in ways]  56 us
    ppermute x45, starting transfers between devices, exchange(): return [lax.ppermute(field, AXES, way) for way in ways]  40.8 us
    pallas_call x28, Pallas kernels, call(): pl.pallas_call(kernel, out_shape=shapes if len(shapes) > 1 else shapes[0]...  30.4 us
  transfers between devices with their start and end apart: 45, of which 15 were waited for; matrix products, arithmetic and copies ran while one was open for 0% of the time, Pallas kernels for 14%

profile of v5, /device:TPU:6, one launch (start us, length us, event | category | flops | bytes accessed | tf_op | source)
XLA Modules:
  0.0 129.2 jit_solution(12453938050503892672)
XLA Ops:
  2.2 6.3 %collective-permute-start.2 = (f32[32,128]{1,0:T(8,128)S(1)}, f32[32,128]{1,0:T(8,128)S(1)}, u32[]{:S(2)}, u32[]{:S(2)}) collective-permute-start(f32[32,128]{1,0:T(8,128)S(1)} %get-tuple-element.62.rim), channel_id=1, source_target_pairs={{3,4},{4,3},{5,6},{6,5},{7,8},{8,7},{9,10},{10,9},{11,12},{12,11},... | collective-permute-start | bytes 49160 | tf_op jit(solution)/shard_map/ppermute | solution.py:42
  8.5 4.5 %shard_map.101 = (f32[7,64,32,128]{3,2,1,0:T(8,128)S(1)}, bf16[7,64,32,128]{3,2,1,0:T(8,128)(2,1)S(1)}) custom-call(bf16[64,64,128]{2,1,0:T(8,128)(2,1)} %diag.1, bf16[6,64,64,128]{3,2,1,0:T(8,128)(2,1)} %off.1), custom_call_target="tpu_custom_call" | custom-call | tf_op jit(solution)/shard_map/pallas_call | solution.py:491
  14.1 2.7 %collective-permute-start.5 = (f32[32,128]{1,0:T(8,128)S(1)}, f32[32,128]{1,0:T(8,128)S(1)}, u32[]{:S(2)}, u32[]{:S(2)}) collective-permute-start(f32[32,128]{1,0:T(8,128)S(1)} %shard_map.105.rim), channel_id=1, source_target_pairs={{3,4},{4,3},{5,6},{6,5},{7,8},{8,7},{9,10},{10,9},{11,12},{12,11},... | collective-permute-start | bytes 49160 | tf_op jit(solution)/shard_map/ppermute | solution.py:42
  22.9 2.3 %collective-permute-start.8 = (f32[8,128]{1,0:T(8,128)S(1)}, f32[8,128]{1,0:T(8,128)S(1)}, u32[]{:S(2)}, u32[]{:S(2)}) collective-permute-start(f32[8,128]{1,0:T(8,128)S(1)} %get-tuple-element.71.u), channel_id=1, source_target_pairs={{3,4},{4,3},{5,6},{6,5},{7,8},{8,7},{9,10},{10,9},{11,12},{12,11},... | collective-permute-start | bytes 12296 | tf_op jit(solution)/shard_map/ppermute | solution.py:42
  27.0 3.2 %collective-permute-done.8.cross = f32[8,128]{1,0:T(8,128)S(1)} collective-permute-done((f32[8,128]{1,0:T(8,128)S(1)}, f32[8,128]{1,0:T(8,128)S(1)}, u32[]{:S(2)}, u32[]{:S(2)}) %collective-permute-start.8) | collective-permute-done | bytes 4128 | tf_op jit(solution)/shard_map/ppermute | solution.py:42
  30.7 2.3 %collective-permute-start.11 = (f32[8,128]{1,0:T(8,128)S(1)}, f32[8,128]{1,0:T(8,128)S(1)}, u32[]{:S(2)}, u32[]{:S(2)}) collective-permute-start(f32[8,128]{1,0:T(8,128)S(1)} %shard_map.109.u), channel_id=1, source_target_pairs={{3,4},{4,3},{5,6},{6,5},{7,8},{8,7},{9,10},{10,9},{11,12},{12,11},... | collective-permute-start | bytes 12296 | tf_op jit(solution)/shard_map/ppermute | solution.py:42
  33.0 5.0 %collective-permute-done.11.cross = f32[8,128]{1,0:T(8,128)S(1)} collective-permute-done((f32[8,128]{1,0:T(8,128)S(1)}, f32[8,128]{1,0:T(8,128)S(1)}, u32[]{:S(2)}, u32[]{:S(2)}) %collective-permute-start.11) | collective-permute-done | bytes 4128 | tf_op jit(solution)/shard_map/ppermute | solution.py:42
  38.5 2.3 %collective-permute-start.14 = (f32[8,128]{1,0:T(8,128)S(1)}, f32[8,128]{1,0:T(8,128)S(1)}, u32[]{:S(2)}, u32[]{:S(2)}) collective-permute-start(f32[8,128]{1,0:T(8,128)S(1)} %shard_map.110.u), channel_id=1, source_target_pairs={{3,4},{4,3},{5,6},{6,5},{7,8},{8,7},{9,10},{10,9},{11,12},{12,11},... | collective-permute-start | bytes 12296 | tf_op jit(solution)/shard_map/ppermute | solution.py:42
  40.9 5.0 %collective-permute-done.14.cross = f32[8,128]{1,0:T(8,128)S(1)} collective-permute-done((f32[8,128]{1,0:T(8,128)S(1)}, f32[8,128]{1,0:T(8,128)S(1)}, u32[]{:S(2)}, u32[]{:S(2)}) %collective-permute-start.14) | collective-permute-done | bytes 4128 | tf_op jit(solution)/shard_map/ppermute | solution.py:42
  46.4 2.3 %collective-permute-start.17 = (f32[32,128]{1,0:T(8,128)S(1)}, f32[32,128]{1,0:T(8,128)S(1)}, u32[]{:S(2)}, u32[]{:S(2)}) collective-permute-start(f32[32,128]{1,0:T(8,128)S(1)} %get-tuple-element.72.rim), channel_id=1, source_target_pairs={{3,4},{4,3},{5,6},{6,5},{7,8},{8,7},{9,10},{10,9},{11,12},{12,11},... | collective-permute-start | bytes 49160 | tf_op jit(solution)/shard_map/ppermute | solution.py:42
  50.1 3.7 %collective-permute-done.17.cross = f32[32,128]{1,0:T(8,128)S(1)} collective-permute-done((f32[32,128]{1,0:T(8,128)S(1)}, f32[32,128]{1,0:T(8,128)S(1)}, u32[]{:S(2)}, u32[]{:S(2)}) %collective-permute-start.17) | collective-permute-done | bytes 16416 | tf_op jit(solution)/shard_map/ppermute | solution.py:42
  54.8 2.3 %collective-permute-start.20 = (f32[32,128]{1,0:T(8,128)S(1)}, f32[32,128]{1,0:T(8,128)S(1)}, u32[]{:S(2)}, u32[]{:S(2)}) collective-permute-start(f32[32,128]{1,0:T(8,128)S(1)} %shard_map.113.rim), channel_id=1, source_target_pairs={{3,4},{4,3},{5,6},{6,5},{7,8},{8,7},{9,10},{10,9},{11,12},{12,11},... | collective-permute-start | bytes 49160 | tf_op jit(solution)/shard_map/ppermute | solution.py:42
  58.4 3.8 %collective-permute-done.20.cross = f32[32,128]{1,0:T(8,128)S(1)} collective-permute-done((f32[32,128]{1,0:T(8,128)S(1)}, f32[32,128]{1,0:T(8,128)S(1)}, u32[]{:S(2)}, u32[]{:S(2)}) %collective-permute-start.20) | collective-permute-done | bytes 16416 | tf_op jit(solution)/shard_map/ppermute | solution.py:42
  66.8 3.8 %collective-permute-done.23.cross = f32[32,128]{1,0:T(8,128)S(1)} collective-permute-done((f32[32,128]{1,0:T(8,128)S(1)}, f32[32,128]{1,0:T(8,128)S(1)}, u32[]{:S(2)}, u32[]{:S(2)}) %collective-permute-start.23) | collective-permute-done | bytes 16416 | tf_op jit(solution)/shard_map/ppermute | solution.py:42
  75.1 3.8 %collective-permute-done.26.cross = f32[32,128]{1,0:T(8,128)S(1)} collective-permute-done((f32[32,128]{1,0:T(8,128)S(1)}, f32[32,128]{1,0:T(8,128)S(1)}, u32[]{:S(2)}, u32[]{:S(2)}) %collective-permute-start.26) | collective-permute-done | bytes 16416 | tf_op jit(solution)/shard_map/ppermute | solution.py:42
  83.2 4.0 %collective-permute-done.29.cross = f32[32,128]{1,0:T(8,128)S(1)} collective-permute-done((f32[32,128]{1,0:T(8,128)S(1)}, f32[32,128]{1,0:T(8,128)S(1)}, u32[]{:S(2)}, u32[]{:S(2)}) %collective-permute-start.29) | collective-permute-done | bytes 16416 | tf_op jit(solution)/shard_map/ppermute | solution.py:42
  88.1 2.3 %collective-permute-start.32 = (f32[8,128]{1,0:T(8,128)S(1)}, f32[8,128]{1,0:T(8,128)S(1)}, u32[]{:S(2)}, u32[]{:S(2)}) collective-permute-start(f32[8,128]{1,0:T(8,128)S(1)} %get-tuple-element.90.u), channel_id=1, source_target_pairs={{3,4},{4,3},{5,6},{6,5},{7,8},{8,7},{9,10},{10,9},{11,12},{12,11},... | collective-permute-start | bytes 12296 | tf_op jit(solution)/shard_map/ppermute | solution.py:42
  90.4 5.0 %collective-permute-done.32.cross = f32[8,128]{1,0:T(8,128)S(1)} collective-permute-done((f32[8,128]{1,0:T(8,128)S(1)}, f32[8,128]{1,0:T(8,128)S(1)}, u32[]{:S(2)}, u32[]{:S(2)}) %collective-permute-start.32) | collective-permute-done | bytes 4128 | tf_op jit(solution)/shard_map/ppermute | solution.py:42
  95.9 2.3 %collective-permute-start.35 = (f32[8,128]{1,0:T(8,128)S(1)}, f32[8,128]{1,0:T(8,128)S(1)}, u32[]{:S(2)}, u32[]{:S(2)}) collective-permute-start(f32[8,128]{1,0:T(8,128)S(1)} %shard_map.122.u), channel_id=1, source_target_pairs={{3,4},{4,3},{5,6},{6,5},{7,8},{8,7},{9,10},{10,9},{11,12},{12,11},... | collective-permute-start | bytes 12296 | tf_op jit(solution)/shard_map/ppermute | solution.py:42
  98.2 5.1 %collective-permute-done.35.cross = f32[8,128]{1,0:T(8,128)S(1)} collective-permute-done((f32[8,128]{1,0:T(8,128)S(1)}, f32[8,128]{1,0:T(8,128)S(1)}, u32[]{:S(2)}, u32[]{:S(2)}) %collective-permute-start.35) | collective-permute-done | bytes 4128 | tf_op jit(solution)/shard_map/ppermute | solution.py:42
  103.8 2.3 %collective-permute-start.38 = (f32[8,128]{1,0:T(8,128)S(1)}, f32[8,128]{1,0:T(8,128)S(1)}, u32[]{:S(2)}, u32[]{:S(2)}) collective-permute-start(f32[8,128]{1,0:T(8,128)S(1)} %shard_map.123.u), channel_id=1, source_target_pairs={{3,4},{4,3},{5,6},{6,5},{7,8},{8,7},{9,10},{10,9},{11,12},{12,11},... | collective-permute-start | bytes 12296 | tf_op jit(solution)/shard_map/ppermute | solution.py:42
  106.0 5.1 %collective-permute-done.38.cross = f32[8,128]{1,0:T(8,128)S(1)} collective-permute-done((f32[8,128]{1,0:T(8,128)S(1)}, f32[8,128]{1,0:T(8,128)S(1)}, u32[]{:S(2)}, u32[]{:S(2)}) %collective-permute-start.38) | collective-permute-done | bytes 4128 | tf_op jit(solution)/shard_map/ppermute | solution.py:42
  115.3 3.8 %collective-permute-done.41.cross = f32[32,128]{1,0:T(8,128)S(1)} collective-permute-done((f32[32,128]{1,0:T(8,128)S(1)}, f32[32,128]{1,0:T(8,128)S(1)}, u32[]{:S(2)}, u32[]{:S(2)}) %collective-permute-start.41) | collective-permute-done | bytes 16416 | tf_op jit(solution)/shard_map/ppermute | solution.py:42
  123.6 3.8 %collective-permute-done.44.cross = f32[32,128]{1,0:T(8,128)S(1)} collective-permute-done((f32[32,128]{1,0:T(8,128)S(1)}, f32[32,128]{1,0:T(8,128)S(1)}, u32[]{:S(2)}, u32[]{:S(2)}) %collective-permute-start.44) | collective-permute-done | bytes 16416 | tf_op jit(solution)/shard_map/ppermute | solution.py:42
  (101 shorter events, 42.2 us)
Async XLA Ops:
  2.2 11.0 %collective-permute-start.2 = (f32[32,128]{1,0:T(8,128)S(1)}, f32[32,128]{1,0:T(8,128)S(1)}, u32[]{:S(2)}, u32[]{:S(2)}) collective-permute-start(f32[32,128]{1,0:T(8,128)S(1)} %get-tuple-element.62.rim), channel_id=1, source_target_pairs={{3,4},{4,3},{5,6},{6,5},{7,8},{8,7},{9,10},{10,9},{11,12},{12,11},... | collective-permute-start | bytes 49160 | tf_op jit(solution)/shard_map/ppermute | solution.py:42
  14.1 7.4 %collective-permute-start.5 = (f32[32,128]{1,0:T(8,128)S(1)}, f32[32,128]{1,0:T(8,128)S(1)}, u32[]{:S(2)}, u32[]{:S(2)}) collective-permute-start(f32[32,128]{1,0:T(8,128)S(1)} %shard_map.105.rim), channel_id=1, source_target_pairs={{3,4},{4,3},{5,6},{6,5},{7,8},{8,7},{9,10},{10,9},{11,12},{12,11},... | collective-permute-start | bytes 49160 | tf_op jit(solution)/shard_map/ppermute | solution.py:42
  22.9 7.3 %collective-permute-start.8 = (f32[8,128]{1,0:T(8,128)S(1)}, f32[8,128]{1,0:T(8,128)S(1)}, u32[]{:S(2)}, u32[]{:S(2)}) collective-permute-start(f32[8,128]{1,0:T(8,128)S(1)} %get-tuple-element.71.u), channel_id=1, source_target_pairs={{3,4},{4,3},{5,6},{6,5},{7,8},{8,7},{9,10},{10,9},{11,12},{12,11},... | collective-permute-start | bytes 12296 | tf_op jit(solution)/shard_map/ppermute | solution.py:42
  30.7 7.3 %collective-permute-start.11 = (f32[8,128]{1,0:T(8,128)S(1)}, f32[8,128]{1,0:T(8,128)S(1)}, u32[]{:S(2)}, u32[]{:S(2)}) collective-permute-start(f32[8,128]{1,0:T(8,128)S(1)} %shard_map.109.u), channel_id=1, source_target_pairs={{3,4},{4,3},{5,6},{6,5},{7,8},{8,7},{9,10},{10,9},{11,12},{12,11},... | collective-permute-start | bytes 12296 | tf_op jit(solution)/shard_map/ppermute | solution.py:42
  38.5 7.3 %collective-permute-start.14 = (f32[8,128]{1,0:T(8,128)S(1)}, f32[8,128]{1,0:T(8,128)S(1)}, u32[]{:S(2)}, u32[]{:S(2)}) collective-permute-start(f32[8,128]{1,0:T(8,128)S(1)} %shard_map.110.u), channel_id=1, source_target_pairs={{3,4},{4,3},{5,6},{6,5},{7,8},{8,7},{9,10},{10,9},{11,12},{12,11},... | collective-permute-start | bytes 12296 | tf_op jit(solution)/shard_map/ppermute | solution.py:42
  46.4 7.4 %collective-permute-start.17 = (f32[32,128]{1,0:T(8,128)S(1)}, f32[32,128]{1,0:T(8,128)S(1)}, u32[]{:S(2)}, u32[]{:S(2)}) collective-permute-start(f32[32,128]{1,0:T(8,128)S(1)} %get-tuple-element.72.rim), channel_id=1, source_target_pairs={{3,4},{4,3},{5,6},{6,5},{7,8},{8,7},{9,10},{10,9},{11,12},{12,11},... | collective-permute-start | bytes 49160 | tf_op jit(solution)/shard_map/ppermute | solution.py:42
  54.8 7.4 %collective-permute-start.20 = (f32[32,128]{1,0:T(8,128)S(1)}, f32[32,128]{1,0:T(8,128)S(1)}, u32[]{:S(2)}, u32[]{:S(2)}) collective-permute-start(f32[32,128]{1,0:T(8,128)S(1)} %shard_map.113.rim), channel_id=1, source_target_pairs={{3,4},{4,3},{5,6},{6,5},{7,8},{8,7},{9,10},{10,9},{11,12},{12,11},... | collective-permute-start | bytes 49160 | tf_op jit(solution)/shard_map/ppermute | solution.py:42
  63.1 7.4 %collective-permute-start.23 = (f32[32,128]{1,0:T(8,128)S(1)}, f32[32,128]{1,0:T(8,128)S(1)}, u32[]{:S(2)}, u32[]{:S(2)}) collective-permute-start(f32[32,128]{1,0:T(8,128)S(1)} %shard_map.115.rim), channel_id=1, source_target_pairs={{3,4},{4,3},{5,6},{6,5},{7,8},{8,7},{9,10},{10,9},{11,12},{12,11},... | collective-permute-start | bytes 49160 | tf_op jit(solution)/shard_map/ppermute | solution.py:42
  65.3 5.2 %collective-permute-start.22 = (f32[32,128]{1,0:T(8,128)S(1)}, f32[32,128]{1,0:T(8,128)S(1)}, u32[]{:S(2)}, u32[]{:S(2)}) collective-permute-start(f32[32,128]{1,0:T(8,128)S(1)} %shard_map.115.rim), channel_id=1, source_target_pairs={{0,1},{1,0},{2,3},{3,2},{4,5},{5,4},{6,7},{7,6},{8,9},{9,8},{10,11... | collective-permute-start | bytes 49160 | tf_op jit(solution)/shard_map/ppermute | solution.py:42
  71.4 7.4 %collective-permute-start.26 = (f32[32,128]{1,0:T(8,128)S(1)}, f32[32,128]{1,0:T(8,128)S(1)}, u32[]{:S(2)}, u32[]{:S(2)}) collective-permute-start(f32[32,128]{1,0:T(8,128)S(1)} %shard_map.117.rim), channel_id=1, source_target_pairs={{3,4},{4,3},{5,6},{6,5},{7,8},{8,7},{9,10},{10,9},{11,12},{12,11},... | collective-permute-start | bytes 49160 | tf_op jit(solution)/shard_map/ppermute | solution.py:42
  73.7 5.2 %collective-permute-start.25 = (f32[32,128]{1,0:T(8,128)S(1)}, f32[32,128]{1,0:T(8,128)S(1)}, u32[]{:S(2)}, u32[]{:S(2)}) collective-permute-start(f32[32,128]{1,0:T(8,128)S(1)} %shard_map.117.rim), channel_id=1, source_target_pairs={{0,1},{1,0},{2,3},{3,2},{4,5},{5,4},{6,7},{7,6},{8,9},{9,8},{10,11... | collective-permute-start | bytes 49160 | tf_op jit(solution)/shard_map/ppermute | solution.py:42
  73.7 5.2 %collective-permute-start.24 = (f32[32,128]{1,0:T(8,128)S(1)}, f32[32,128]{1,0:T(8,128)S(1)}, u32[]{:S(2)}, u32[]{:S(2)}) collective-permute-start(f32[32,128]{1,0:T(8,128)S(1)} %shard_map.117.rim), channel_id=1, source_target_pairs={{0,4},{1,5},{2,1},{3,7},{4,0},{5,6},{6,2},{7,3},{8,12},{9,10},{10,... | collective-permute-start | bytes 49160 | tf_op jit(solution)/shard_map/ppermute | solution.py:42
  79.7 7.4 %collective-permute-start.29 = (f32[32,128]{1,0:T(8,128)S(1)}, f32[32,128]{1,0:T(8,128)S(1)}, u32[]{:S(2)}, u32[]{:S(2)}) collective-permute-start(f32[32,128]{1,0:T(8,128)S(1)} %shard_map.119.rim), channel_id=1, source_target_pairs={{3,4},{4,3},{5,6},{6,5},{7,8},{8,7},{9,10},{10,9},{11,12},{12,11},... | collective-permute-start | bytes 49160 | tf_op jit(solution)/shard_map/ppermute | solution.py:42
  82.0 5.2 %collective-permute-start.28 = (f32[32,128]{1,0:T(8,128)S(1)}, f32[32,128]{1,0:T(8,128)S(1)}, u32[]{:S(2)}, u32[]{:S(2)}) collective-permute-start(f32[32,128]{1,0:T(8,128)S(1)} %shard_map.119.rim), channel_id=1, source_target_pairs={{0,1},{1,0},{2,3},{3,2},{4,5},{5,4},{6,7},{7,6},{8,9},{9,8},{10,11... | collective-permute-start | bytes 49160 | tf_op jit(solution)/shard_map/ppermute | solution.py:42
  82.0 5.2 %collective-permute-start.27 = (f32[32,128]{1,0:T(8,128)S(1)}, f32[32,128]{1,0:T(8,128)S(1)}, u32[]{:S(2)}, u32[]{:S(2)}) collective-permute-start(f32[32,128]{1,0:T(8,128)S(1)} %shard_map.119.rim), channel_id=1, source_target_pairs={{0,4},{1,5},{2,1},{3,7},{4,0},{5,6},{6,2},{7,3},{8,12},{9,10},{10,... | collective-permute-start | bytes 49160 | tf_op jit(solution)/shard_map/ppermute | solution.py:42
  88.1 7.3 %collective-permute-start.32 = (f32[8,128]{1,0:T(8,128)S(1)}, f32[8,128]{1,0:T(8,128)S(1)}, u32[]{:S(2)}, u32[]{:S(2)}) collective-permute-start(f32[8,128]{1,0:T(8,128)S(1)} %get-tuple-element.90.u), channel_id=1, source_target_pairs={{3,4},{4,3},{5,6},{6,5},{7,8},{8,7},{9,10},{10,9},{11,12},{12,11},... | collective-permute-start | bytes 12296 | tf_op jit(solution)/shard_map/ppermute | solution.py:42
  95.9 7.3 %collective-permute-start.35 = (f32[8,128]{1,0:T(8,128)S(1)}, f32[8,128]{1,0:T(8,128)S(1)}, u32[]{:S(2)}, u32[]{:S(2)}) collective-permute-start(f32[8,128]{1,0:T(8,128)S(1)} %shard_map.122.u), channel_id=1, source_target_pairs={{3,4},{4,3},{5,6},{6,5},{7,8},{8,7},{9,10},{10,9},{11,12},{12,11},... | collective-permute-start | bytes 12296 | tf_op jit(solution)/shard_map/ppermute | solution.py:42
  103.8 7.3 %collective-permute-start.38 = (f32[8,128]{1,0:T(8,128)S(1)}, f32[8,128]{1,0:T(8,128)S(1)}, u32[]{:S(2)}, u32[]{:S(2)}) collective-permute-start(f32[8,128]{1,0:T(8,128)S(1)} %shard_map.123.u), channel_id=1, source_target_pairs={{3,4},{4,3},{5,6},{6,5},{7,8},{8,7},{9,10},{10,9},{11,12},{12,11},... | collective-permute-start | bytes 12296 | tf_op jit(solution)/shard_map/ppermute | solution.py:42
  111.7 7.4 %collective-permute-start.41 = (f32[32,128]{1,0:T(8,128)S(1)}, f32[32,128]{1,0:T(8,128)S(1)}, u32[]{:S(2)}, u32[]{:S(2)}) collective-permute-start(f32[32,128]{1,0:T(8,128)S(1)} %get-tuple-element.91.rim), channel_id=1, source_target_pairs={{3,4},{4,3},{5,6},{6,5},{7,8},{8,7},{9,10},{10,9},{11,12},{12,11},... | collective-permute-start | bytes 49160 | tf_op jit(solution)/shard_map/ppermute | solution.py:42
  113.9 5.2 %collective-permute-start.40 = (f32[32,128]{1,0:T(8,128)S(1)}, f32[32,128]{1,0:T(8,128)S(1)}, u32[]{:S(2)}, u32[]{:S(2)}) collective-permute-start(f32[32,128]{1,0:T(8,128)S(1)} %get-tuple-element.91.rim), channel_id=1, source_target_pairs={{0,1},{1,0},{2,3},{3,2},{4,5},{5,4},{6,7},{7,6},{8,9},{9,8},{10,11... | collective-permute-start | bytes 49160 | tf_op jit(solution)/shard_map/ppermute | solution.py:42
  113.9 5.2 %collective-permute-start.39 = (f32[32,128]{1,0:T(8,128)S(1)}, f32[32,128]{1,0:T(8,128)S(1)}, u32[]{:S(2)}, u32[]{:S(2)}) collective-permute-start(f32[32,128]{1,0:T(8,128)S(1)} %get-tuple-element.91.rim), channel_id=1, source_target_pairs={{0,4},{1,5},{2,1},{3,7},{4,0},{5,6},{6,2},{7,3},{8,12},{9,10},{10,... | collective-permute-start | bytes 49160 | tf_op jit(solution)/shard_map/ppermute | solution.py:42
  120.0 7.4 %collective-permute-start.44 = (f32[32,128]{1,0:T(8,128)S(1)}, f32[32,128]{1,0:T(8,128)S(1)}, u32[]{:S(2)}, u32[]{:S(2)}) collective-permute-start(f32[32,128]{1,0:T(8,128)S(1)} %shard_map.126.rim), channel_id=1, source_target_pairs={{3,4},{4,3},{5,6},{6,5},{7,8},{8,7},{9,10},{10,9},{11,12},{12,11},... | collective-permute-start | bytes 49160 | tf_op jit(solution)/shard_map/ppermute | solution.py:42
  122.2 5.2 %collective-permute-start.43 = (f32[32,128]{1,0:T(8,128)S(1)}, f32[32,128]{1,0:T(8,128)S(1)}, u32[]{:S(2)}, u32[]{:S(2)}) collective-permute-start(f32[32,128]{1,0:T(8,128)S(1)} %shard_map.126.rim), channel_id=1, source_target_pairs={{0,1},{1,0},{2,3},{3,2},{4,5},{5,4},{6,7},{7,6},{8,9},{9,8},{10,11... | collective-permute-start | bytes 49160 | tf_op jit(solution)/shard_map/ppermute | solution.py:42
  122.2 5.2 %collective-permute-start.42 = (f32[32,128]{1,0:T(8,128)S(1)}, f32[32,128]{1,0:T(8,128)S(1)}, u32[]{:S(2)}, u32[]{:S(2)}) collective-permute-start(f32[32,128]{1,0:T(8,128)S(1)} %shard_map.126.rim), channel_id=1, source_target_pairs={{0,4},{1,5},{2,1},{3,7},{4,0},{5,6},{6,2},{7,3},{8,12},{9,10},{10,... | collective-permute-start | bytes 49160 | tf_op jit(solution)/shard_map/ppermute | solution.py:42
  (24 other events, 118.3 us)
